TPU v7x, 256 devices: a whole 4x4x8 slice. The times are simulated.
256 devices in a mesh: section: 16 (over x_lo, z), tp: 16 (over x_hi, y, core).
Axes of the slice: x: 4 (x_hi: 2, x_lo: 2; x = x_hi * 2 + x_lo), y: 4, z: 8, core: 2. Of those that a mesh axis runs over, the one named last changes fastest.
Arguments:
- hidden: bfloat16 [16384, 8192], P(('section', 'tp')), may hold values from -6 to 6
- norm_gain: float32 [16, 8192], P('section'), may hold values from 0.5 to 1.5
- query_weight: bfloat16 [16, 8192, 4096], P('section', None, 'tp'), may hold values from -0.0625 to 0.0625
- kv_weight: bfloat16 [16, 8192, 1024], P('section', None, 'tp'), may hold values from -0.13368738 to 0.13368738
- out_weight: bfloat16 [16, 4096, 8192], P('section', 'tp'), may hold values from -0.09375 to 0.09375
- prompt_cache: bfloat16 [16, 4, 1024, 1024], P('section', None, 'tp'), may hold values from -320 to 320
- resp_len: int32 [128], P('section'), may hold values from 1 to 128, as said below
- prompt_id: int32 [128], P('section'), may hold values from 0 to 3
Outputs:
- next_hidden: bfloat16 [16384, 8192], P(('section', 'tp'))
Inputs may be any that keep to these rules, and one draw needn't show every extreme that they name: `resp_len`: some response of the draw has exactly 128 live tokens.
All inputs are finite; a program needn't handle non-finite values.
Results may differ from a plain program's by a relative error of at most 0.011.
Values may be sent and summed in bfloat16 or wider, within the bound.
No kernel may reach another device: no remote copies, remote signals or barrier semaphores. Data moves between devices by JAX's collectives and lax.ppermute only.
A program may use at most 128 MiB of HBM per device.

v0:
```python
import jax
import jax.numpy as jnp
from jax import lax
from jax.sharding import PartitionSpec as P

QH = 32
KVH = 4
HD = 128
PROMPT = 1024


def from_behind(value, axis, by):
    length = lax.axis_size(axis)
    return lax.ppermute(value, axis, [(i, (i + by) % length) for i in range(length)])


def rope_tables(offset, length, head_width):
    half_width = head_width // 2
    position = (offset + jnp.arange(length)).astype(jnp.float32)
    inverse = jnp.exp(
        -(2.0 * jnp.arange(half_width).astype(jnp.float32) / head_width) * jnp.log(10000.0)
    )
    angles = position[:, None] * inverse[None, :]
    return (jnp.cos(angles), jnp.sin(angles))


def rotate(tensor, cosine_table, sine_table):
    half_width = tensor.shape[-1] // 2
    first_half = tensor[..., :half_width]
    second_half = tensor[..., half_width:]
    return jnp.concatenate(
        [
            first_half * cosine_table - second_half * sine_table,
            second_half * cosine_table + first_half * sine_table,
        ],
        axis=-1,
    )


def block_state(queries, block_keys, block_values, visible):
    scores = jnp.einsum(
        "shqd,skd->shqk", queries, block_keys, preferred_element_type=jnp.float32
    ) * HD ** (-0.5)
    if visible is not None:
        scores = jnp.where(visible, scores, -jnp.inf)
    maxima = jnp.max(scores, axis=-1)
    probs = jnp.exp(scores - maxima[..., None])
    totals = jnp.sum(probs, axis=-1)
    weighted = jnp.einsum(
        "shqk,skd->shqd",
        probs.astype(jnp.bfloat16),
        block_values,
        preferred_element_type=jnp.float32,
    )
    return (maxima, totals, weighted)


def combine(earlier, later):
    joined = jnp.maximum(earlier[0], later[0])
    scale_one = jnp.exp(earlier[0] - joined)
    scale_two = jnp.exp(later[0] - joined)
    totals = earlier[1] * scale_one + later[1] * scale_two
    weighted = earlier[2] * scale_one[..., None] + later[2] * scale_two[..., None]
    return (joined, totals, weighted)


def body(hidden, norm_gain, query_weight, kv_weight, out_weight, prompt_cache, resp_len, prompt_id):
    group_size = QH // KVH
    head_cols = query_weight.shape[2]
    local_heads = head_cols // HD
    head_index = lax.axis_index("tp") * local_heads // group_size
    widened = hidden.astype(jnp.float32)
    normed = (
        widened
        * lax.rsqrt(jnp.mean(widened * widened, axis=-1, keepdims=True) + 1e-06)
        * norm_gain[0]
    ).astype(jnp.bfloat16)
    shard_piece = lax.all_gather(normed, "tp", axis=0, tiled=True)
    projected = jnp.concatenate(
        [
            jnp.dot(shard_piece, query_weight[0], preferred_element_type=jnp.float32),
            jnp.dot(shard_piece, kv_weight[0], preferred_element_type=jnp.float32),
        ],
        axis=1,
    )
    row_count = projected.shape[0]
    seq_count = resp_len.shape[0]
    resp_size = row_count // seq_count
    cosine_table, sine_table = rope_tables(PROMPT, resp_size, HD)
    queries = (
        projected[:, :head_cols]
        .reshape(seq_count, resp_size, local_heads, HD)
        .transpose(0, 2, 1, 3)
    )
    queries = rotate(queries, cosine_table, sine_table).astype(jnp.bfloat16)
    kv_part = projected[:, head_cols:].astype(jnp.bfloat16).T
    kv_all = lax.all_gather(kv_part, "tp", axis=0, tiled=True)
    key_rows = lax.dynamic_slice_in_dim(kv_all, head_index * HD, HD, 0)
    value_rows = lax.dynamic_slice_in_dim(kv_all, KVH * HD + head_index * HD, HD, 0)
    own_keys = rotate(
        key_rows.reshape(HD, seq_count, resp_size).transpose(1, 2, 0).astype(jnp.float32),
        cosine_table,
        sine_table,
    ).astype(jnp.bfloat16)
    own_values = value_rows.reshape(HD, seq_count, resp_size).transpose(1, 2, 0)
    query_pos = jnp.arange(resp_size)
    causal = (query_pos[None, None, :] <= query_pos[None, :, None]) & (
        query_pos[None, None, :] < resp_len[:, None, None]
    )
    attn_state = block_state(queries, own_keys, own_values, causal[:, None])
    chosen = jnp.take(lax.all_gather(prompt_cache, "tp", axis=2, tiled=True)[0], prompt_id, axis=0)
    block_keys = lax.dynamic_slice_in_dim(chosen, head_index * HD, HD, 2)
    block_values = lax.dynamic_slice_in_dim(chosen, KVH * HD + head_index * HD, HD, 2)
    attn_state = combine(attn_state, block_state(queries, block_keys, block_values, None))
    blended = attn_state[2] / attn_state[1][..., None]
    live_rows = query_pos[None, :] < resp_len[:, None]
    blended = jnp.where(live_rows[:, None, :, None], blended, 0.0)
    attended = blended.transpose(0, 2, 1, 3).reshape(row_count, head_cols).astype(jnp.bfloat16)
    summed = lax.psum_scatter(
        jnp.dot(attended, out_weight[0], preferred_element_type=jnp.float32).astype(jnp.bfloat16),
        "tp",
        scatter_dimension=0,
        tiled=True,
    ).astype(jnp.float32)
    layer_out = (widened + summed).astype(jnp.bfloat16)
    return from_behind(layer_out, "section", 1)


def solution(mesh):
    in_specs = (
        P(("section", "tp"), None),
        P("section", None),
        P("section", None, "tp"),
        P("section", None, "tp"),
        P("section", "tp", None),
        P("section", None, "tp", None),
        P("section"),
        P("section"),
    )
    out_specs = P(("section", "tp"), None)
    return jax.shard_map(body, mesh=mesh, in_specs=in_specs, out_specs=out_specs, check_vma=False)
```

profile of v0, /device:TPU:2, one launch (start us, length us, event | category | flops | bytes accessed | tf_op | source)
XLA Modules:
  0.0 476.1 jit_solution(802149036153354014)
XLA Ops:
  6.5 0.0 copy-start
  6.5 0.7 all-gather.8.cloned.1.call-update
  7.3 0.0 all-gather.4.cloned.1.call-start
  7.3 1.5 fusion.7
  8.9 2.5 fusion.9
  11.4 0.0 all-gather.4.cloned.1.call-update
  11.4 0.0 all-gather.6.cloned.1.call-start
  11.5 6.4 %copy.33 = bf16[256,8192]{1,0:T(8,128)(2,1)} copy(bf16[256,8192]{0,1:T(8,128)(2,1)} %bitcast.104) | data formatting | bytes 8388608 | tf_op jit(solution)/shard_map/dot_general | solution.py:81
  17.9 0.2 multiply_cosine_fusion
  18.1 0.1 copy.19
  18.2 0.1 copy.18
  18.4 0.0 copy-done.7
  18.4 0.1 iota_compare_fusion.1
  18.4 0.2 broadcast_and_fusion
  18.7 71.6 %all-gather.8.cloned.1.call-done = bf16[1,4,1024,1024]{3,2,1,0:T(8,128)(2,1)} async-done(((bf16[1,4,64,1024]{3,2,1,0:T(8,128)(2,1)}), bf16[1,4,1024,1024]{3,2,1,0:T(8,128)(2,1)}) %all-gather.8.cloned.1.call-update) | async-done | bytes 8388624 | tf_op jit(solution)/shard_map/all_gather | solution.py:111
  90.3 6.0 %fusion.52 = (bf16[4,512,1024]{2,1,0:T(8,128)(2,1)}, bf16[4,512,1024]{2,1,0:T(8,128)(2,1)}) fusion(bf16[4,1024,1024]{2,1,0:T(8,128)(2,1)} %bitcast.102), kind=kLoop, calls=%fused_computation.77 | loop fusion | bytes 16777216 | tf_op jit(solution)/shard_map/jit(_take)/gather | solution.py:111
  96.2 6.8 %gather_fusion.1 = bf16[8,512,1024]{2,1,0:T(8,128)(2,1)} fusion(bf16[4,512,1024]{2,1,0:T(8,128)(2,1)} %get-tuple-element.9, s32[1024]{0:T(1024)S(1)} %pad_clamp_fusion), kind=kCustom, calls=%fused_computation.1 | custom fusion | bytes 16777248 | tf_op jit(solution)/shard_map/jit(_take)/gather | solution.py:111
  103.0 7.3 %gather_fusion = bf16[8,512,1024]{2,1,0:T(8,128)(2,1)} fusion(bf16[4,512,1024]{2,1,0:T(8,128)(2,1)} %get-tuple-element.8, s32[1024]{0:T(1024)S(1)} %pad_clamp_fusion), kind=kCustom, calls=%fused_computation | custom fusion | bytes 16777248 | tf_op jit(solution)/shard_map/jit(_take)/gather | solution.py:111
  110.3 94.8 %all-gather.4.cloned.1.call-done = bf16[1024,8192]{1,0:T(8,128)(2,1)} async-done(((bf16[64,8192]{1,0:T(8,128)(2,1)}), bf16[1024,8192]{1,0:T(8,128)(2,1)}) %all-gather.4.cloned.1.call-update) | async-done | bytes 16777232 | tf_op jit(solution)/shard_map/all_gather | solution.py:78
  205.2 11.6 %fusion.32 = bf16[64,1024]{1,0:T(8,128)(2,1)} fusion(bf16[1024,8192]{1,0:T(8,128)(2,1)} %all-gather.4.cloned.1.call-done, bf16[1,8192,64]{1,2,0:T(8,128)(2,1)S(1)} %copy-done), kind=kOutput, calls=%fused_computation.36 | convolution fusion | flops 1073807360 | bytes 17956864 | tf_op jit(solution)/shard_map/dot_general | solution.py:82
  216.8 0.0 all-gather.6.cloned.1.call-update
  216.8 0.2 reduce-scatter.2.cloned.1.call-start
  217.1 10.4 %maximum_select_fusion = bf16[8,1024,1024]{2,1,0:T(8,128)(2,1)S(1)} fusion(bf16[8,512,1024]{2,1,0:T(8,128)(2,1)} %gather_fusion.1, bf16[8,512,1024]{2,1,0:T(8,128)(2,1)} %gather_fusion, pred[8]{0:T(512)(128)(4,1)S(1)} %compare_and_fusion), kind=kLoop, calls=%fused_computation.2 | loop fusion | flops 41943040 | bytes 33554440 | tf_op jit(solution)/shard_map/jit(_take)/select_n | solution.py:111
  227.4 0.0 copy-start.3
  227.4 0.0 copy-done.5
  227.4 14.3 %convolution_bitcast_fusion.1 = f32[8,2,128,128]{2,3,1,0:T(8,128)S(1)} fusion(bf16[8,128,8192,1]{2,1,3,0:T(8,128)(2,1)} %bitcast.101, bf16[2,128,8192,1]{2,1,0,3:T(8,128)(2,1)S(1)} %bitcast.105), kind=kOutput, calls=%fused_computation.32 | convolution fusion | flops 4294967296 | bytes 22020096 | tf_op jit(solution)/shard_map/dot_general | solution.py:81
  241.8 0.2 subtract_convert_fusion.1
  242.0 0.0 copy-done.3
  242.0 1.5 multiply_reduce_fusion
  243.5 3.2 copy-done.2
  246.7 1.7 fusion
  248.5 18.8 %all-gather.6.cloned.1.call-done = bf16[1024,1024]{1,0:T(8,128)(2,1)} async-done(((bf16[64,1024]{1,0:T(8,128)(2,1)}), bf16[1024,1024]{1,0:T(8,128)(2,1)}) %all-gather.6.cloned.1.call-update) | async-done | bytes 2097168 | tf_op jit(solution)/shard_map/all_gather | solution.py:97
  267.3 1.1 constant_dynamic-slice_fusion
  268.4 0.2 copy.34
  268.6 0.3 subtract_convert_fusion
  268.9 0.4 fusion.53
  269.2 0.2 fusion.34
  269.4 5.2 %fusion.26 = f32[8,128,2,128]{3,1,2,0:T(8,128)S(1)} fusion(bf16[8,1024,1024]{2,1,0:T(8,128)(2,1)} %copy-done.3, s32[]{:T(128)S(6)} %select_n.34, f32[8,2,128,1024]{3,2,1,0:T(8,128)} %copy-done.2, f32[8,2,128]{2,1,0:T(2,128)S(1)} %get-tuple-element.18, f32[8,128,2]{1,2,0:T(2,128)S(1)} %get-tuple-element.7), kind=kOutput, calls=%fused_computation.33 | convolution fusion | flops 543424512 | bytes 11550724 | tf_op jit(solution)/shard_map/shqk,skd->shqd/dot_general | solution.py:49
  274.6 0.2 copy.21
  274.8 1.1 fusion.31
  275.9 0.3 copy.24
  276.2 10.4 %convolution_convert_fusion = bf16[1024,8192]{1,0:T(8,128)(2,1)} fusion(bf16[1,256,8192]{2,1,0:T(8,128)(2,1)} %param.12, bf16[32,8,8,128]{3,2,1,0:T(8,128)(2,1)S(1)} %bitcast.106), kind=kOutput, calls=%fused_computation.3 | convolution fusion | flops 4303355904 | bytes 21495808 | tf_op jit(solution)/shard_map/dot_general | solution.py:120
  286.6 0.0 reduce-scatter.2.cloned.1.call-update
  286.6 153.6 %reduce-scatter.2.cloned.1.call-done = bf16[64,8192]{1,0:T(8,128)(2,1)} async-done(((bf16[1024,8192]{1,0:T(8,128)(2,1)}), bf16[64,8192]{1,0:T(8,128)(2,1)}) %reduce-scatter.2.cloned.1.call-update) | async-done | bytes 1048592 | tf_op jit(solution)/shard_map/reduce_scatter | solution.py:119
  440.2 1.5 fusion.10
  441.7 1.6 collective-permute-start
  443.3 25.2 %collective-permute-done = bf16[64,8192]{1,0:T(8,128)(2,1)S(1)} collective-permute-done((bf16[64,8192]{1,0:T(8,128)(2,1)S(1)}, bf16[64,8192]{1,0:T(8,128)(2,1)S(1)}, u32[]{:S(2)}, u32[]{:S(2)}) %collective-permute-start) | collective-permute-done | bytes 1048608 | tf_op jit(solution)/shard_map/ppermute | solution.py:14
  468.6 1.0 copy.41
  (19 shorter events, 0.1 us)
Async XLA Ops:
  6.5 198.6 %copy-start = (bf16[1,8192,64]{1,2,0:T(8,128)(2,1)S(1)}, bf16[1,8192,64]{1,2,0:T(8,128)(2,1)}, u32[]{:S(2)}) copy-start(bf16[1,8192,64]{1,2,0:T(8,128)(2,1)} %param.11) | copy-start | bytes 3145732
  6.5 11.8 %copy-start.6 = (s32[8]{0:T(128)S(1)}, s32[8]{0:T(128)}, u32[]{:S(2)}) copy-start(s32[8]{0:T(128)} %param.15) | copy-start | bytes 100
  6.5 11.8 %copy-start.7 = (s32[8]{0:T(128)S(1)}, s32[8]{0:T(128)}, u32[]{:S(2)}) copy-start(s32[8]{0:T(128)} %param.14) | copy-start | bytes 100
  6.5 83.7 %all-gather.8.cloned.1.call-start = ((), (), s32[]{:S(2)}) async-start(), calls=%async_computation.3 | async-start | bytes 8912896 | tf_op jit(solution)/shard_map/all_gather | solution.py:111
  7.3 197.9 %all-gather.4.cloned.1.call-start = ((), (), s32[]{:S(2)}) async-start(), calls=%async_computation.1 | async-start | bytes 17825792 | tf_op jit(solution)/shard_map/all_gather | solution.py:78
  11.4 255.9 %all-gather.6.cloned.1.call-start = ((), (), s32[]{:S(2)}) async-start(), calls=%async_computation.2 | async-start | bytes 2228224 | tf_op jit(solution)/shard_map/all_gather | solution.py:97
  216.8 223.4 %reduce-scatter.2.cloned.1.call-start = ((), (), s32[]{:S(2)}) async-start(), calls=%async_computation.4 | async-start | bytes 17825792 | tf_op jit(solution)/shard_map/reduce_scatter | solution.py:119
  217.0 10.4 %copy-start.5 = (bf16[256,8192]{1,0:T(8,128)(2,1)S(1)}, bf16[256,8192]{1,0:T(8,128)(2,1)}, u32[]{:S(2)}) copy-start(bf16[256,8192]{1,0:T(8,128)(2,1)} %copy.33) | copy-start | bytes 12582916
  227.4 14.5 %copy-start.3 = (bf16[8,1024,1024]{2,1,0:T(8,128)(2,1)}, bf16[8,1024,1024]{2,1,0:T(8,128)(2,1)S(1)}, u32[]{:S(2)}) copy-start(bf16[8,1024,1024]{2,1,0:T(8,128)(2,1)S(1)} %maximum_select_fusion) | copy-start | bytes 50331652
  243.5 3.2 copy-start.2
  286.6 182.9 %copy-start.1 = (bf16[1,8192,64]{1,2,0:T(8,128)(2,1)S(1)}, bf16[1,8192,64]{1,2,0:T(8,128)(2,1)}, u32[]{:S(2)}) copy-start(bf16[1,8192,64]{1,2,0:T(8,128)(2,1)} %param.11) | copy-start | bytes 3145732
  286.6 153.6 %copy-start.4 = (bf16[64,8192]{1,0:T(8,128)(2,1)S(1)}, bf16[64,8192]{1,0:T(8,128)(2,1)}, u32[]{:S(2)}) copy-start(bf16[64,8192]{1,0:T(8,128)(2,1)} %param.8) | copy-start | bytes 3145732
  441.7 26.9 %collective-permute-start = (bf16[64,8192]{1,0:T(8,128)(2,1)S(1)}, bf16[64,8192]{1,0:T(8,128)(2,1)S(1)}, u32[]{:S(2)}, u32[]{:S(2)}) collective-permute-start(bf16[64,8192]{1,0:T(8,128)(2,1)S(1)} %fusion.10), channel_id=1, source_target_pairs={{0,16},{16,32},{32,48},{48,64},{64,80},{80,96},{96,112},{112,128},... | collective-permute-start | bytes 3145736 | tf_op jit(solution)/shard_map/ppermute | solution.py:14
Sparse Core Ops, SparseCore 0:
  10.2 80.0 all-gather.7
  93.0 112.0 all-gather.3
  216.9 50.3 all-gather.5
  286.7 153.4 reduce-scatter.1
where the time goes:
time: 477 us; the launch traced here: 476 us
  waiting for transfers between devices  365 us (77%)
  matrix products  44.5 us (9%)
  local copies, waits for them, and re-layouts  31.5 us (7%)
  other arithmetic  19.8 us (4%)
  between operations  13.4 us (3%)
    reduce_scatter x1, waiting for transfers between devices, body(): lax.psum_scatter(jnp.dot(attended, out_weight[0], preferred_element_type=...  154 us
    all_gather x1, waiting for transfers between devices, body(): shard_piece = lax.all_gather(normed, 'tp', axis=0, tiled=True)  94.8 us
    all_gather x1, waiting for transfers between devices, body(): lax.all_gather(prompt_cache, 'tp', axis=2, tiled=True)[0]  71.6 us
    ppermute x1, waiting for transfers between devices, from_behind(): lax.ppermute(value, axis, [(i, (i + by) % length) for i in range(length)])  25.2 us
    gather x3, local copies, waits for them, and re-layouts, body(): jnp.take(lax.all_gather(prompt_cache, 'tp', axis=2, tiled=True)[0], promp...  20.1 us
    all_gather x1, waiting for transfers between devices, body(): kv_all = lax.all_gather(kv_part, 'tp', axis=0, tiled=True)  18.8 us
    dot_general x1, matrix products, body(): jnp.dot(shard_piece, query_weight[0], preferred_element_type=jnp.float32)  14.3 us
    dot_general x1, matrix products, body(): jnp.dot(shard_piece, kv_weight[0], preferred_element_type=jnp.float32)  11.6 us
  transfers between devices with their start and end apart: 5, of which 5 were waited for; matrix products, arithmetic and copies ran while one was open for 12% of the time, Pallas kernels for 0%

commit v1 on v0

v1 whole, which is shorter than its diff:
```python
import functools

import jax
import jax.numpy as jnp
from jax import lax
from jax.experimental import pallas as pl
from jax.experimental.pallas import tpu as pltpu
from jax.sharding import Mesh, PartitionSpec as P

D = 8192
QH = 32
KVH = 4
HD = 128
PROMPT = 1024
NPROMPT = 4
RESP = 128
ROWS = 64
EPS = 1e-06
F32 = jnp.float32
BF16 = jnp.bfloat16
VMEM = 48 * 1024 * 1024

PLACES = ((0, 0), (1, 0), (0, 3), (0, 1), (0, 2), (1, 3), (1, 1), (1, 2))


def shift(value, axis, by):
    size = lax.axis_size(axis)
    return lax.ppermute(value, axis, [(i, (i + by) % size) for i in range(size)])


def params(**kw):
    return pltpu.CompilerParams(vmem_limit_bytes=VMEM, **kw)


def norm_kernel(x_ref, gain_ref, out_ref):
    wide = x_ref[...].astype(F32)
    mean = jnp.mean(wide * wide, axis=-1, keepdims=True)
    out_ref[...] = (wide * lax.rsqrt(mean + EPS) * gain_ref[...]).astype(BF16)


def norm(hidden, gain):
    return pl.pallas_call(
        norm_kernel,
        out_shape=jax.ShapeDtypeStruct((ROWS, D), BF16),
        grid=(2,),
        in_specs=[
            pl.BlockSpec((ROWS // 2, D), lambda i: (i, 0)),
            pl.BlockSpec((1, D), lambda i: (0, 0)),
        ],
        out_specs=pl.BlockSpec((ROWS // 2, D), lambda i: (i, 0)),
        compiler_params=params(),
        name="norm",
    )(hidden, gain)


def turned(value, cosines, sines):
    return value * cosines + pltpu.roll(value, HD // 2, 1) * sines


def query_kernel(count, *refs):
    pieces = refs[:count]
    wa_ref, wb_ref, cos_ref, sin_ref, out_ref, acc_ref = refs[count:]
    step = pl.program_id(0)
    rows = jnp.concatenate([piece[...] for piece in pieces], axis=0)
    half = wa_ref.shape[1]

    @pl.when(step == 0)
    def _():
        acc_ref[...] = jnp.zeros_like(acc_ref)

    acc_ref[:, :half] += jnp.dot(rows, wa_ref[...], preferred_element_type=F32)
    acc_ref[:, half:] += jnp.dot(rows, wb_ref[...], preferred_element_type=F32)

    @pl.when(step == pl.num_programs(0) - 1)
    def _():
        for block in range(out_ref.shape[0]):
            for head in range(4):
                part = acc_ref[block * ROWS : (block + 1) * ROWS, head * HD : (head + 1) * HD]
                out_ref[block, head * ROWS : (head + 1) * ROWS, :] = turned(
                    part, cos_ref[...], sin_ref[...]
                ).astype(BF16)


def project_queries(pieces, own, other, cosines, sines):
    depth = 4096
    rows = sum(piece.shape[0] for piece in pieces)
    half = own.shape[1]
    return pl.pallas_call(
        functools.partial(query_kernel, len(pieces)),
        out_shape=jax.ShapeDtypeStruct((rows // ROWS, 4 * ROWS, HD), BF16),
        grid=(D // depth,),
        in_specs=[pl.BlockSpec((piece.shape[0], depth), lambda k: (0, k)) for piece in pieces]
        + [pl.BlockSpec((depth, half), lambda k: (k, 0))] * 2
        + [pl.BlockSpec((ROWS, HD), lambda k: (0, 0))] * 2,
        out_specs=pl.BlockSpec((rows // ROWS, 4 * ROWS, HD), lambda k: (0, 0, 0)),
        scratch_shapes=[pltpu.VMEM((rows, 2 * half), F32)],
        compiler_params=params(),
        cost_estimate=pl.CostEstimate(
            flops=2 * rows * D * 2 * half,
            bytes_accessed=2 * D * (rows + 2 * half),
            transcendentals=0,
        ),
        name="queries",
    )(*pieces, own, other, cosines, sines)


def dot_t(a, b):
    return lax.dot_general(a, b, (((1,), (1,)), ((), ())), preferred_element_type=F32)


def pair_kernel(count, *refs):
    pieces = refs[:count]
    core_ref, wa_ref, wb_ref, cos_ref, sin_ref, out_ref, acc_ref = refs[count:]
    step = pl.program_id(0)
    rows = jnp.concatenate([piece[...] for piece in pieces], axis=0)
    weight = jnp.concatenate([wa_ref[...], wb_ref[...]], axis=0)

    @pl.when(step == 0)
    def _():
        acc_ref[...] = jnp.zeros_like(acc_ref)

    acc_ref[...] += dot_t(rows, weight)

    @pl.when(step == pl.num_programs(0) - 1)
    def _():
        pairs = acc_ref[...].astype(BF16).astype(F32)
        pairs = jnp.where(core_ref[0] == 0, pairs, pltpu.roll(pairs, HD // 2, 1))
        for block in range(out_ref.shape[0]):
            part = pairs[block * ROWS : (block + 1) * ROWS, :]
            out_ref[block] = turned(part, cos_ref[...], sin_ref[...]).astype(BF16)


def project_pairs(pieces, core, own, other, cosines, sines):
    depth = 4096
    rows = sum(piece.shape[0] for piece in pieces)
    return pl.pallas_call(
        functools.partial(pair_kernel, len(pieces)),
        out_shape=jax.ShapeDtypeStruct((rows // ROWS, ROWS, HD), BF16),
        grid=(D // depth,),
        in_specs=[pl.BlockSpec((piece.shape[0], depth), lambda k: (0, k)) for piece in pieces]
        + [pl.BlockSpec(memory_space=pltpu.SMEM)]
        + [pl.BlockSpec((HD // 2, depth), lambda k: (0, k))] * 2
        + [pl.BlockSpec((ROWS, HD), lambda k: (0, 0))] * 2,
        out_specs=pl.BlockSpec((rows // ROWS, ROWS, HD), lambda k: (0, 0, 0)),
        scratch_shapes=[pltpu.VMEM((rows, HD), F32)],
        compiler_params=params(),
        cost_estimate=pl.CostEstimate(
            flops=2 * rows * D * HD, bytes_accessed=2 * D * (rows + HD), transcendentals=0
        ),
        name="pairs",
    )(*pieces, core, own, other, cosines, sines)


def sort_kernel(key_ref, value_ref, out_ref):
    out_ref[0, :, :, :HD] = key_ref[...]
    out_ref[0, :, :, HD:] = value_ref[...]


def sort_cache(cache):
    return pl.pallas_call(
        sort_kernel,
        out_shape=jax.ShapeDtypeStruct((2 * KVH, NPROMPT, ROWS, 2 * HD), BF16),
        grid=(2 * KVH,),
        in_specs=[
            pl.BlockSpec((NPROMPT, ROWS, HD), lambda i: (0, 0, i // 2)),
            pl.BlockSpec((NPROMPT, ROWS, HD), lambda i: (0, 0, KVH + i // 2)),
        ],
        out_specs=pl.BlockSpec((1, NPROMPT, ROWS, 2 * HD), lambda i: (i, 0, 0, 0)),
        compiler_params=params(),
        name="sort_cache",
    )(cache, cache)


def prompt_kernel(prompt_ref, q_ref, own_ref, other_ref, acc_ref, state_ref):
    queries = q_ref[0]
    half = PROMPT // 2
    own = own_ref[...].reshape(half, 2 * HD)
    other = other_ref[...].reshape(half, 2 * HD)
    score_a = dot_t(queries, own[:, :HD]) * HD ** (-0.5)
    score_b = dot_t(queries, other[:, :HD]) * HD ** (-0.5)
    top = jnp.maximum(
        jnp.max(score_a, axis=-1, keepdims=True), jnp.max(score_b, axis=-1, keepdims=True)
    )
    prob_a = jnp.exp(score_a - top)
    prob_b = jnp.exp(score_b - top)
    total = jnp.sum(prob_a, axis=-1, keepdims=True) + jnp.sum(prob_b, axis=-1, keepdims=True)
    acc_ref[0] = jnp.dot(
        prob_a.astype(BF16), own[:, HD:], preferred_element_type=F32
    ) + jnp.dot(prob_b.astype(BF16), other[:, HD:], preferred_element_type=F32)
    lane = lax.broadcasted_iota(jnp.int32, (4 * ROWS, HD), 1)
    state_ref[0] = jnp.where(lane < HD // 2, top, total)


def attend_prompt(queries, own, other, prompts):
    count = queries.shape[0]
    shape = jax.ShapeDtypeStruct((count, 4 * ROWS, HD), F32)
    block = pl.BlockSpec((1, 4 * ROWS, HD), lambda i, p: (i, 0, 0))
    cache = pl.BlockSpec((8, 1, ROWS, 2 * HD), lambda i, p: (0, p[i], 0, 0))
    return pl.pallas_call(
        prompt_kernel,
        out_shape=(shape, shape),
        grid_spec=pltpu.PrefetchScalarGridSpec(
            num_scalar_prefetch=1,
            grid=(count,),
            in_specs=[block, cache, cache],
            out_specs=(block, block),
        ),
        compiler_params=params(),
        cost_estimate=pl.CostEstimate(
            flops=count * 4 * 4 * ROWS * PROMPT * HD,
            bytes_accessed=count * PROMPT * HD * 6,
            transcendentals=count * 4 * ROWS * PROMPT,
        ),
        name="attend_prompt",
    )(prompts, queries, own, other)


def own_kernel(
    info_ref, q_ref, acc_ref, state_ref, key_a, key_b, value_a, value_b, out_ref
):
    i = pl.program_id(0)
    length = info_ref[0, i]
    core = info_ref[1, i]
    queries = q_ref[0]
    keys = jnp.concatenate([key_a[0, 0], key_b[0, 0]], axis=0)
    values = jnp.concatenate([value_a[0, 0], value_b[0, 0]], axis=0)
    scores = dot_t(queries, keys) * HD ** (-0.5)
    row = lax.broadcasted_iota(jnp.int32, (4 * ROWS, HD), 0) % ROWS + core * ROWS
    lane = lax.broadcasted_iota(jnp.int32, (4 * ROWS, HD), 1)
    place = jnp.where(lane < ROWS, lane + core * ROWS, lane - core * ROWS)
    visible = (place <= row) & (place < length)
    scores = jnp.where(visible, scores, -jnp.inf)
    top_a = state_ref[0, :, :1]
    total_a = state_ref[0, :, HD // 2 : HD // 2 + 1]
    top = jnp.maximum(top_a, jnp.max(scores, axis=-1, keepdims=True))
    scale = jnp.exp(top_a - top)
    probs = jnp.exp(scores - top)
    total = total_a * scale + jnp.sum(probs, axis=-1, keepdims=True)
    blended = acc_ref[0] * scale + jnp.dot(
        probs.astype(BF16), values, preferred_element_type=F32
    )
    blended = jnp.where(row < length, blended / total, 0.0).astype(BF16)
    for head in range(4):
        out_ref[:, head * HD : (head + 1) * HD] = blended[head * ROWS : (head + 1) * ROWS, :]


def attend_own(queries, acc, state, pairs_own, pairs_other, info):
    count = queries.shape[0]
    block = pl.BlockSpec((1, 4 * ROWS, HD), lambda i, t: (i, 0, 0))
    key = pl.BlockSpec((1, 1, ROWS, HD), lambda i, t: (t[2, i], t[3, i], 0, 0))
    value = pl.BlockSpec((1, 1, ROWS, HD), lambda i, t: (1 - t[2, i], t[4, i], 0, 0))
    return pl.pallas_call(
        own_kernel,
        out_shape=jax.ShapeDtypeStruct((count * ROWS, 4 * HD), BF16),
        grid_spec=pltpu.PrefetchScalarGridSpec(
            num_scalar_prefetch=1,
            grid=(count,),
            in_specs=[block, block, block, key, key, value, value],
            out_specs=pl.BlockSpec((ROWS, 4 * HD), lambda i, t: (i, 0)),
        ),
        compiler_params=params(),
        cost_estimate=pl.CostEstimate(
            flops=count * 4 * 4 * ROWS * RESP * HD,
            bytes_accessed=count * 4 * ROWS * HD * 12,
            transcendentals=count * 4 * ROWS * RESP,
        ),
        name="attend_own",
    )(info, queries, acc, state, pairs_own, pairs_other, pairs_own, pairs_other)


def output_kernel(x_ref, wa_ref, wb_ref, *out_refs):
    half = wa_ref.shape[0]
    total = jnp.dot(x_ref[:, :half], wa_ref[...], preferred_element_type=F32)
    total += jnp.dot(x_ref[:, half:], wb_ref[...], preferred_element_type=F32)
    for block, out_ref in enumerate(out_refs):
        out_ref[...] = total[block * ROWS : (block + 1) * ROWS, :].astype(BF16)


def project_out(attended, own, other, start, width):
    count = attended.shape[0] // ROWS
    tile = 1024
    first = start // tile
    half = own.shape[0]
    return pl.pallas_call(
        output_kernel,
        out_shape=[jax.ShapeDtypeStruct((ROWS, width), BF16)] * count,
        grid=(width // tile,),
        in_specs=[
            pl.BlockSpec((count * ROWS, 2 * half), lambda n: (0, 0)),
            pl.BlockSpec((half, tile), lambda n: (0, n + first)),
            pl.BlockSpec((half, tile), lambda n: (0, n + first)),
        ],
        out_specs=[pl.BlockSpec((ROWS, tile), lambda n: (0, n))] * count,
        compiler_params=params(),
        cost_estimate=pl.CostEstimate(
            flops=2 * count * ROWS * 2 * half * width,
            bytes_accessed=2 * width * (2 * half + count * ROWS),
            transcendentals=0,
        ),
        name="project_out",
    )(attended, own, other)


def sum_kernel(*refs):
    total = refs[0][...].astype(F32)
    for ref in refs[1:-1]:
        total += ref[...].astype(F32)
    refs[-1][...] = total.astype(BF16)


def split_kernel(a_ref, b_ref, low_ref, high_ref):
    total = (a_ref[...].astype(F32) + b_ref[...].astype(F32)).astype(BF16)
    half = low_ref.shape[1]
    low_ref[...] = total[:, :half]
    high_ref[...] = total[:, half:]


def split_sum(a, b):
    half = jax.ShapeDtypeStruct((a.shape[0], a.shape[1] // 2), BF16)
    return pl.pallas_call(
        split_kernel, out_shape=(half, half), compiler_params=params(), name="split_sum"
    )(a, b)


def relay_kernel(a_ref, up_ref, b_ref, down_ref, a_out, b_out):
    half = up_ref.shape[1]
    a_out[:, :half] = (a_ref[:, :half].astype(F32) + up_ref[...].astype(F32)).astype(BF16)
    a_out[:, half:] = a_ref[:, half:]
    b_out[:, :half] = b_ref[:, :half]
    b_out[:, half:] = (b_ref[:, half:].astype(F32) + down_ref[...].astype(F32)).astype(BF16)


def relay_sum(a, up, b, down):
    whole = jax.ShapeDtypeStruct(a.shape, BF16)
    return pl.pallas_call(
        relay_kernel, out_shape=(whole, whole), compiler_params=params(), name="relay_sum"
    )(a, up, b, down)


def add(*terms):
    return pl.pallas_call(
        sum_kernel,
        out_shape=jax.ShapeDtypeStruct(terms[0].shape, BF16),
        compiler_params=params(),
        name="add",
    )(*terms)


def after(value, *others):
    return lax.optimization_barrier((value, *others))[0]


def rope_tables():
    half = HD // 2
    position = (PROMPT + jnp.arange(RESP)).astype(F32)
    inverse = jnp.exp(-(2.0 * jnp.arange(half).astype(F32) / HD) * jnp.log(10000.0))
    angles = position[:, None] * inverse[None, :]
    cosines, sines = jnp.cos(angles), jnp.sin(angles)
    return (
        jnp.concatenate([cosines, cosines], axis=1),
        jnp.concatenate([-sines, sines], axis=1),
    )


def body(hidden, norm_gain, query_weight, kv_weight, out_weight, prompt_cache, resp_len, prompt_id):
    xh, y, core = lax.axis_index("xh"), lax.axis_index("y"), lax.axis_index("c")
    wq, wkv, wo = query_weight[0], kv_weight[0].T, out_weight[0]
    chips = ("xh", "y")

    normed = norm(hidden, norm_gain)
    b10 = shift(normed, "xh", 1)
    b03 = shift(normed, "y", 1)
    b01 = shift(normed, "y", -1)
    wkv_other = shift(wkv, "c", 1)
    wq_other = shift(wq, "c", 1)
    wo_other = shift(wo, "c", 1)
    cache = sort_cache(prompt_cache[0])

    cosines, sines = rope_tables()
    cosines = lax.dynamic_slice_in_dim(cosines, core * ROWS, ROWS, 0)
    sines = lax.dynamic_slice_in_dim(sines, core * ROWS, ROWS, 0)
    key_cosines = jnp.where(xh == 0, cosines, 1.0)
    key_sines = jnp.where(xh == 0, sines, 0.0)

    def pick(values, index):
        lanes = jnp.arange(8)
        return jnp.sum(jnp.where(index[:, None] == lanes[None, :], values[None, :], 0), axis=1)

    responses = jnp.stack([(xh ^ dx) * 4 + (y + dy) % 4 for dx, dy in PLACES])
    prompts = pick(prompt_id, responses).astype(jnp.int32)
    lengths = pick(resp_len, responses)
    maker_y = xh * 2 + y // 2
    table = [0] * 8
    for at, (dx, dy) in enumerate(PLACES):
        table[dx * 4 + dy] = at
    table = jnp.array(table, jnp.int32)
    away = (responses % 4 - maker_y) % 4
    key_at = pick(table, (responses // 4) * 4 + away)
    value_at = pick(table, (1 - responses // 4) * 4 + away)
    info = jnp.stack(
        [
            lengths,
            jnp.full((8,), core, jnp.int32),
            jnp.full((8,), y % 2, jnp.int32),
            key_at,
            value_at,
        ]
    ).astype(jnp.int32)
    core_word = jnp.full((1,), core, jnp.int32)

    b03 = after(b03, wkv_other, wq_other, wo_other, cache, info, key_cosines, key_sines)
    b01 = after(b01, b03)
    top02 = shift(b03[: ROWS // 2], "y", 1)
    low02 = shift(b01[ROWS // 2 :], "y", -1)
    b13 = shift(b10, "y", 1)
    b11 = shift(b10, "y", -1)
    top12 = shift(top02, "xh", 1)
    low12 = shift(low02, "xh", 1)
    cache = lax.all_to_all(after(cache, top02, low02), chips, 0, 0, tiled=True)
    cache_other = shift(cache, "c", 1)

    near = [normed, b10, b03, b01, top02, low02]
    far = [b13, b11, top12, low12]
    pairs_near = project_pairs(near, core_word, wkv, wkv_other, key_cosines, key_sines)
    q_near = project_queries(near, wq, wq_other, cosines, sines)
    far[0] = after(far[0], pairs_near, q_near)
    pairs_far = project_pairs(far, core_word, wkv, wkv_other, key_cosines, key_sines)
    pairs = jnp.concatenate([pairs_near, pairs_far], axis=0)
    straight = [(g, 2 * g) for g in range(4)] + [(4 + g, 2 * g + 1) for g in range(4)]
    crossed = [(g, 2 * g + 1) for g in range(4)] + [(4 + g, 2 * g) for g in range(4)]
    pairs = jnp.stack(
        [lax.ppermute(pairs, chips, straight), lax.ppermute(pairs, chips, crossed)]
    )
    pairs_other = shift(pairs, "c", 1)
    q_far = project_queries(far, wq, wq_other, cosines, sines)
    acc, state = attend_prompt(q_far, cache, cache_other, prompts[5:])
    acc_near, state_near = attend_prompt(q_near, cache, cache_other, after(prompts[:5], acc))
    pairs = after(pairs, acc_near)
    att_far = attend_own(q_far, acc, state, pairs, pairs_other, info[:, 5:])

    parts = 2
    width = D // parts
    far = []
    sent = []
    for part in range(parts):
        p13, p11, p12 = project_out(att_far, wo, wo_other, part * width, width)
        sent.append((shift(p11, "y", 1), shift(p13, "y", -1), shift(p12, "xh", 1)))
        att_far = after(att_far, p11)
    att_near = attend_own(
        q_near, acc_near, state_near, after(pairs, p11), pairs_other, info[:, :5]
    )
    mine = []
    for part in range(parts):
        mine.append(project_out(att_near, wo, wo_other, part * width, width))
        att_near = after(att_near, mine[-1][0])
    hops = []
    for part in range(parts):
        p00, p10, p03, p01, p02 = mine[part]
        up, down = split_sum(p02, sent[part][2])
        hops.append((shift(up, "y", 1), shift(down, "y", -1)))
    lasts = []
    for part in range(parts):
        p00, p10, p03, p01, p02 = mine[part]
        across = shift(add(p10, sent[part][0], sent[part][1]), "xh", 1)
        p01, p03 = relay_sum(p01, hops[part][0], p03, hops[part][1])
        lasts.append((shift(p01, "y", 1), shift(p03, "y", -1), across))
    outs = []
    for part in range(parts):
        own_rows = hidden[:, part * width : (part + 1) * width]
        total = add(own_rows, mine[part][0], *lasts[part])
        outs.append(
            lax.ppermute(total, ("xl", "z"), [(i, (i + 1) % 16) for i in range(16)])
        )
    return jnp.concatenate(outs, axis=1)


def solution(mesh):
    whole = Mesh(mesh.devices.reshape(2, 8, 2, 4, 2), ("xl", "z", "xh", "y", "c"))
    section, tp = ("xl", "z"), ("xh", "y", "c")
    in_specs = (
        P(section + tp, None),
        P(section, None),
        P(section, None, tp),
        P(section, None, tp),
        P(section, tp, None),
        P(section, None, tp, None),
        P(section),
        P(section),
    )
    out_specs = P(section + tp, None)
    return jax.shard_map(body, mesh=whole, in_specs=in_specs, out_specs=out_specs, check_vma=False)
```

time: 477 us -> 215 us (0.45)
  waiting for transfers between devices: 365 us -> 96.6 us
  starting transfers between devices: 1.94 us -> 55.9 us
  Pallas kernels: 0 us -> 52.9 us
  matrix products: 44.5 us -> 0 us
  local copies, waits for them, and re-layouts: 31.5 us -> 4.42 us
  other arithmetic: 19.8 us -> 3.27 us
  between operations: 13.4 us -> 0.48 us
    all_gather x3 -> x0, waiting for transfers between devices: 185 us -> none  [the longest x1 94.8 us: body(): shard_piece = lax.all_gather(normed, 'tp', axis=0, tiled=True)]
    reduce_scatter x1 -> x0, waiting for transfers between devices: 154 us -> none  [body(): lax.psum_scatter(jnp.dot(attended, out_weight[0], preferred_element_type=...]
    ppermute x1 -> x34, waiting for transfers between devices: 25.2 us -> 87 us  [the longest x30 65.5 us: shift(): lax.ppermute(value, axis, [(i, (i + by) % size) for i in range(size)])]
    pallas_call x0 -> x22, Pallas kernels: none -> 52.9 us  [the longest x4 15.3 us: project_out(): pl.pallas_call(output_kernel, out_shape=[jax.ShapeDtypeStruct((ROWS, widt...]
    ppermute x1 -> x34, starting transfers between devices: 1.64 us -> 51.7 us  [the longest x30 42.8 us: shift(): lax.ppermute(value, axis, [(i, (i + by) % size) for i in range(size)])]
    dot_general x7 -> x0, matrix products: 44.5 us -> none  [the longest x1 14.3 us: body(): jnp.dot(shard_piece, query_weight[0], preferred_element_type=jnp.float32)]
    gather x3 -> x0, local copies, waits for them, and re-layouts: 20.1 us -> none  [body(): jnp.take(lax.all_gather(prompt_cache, 'tp', axis=2, tiled=True)[0], promp...]
    select_n x2 -> x1, other arithmetic: 10.4 us -> 0.09 us  [body(): key_sines = jnp.where(xh == 0, sines, 0.0)]
  transfers between devices with their start and end apart: 5 -> 35, of which waited for: 5 -> 16; matrix products, arithmetic and copies ran while one was open for 12% -> 1% of each run, Pallas kernels for 0% -> 22%
where the time goes in v1:
time: 215 us; the launch traced here: 214 us
  waiting for transfers between devices  96.6 us (45%)
  starting transfers between devices  55.9 us (26%)
  Pallas kernels  52.9 us (25%)
  local copies, waits for them, and re-layouts  4.42 us (2%)
  other arithmetic  3.27 us (2%)
    ppermute x30, waiting for transfers between devices, shift(): lax.ppermute(value, axis, [(i, (i + by) % size) for i in range(size)])  65.5 us
    ppermute x30, starting transfers between devices, shift(): lax.ppermute(value, axis, [(i, (i + by) % size) for i in range(size)])  42.8 us
    ppermute x2, waiting for transfers between devices, body(): lax.ppermute(total, ('xl', 'z'), [(i, (i + 1) % 16) for i in range(16)])  16.1 us
    pallas_call x4, Pallas kernels, project_out(): pl.pallas_call(output_kernel, out_shape=[jax.ShapeDtypeStruct((ROWS, widt...  15.3 us
    pallas_call x2, Pallas kernels, project_queries(): pl.pallas_call(functools.partial(query_kernel, len(pieces)), out_shape=ja...  12 us
    all_to_all x1, waiting for transfers between devices, body(): cache = lax.all_to_all(after(cache, top02, low02), chips, 0, 0, tiled=True)  9.69 us
    pallas_call x2, Pallas kernels, attend_prompt(): pl.pallas_call(prompt_kernel, out_shape=(shape, shape), grid_spec=pltpu.P...  9.49 us
    pallas_call x2, Pallas kernels, project_pairs(): pl.pallas_call(functools.partial(pair_kernel, len(pieces)), out_shape=jax...  7.15 us
  transfers between devices with their start and end apart: 35, of which 16 were waited for; matrix products, arithmetic and copies ran while one was open for 1% of the time, Pallas kernels for 22%

profile of v1, /device:TPU:2, one launch (start us, length us, event | category | flops | bytes accessed | tf_op | source)
XLA Modules:
  0.0 213.7 jit_solution(399031345918037361)
XLA Ops:
  0.5 1.2 copy-done.1
  3.2 1.7 collective-permute-start.1
  4.8 1.7 collective-permute-start.5
  7.9 21.7 %collective-permute-done.1.refs_2_ = bf16[64,8192]{1,0:T(8,128)(2,1)S(1)} collective-permute-done((bf16[64,8192]{1,0:T(8,128)(2,1)S(1)}, bf16[64,8192]{1,0:T(8,128)(2,1)S(1)}, u32[]{:S(2)}, u32[]{:S(2)}) %collective-permute-start.1) | collective-permute-done | bytes 1048608 | tf_op jit(solution)/shard_map/ppermute | solution.py:28
  29.6 2.1 collective-permute-start
  35.5 1.8 collective-permute-start.7
  37.6 10.9 %collective-permute-done.7.refs_5_ = bf16[32,8192]{1,0:T(8,128)(2,1)} collective-permute-done((bf16[32,8192]{1,0:T(8,128)(2,1)S(1)}, bf16[32,8192]{1,0:T(8,128)(2,1)}, u32[]{:S(2)}, u32[]{:S(2)}) %collective-permute-start.7) | collective-permute-done | bytes 524320 | tf_op jit(solution)/shard_map/ppermute | solution.py:28
  48.4 2.6 %collective-permute-done.6.refs_4_ = bf16[32,8192]{1,0:T(8,128)(2,1)} collective-permute-done((bf16[32,8192]{1,0:T(8,128)(2,1)S(1)}, bf16[32,8192]{1,0:T(8,128)(2,1)}, u32[]{:S(2)}, u32[]{:S(2)}) %collective-permute-start.6) | collective-permute-done | bytes 524320 | tf_op jit(solution)/shard_map/ppermute | solution.py:28
  51.0 4.2 %all-to-all-start = ((bf16[8,4,64,256]{3,2,1,0:T(8,128)(2,1)}), bf16[8,4,64,256]{3,2,1,0:T(8,128)(2,1)}, u32[]{:S(2)}, u32[]{:S(2)}) async-start(bf16[8,4,64,256]{3,2,1,0:T(8,128)(2,1)} %copy-done.3), calls=%async_computation | async-start | bytes 2097152 | tf_op jit(solution)/shard_map/all_to_all | solution.py:419
  55.5 1.7 collective-permute-start.8
  57.2 1.5 collective-permute-start.9
  58.7 3.2 %collective-permute-start.11 = (bf16[32,8192]{1,0:T(8,128)(2,1)}, bf16[32,8192]{1,0:T(8,128)(2,1)}, u32[]{:S(2)}, u32[]{:S(2)}) collective-permute-start(bf16[32,8192]{1,0:T(8,128)(2,1)} %collective-permute-done.7.refs_5_), channel_id=1, source_target_pairs={{0,8},{8,0},{1,9},{9,1},{2,10},{10,2},{3,11},{11,3},{4,12},{12,4},... | collective-permute-start | bytes 1572872 | tf_op jit(solution)/shard_map/ppermute | solution.py:28
  62.2 9.7 %all-to-all-done.own_ref = bf16[8,4,64,256]{3,2,1,0:T(8,128)(2,1)} async-done(((bf16[8,4,64,256]{3,2,1,0:T(8,128)(2,1)}), bf16[8,4,64,256]{3,2,1,0:T(8,128)(2,1)}, u32[]{:S(2)}, u32[]{:S(2)}) %all-to-all-start) | async-done | bytes 1048608 | tf_op jit(solution)/shard_map/all_to_all | solution.py:419
  71.9 3.9 %pairs.2 = bf16[5,64,128]{2,1,0:T(8,128)(2,1)S(1)} custom-call(bf16[64,8192]{1,0:T(8,128)(2,1)S(1)} %norm.1.refs_0_, bf16[64,8192]{1,0:T(8,128)(2,1)} %collective-permute-done.refs_1_, bf16[64,8192]{1,0:T(8,128)(2,1)S(1)} %collective-permute-done.1.refs_2_, bf16[64,8192]{1,0:T(8,128)(2,1)S(1)} %collective-permute-done.5.refs_3_, ...), custom_call_target="tpu_custom_call" | custom-call | flops 671088640 | bytes 7340032 | tf_op jit(solution)/shard_map/pairs/pallas_call | solution.py:136
  75.9 6.4 %queries.2.q_ref = bf16[5,256,128]{2,1,0:T(8,128)(2,1)S(1)} custom-call(bf16[64,8192]{1,0:T(8,128)(2,1)S(1)} %norm.1.refs_0_, bf16[64,8192]{1,0:T(8,128)(2,1)} %collective-permute-done.refs_1_, bf16[64,8192]{1,0:T(8,128)(2,1)S(1)} %collective-permute-done.1.refs_2_, bf16[64,8192]{1,0:T(8,128)(2,1)S(1)} %collective-permute-done.5.refs_3_, ...), custom_call_target="tpu_custom_call" | custom-call | flops 2684354560 | bytes 13631488 | tf_op jit(solution)/shard_map/queries/pallas_call | solution.py:88
  82.3 8.3 %collective-permute-done.8.refs_0_ = bf16[64,8192]{1,0:T(8,128)(2,1)} collective-permute-done((bf16[64,8192]{1,0:T(8,128)(2,1)}, bf16[64,8192]{1,0:T(8,128)(2,1)}, u32[]{:S(2)}, u32[]{:S(2)}) %collective-permute-start.8) | collective-permute-done | bytes 1048608 | tf_op jit(solution)/shard_map/ppermute | solution.py:28
  91.4 3.2 %pairs.3 = bf16[3,64,128]{2,1,0:T(8,128)(2,1)S(1)} custom-call(bf16[64,8192]{1,0:T(8,128)(2,1)} %collective-permute-done.8.refs_0_, bf16[64,8192]{1,0:T(8,128)(2,1)} %collective-permute-done.9.refs_1_, bf16[32,8192]{1,0:T(8,128)(2,1)} %collective-permute-done.10.refs_2_, bf16[32,8192]{1,0:T(8,128)(2,1)} %collective-permute-done.11.refs_3_, ...), custom_call_target="tpu_custom_call" | custom-call | flops 402653184 | bytes 5242880 | tf_op jit(solution)/shard_map/pairs/pallas_call | solution.py:136
  95.3 4.3 %collective-permute-start.14 = (bf16[8,64,128]{2,1,0:T(8,128)(2,1)S(1)}, bf16[8,64,128]{2,1,0:T(8,128)(2,1)S(1)}, u32[]{:S(2)}, u32[]{:S(2)}) collective-permute-start(bf16[8,64,128]{2,1,0:T(8,128)(2,1)S(1)} %pad_maximum_fusion.2), channel_id=1, source_target_pairs={{0,2},{2,6},{4,10},{6,14},{8,0},{10,4},{12,8},{14,12},{1,3},{3,7},... | collective-permute-start | bytes 393224 | tf_op jit(solution)/shard_map/ppermute | solution.py:432
  99.6 5.3 %collective-permute-done.14 = bf16[8,64,128]{2,1,0:T(8,128)(2,1)S(1)} collective-permute-done((bf16[8,64,128]{2,1,0:T(8,128)(2,1)S(1)}, bf16[8,64,128]{2,1,0:T(8,128)(2,1)S(1)}, u32[]{:S(2)}, u32[]{:S(2)}) %collective-permute-start.14) | collective-permute-done | bytes 131104 | tf_op jit(solution)/shard_map/ppermute | solution.py:432
  105.2 5.7 %queries.3.q_ref = bf16[3,256,128]{2,1,0:T(8,128)(2,1)S(1)} custom-call(bf16[64,8192]{1,0:T(8,128)(2,1)} %collective-permute-done.8.refs_0_, bf16[64,8192]{1,0:T(8,128)(2,1)} %collective-permute-done.9.refs_1_, bf16[32,8192]{1,0:T(8,128)(2,1)} %collective-permute-done.10.refs_2_, bf16[32,8192]{1,0:T(8,128)(2,1)} %collective-permute-done.11.refs_3_, ...), custom_call_target="tpu_custom_call" | custom-call | flops 1610612736 | bytes 11534336 | tf_op jit(solution)/shard_map/queries/pallas_call | solution.py:88
  110.9 4.2 %attend_prompt.2 = (f32[3,256,128]{2,1,0:T(8,128)S(1)}, f32[3,256,128]{2,1,0:T(8,128)S(1)}) custom-call(s32[3]{0:T(128)S(1)} %slice.29.prompt_ref, bf16[3,256,128]{2,1,0:T(8,128)(2,1)S(1)} %queries.3.q_ref, bf16[8,4,64,256]{3,2,1,0:T(8,128)(2,1)} %all-to-all-done.own_ref, bf16[8,4,64,256]{3,2,1,0:T(8,128)(2,1)S(1)} %collective-permute-done.12.other_ref), custom_call_target="tpu_custom_call" | custom-call | flops 402653184 | bytes 2359296 | tf_op jit(solution)/shard_map/attend_prompt/pallas_call | solution.py:199
  115.1 5.3 %attend_prompt.3 = (f32[5,256,128]{2,1,0:T(8,128)S(1)}, f32[5,256,128]{2,1,0:T(8,128)S(1)}) custom-call(s32[5]{0:T(128)S(1)} %bitcast.33, bf16[5,256,128]{2,1,0:T(8,128)(2,1)S(1)} %queries.2.q_ref, bf16[8,4,64,256]{3,2,1,0:T(8,128)(2,1)} %all-to-all-done.own_ref, bf16[8,4,64,256]{3,2,1,0:T(8,128)(2,1)S(1)} %collective-permute-done.12.other_ref), custom_call_target="tpu_custom_call" | custom-call | flops 671088640 | bytes 3932160 | tf_op jit(solution)/shard_map/attend_prompt/pallas_call | solution.py:199
  120.5 2.4 %attend_own.2.x_ref = bf16[192,512]{1,0:T(8,128)(2,1)S(1)} custom-call(s32[5,3]{1,0:T(8,128)S(1)} %slice.30.info_ref, bf16[3,256,128]{2,1,0:T(8,128)(2,1)S(1)} %queries.3.q_ref, f32[3,256,128]{2,1,0:T(8,128)S(1)} %get-tuple-element.46.acc_ref, f32[3,256,128]{2,1,0:T(8,128)S(1)} %get-tuple-element.51.state_ref, ...), custom_call_target="tpu_custom_call" | custom-call | flops 50331648 | bytes 1179648 | tf_op jit(solution)/shard_map/attend_own/pallas_call | solution.py:252
  122.9 3.5 %project_out.4 = (bf16[64,4096]{1,0:T(8,128)(2,1)S(1)}, bf16[64,4096]{1,0:T(8,128)(2,1)S(1)}, bf16[64,4096]{1,0:T(8,128)(2,1)S(1)}) custom-call(bf16[192,512]{1,0:T(8,128)(2,1)S(1)} %attend_own.2.x_ref, bf16[256,8192]{1,0:T(8,128)(2,1)S(1)} %bitcast.25, bf16[256,8192]{1,0:T(8,128)(2,1)} %collective-permute-done.4.wb_ref), custom_call_target="tpu_custom_call" | custom-call | flops 805306368 | bytes 5767168 | tf_op jit(solution)/shard_map/project_out/pallas_call | solution.py:284
  126.4 1.1 collective-permute-start.21
  127.5 2.6 %collective-permute-start.22 = (bf16[64,4096]{1,0:T(8,128)(2,1)S(1)}, bf16[64,4096]{1,0:T(8,128)(2,1)S(1)}, u32[]{:S(2)}, u32[]{:S(2)}) collective-permute-start(bf16[64,4096]{1,0:T(8,128)(2,1)S(1)} %get-tuple-element.66), channel_id=1, source_target_pairs={{0,6},{2,0},{4,2},{6,4},{1,7},{3,1},{5,3},{7,5},{8,14},{10,8},{12,... | collective-permute-start | bytes 1572872 | tf_op jit(solution)/shard_map/ppermute | solution.py:28
  130.2 3.7 %collective-permute-start.16 = (bf16[64,4096]{1,0:T(8,128)(2,1)S(1)}, bf16[64,4096]{1,0:T(8,128)(2,1)S(1)}, u32[]{:S(2)}, u32[]{:S(2)}) collective-permute-start(bf16[64,4096]{1,0:T(8,128)(2,1)S(1)} %get-tuple-element.59), channel_id=1, source_target_pairs={{0,8},{8,0},{1,9},{9,1},{2,10},{10,2},{3,11},{11,3},{4,12},{12,4},... | collective-permute-start | bytes 1572872 | tf_op jit(solution)/shard_map/ppermute | solution.py:28
  133.9 3.5 %project_out.5 = (bf16[64,4096]{1,0:T(8,128)(2,1)S(1)}, bf16[64,4096]{1,0:T(8,128)(2,1)S(1)}, bf16[64,4096]{1,0:T(8,128)(2,1)S(1)}) custom-call(bf16[192,512]{1,0:T(8,128)(2,1)S(1)} %attend_own.2.x_ref, bf16[256,8192]{1,0:T(8,128)(2,1)S(1)} %bitcast.26, bf16[256,8192]{1,0:T(8,128)(2,1)} %collective-permute-done.4.wb_ref), custom_call_target="tpu_custom_call" | custom-call | flops 805306368 | bytes 5767168 | tf_op jit(solution)/shard_map/project_out/pallas_call | solution.py:284
  138.5 4.4 %collective-permute-done.21.refs_1_ = bf16[64,4096]{1,0:T(8,128)(2,1)S(1)} collective-permute-done((bf16[64,4096]{1,0:T(8,128)(2,1)S(1)}, bf16[64,4096]{1,0:T(8,128)(2,1)S(1)}, u32[]{:S(2)}, u32[]{:S(2)}) %collective-permute-start.21) | collective-permute-done | bytes 524320 | tf_op jit(solution)/shard_map/ppermute | solution.py:28
  142.9 2.0 collective-permute-start.31
  144.9 3.6 %attend_own.3.x_ref = bf16[320,512]{1,0:T(8,128)(2,1)S(1)} custom-call(s32[5,5]{1,0:T(8,128)S(1)} %bitcast.32, bf16[5,256,128]{2,1,0:T(8,128)(2,1)S(1)} %queries.2.q_ref, f32[5,256,128]{2,1,0:T(8,128)S(1)} %get-tuple-element.48.acc_ref, f32[5,256,128]{2,1,0:T(8,128)S(1)} %get-tuple-element.49.state_ref, ...), custom_call_target="tpu_custom_call" | custom-call | flops 83886080 | bytes 1966080 | tf_op jit(solution)/shard_map/attend_own/pallas_call | solution.py:252
  148.5 4.2 %project_out.6 = (bf16[64,4096]{1,0:T(8,128)(2,1)S(1)}, bf16[64,4096]{1,0:T(8,128)(2,1)S(1)}, bf16[64,4096]{1,0:T(8,128)(2,1)S(1)}, bf16[64,4096]{1,0:T(8,128)(2,1)S(1)}, bf16[64,4096]{1,0:T(8,128)(2,1)S(1)}) custom-call(bf16[320,512]{1,0:T(8,128)(2,1)S(1)} %attend_own.3.x_ref, bf16[256,8192]{1,0:T(8,128)(2,1)} %bitcast.23, ...), custom_call_target="tpu_custom_call" | custom-call | flops 1342177280 | bytes 6815744 | tf_op jit(solution)/shard_map/project_out/pallas_call | solution.py:284
  152.9 1.8 collective-permute-start.23
  154.9 2.1 collective-permute-start.17
  157.9 1.8 collective-permute-start.18
  159.6 4.2 %project_out.7 = (bf16[64,4096]{1,0:T(8,128)(2,1)S(1)}, bf16[64,4096]{1,0:T(8,128)(2,1)S(1)}, bf16[64,4096]{1,0:T(8,128)(2,1)S(1)}, bf16[64,4096]{1,0:T(8,128)(2,1)S(1)}, bf16[64,4096]{1,0:T(8,128)(2,1)S(1)}) custom-call(bf16[320,512]{1,0:T(8,128)(2,1)S(1)} %attend_own.3.x_ref, bf16[256,8192]{1,0:T(8,128)(2,1)} %bitcast.24, ...), custom_call_target="tpu_custom_call" | custom-call | flops 1342177280 | bytes 6815744 | tf_op jit(solution)/shard_map/project_out/pallas_call | solution.py:284
  164.3 3.0 %collective-permute-start.27 = (bf16[64,2048]{1,0:T(8,128)(2,1)S(1)}, bf16[64,2048]{1,0:T(8,128)(2,1)S(1)}, u32[]{:S(2)}, u32[]{:S(2)}) collective-permute-start(bf16[64,2048]{1,0:T(8,128)(2,1)S(1)} %get-tuple-element.74), channel_id=1, source_target_pairs={{0,6},{2,0},{4,2},{6,4},{1,7},{3,1},{5,3},{7,5},{8,14},{10,8},{12,... | collective-permute-start | bytes 786440 | tf_op jit(solution)/shard_map/ppermute | solution.py:28
  167.5 1.9 collective-permute-start.32
  170.5 2.1 collective-permute-done.26.up_ref
  172.5 2.2 %collective-permute-start.20 = (bf16[64,4096]{1,0:T(8,128)(2,1)S(1)}, bf16[64,4096]{1,0:T(8,128)(2,1)S(1)}, u32[]{:S(2)}, u32[]{:S(2)}) collective-permute-start(bf16[64,4096]{1,0:T(8,128)(2,1)S(1)} %get-tuple-element.64), channel_id=1, source_target_pairs={{0,6},{2,0},{4,2},{6,4},{1,7},{3,1},{5,3},{7,5},{8,14},{10,8},{12,... | collective-permute-start | bytes 1572872 | tf_op jit(solution)/shard_map/ppermute | solution.py:28
  175.0 3.2 %collective-permute-start.29 = (bf16[64,4096]{1,0:T(8,128)(2,1)S(1)}, bf16[64,4096]{1,0:T(8,128)(2,1)S(1)}, u32[]{:S(2)}, u32[]{:S(2)}) collective-permute-start(bf16[64,4096]{1,0:T(8,128)(2,1)S(1)} %get-tuple-element.76), channel_id=1, source_target_pairs={{0,6},{2,0},{4,2},{6,4},{1,7},{3,1},{5,3},{7,5},{8,14},{10,8},{12,... | collective-permute-start | bytes 1572872 | tf_op jit(solution)/shard_map/ppermute | solution.py:28
  178.3 7.4 %collective-permute-done.19.refs_2_ = bf16[64,4096]{1,0:T(8,128)(2,1)S(1)} collective-permute-done((bf16[64,4096]{1,0:T(8,128)(2,1)S(1)}, bf16[64,4096]{1,0:T(8,128)(2,1)S(1)}, u32[]{:S(2)}, u32[]{:S(2)}) %collective-permute-start.19) | collective-permute-done | bytes 524320 | tf_op jit(solution)/shard_map/ppermute | solution.py:28
  185.7 1.7 collective-permute-done.20.refs_3_
  187.7 1.9 collective-permute-start.24
  189.7 4.6 %collective-permute-done.28.refs_2_ = bf16[64,4096]{1,0:T(8,128)(2,1)S(1)} collective-permute-done((bf16[64,4096]{1,0:T(8,128)(2,1)S(1)}, bf16[64,4096]{1,0:T(8,128)(2,1)S(1)}, u32[]{:S(2)}, u32[]{:S(2)}) %collective-permute-start.28) | collective-permute-done | bytes 524320 | tf_op jit(solution)/shard_map/ppermute | solution.py:28
  194.6 2.0 collective-permute-start.33
  196.6 6.8 %collective-permute-done.24 = bf16[64,4096]{1,0:T(8,128)(2,1)S(1)} collective-permute-done((bf16[64,4096]{1,0:T(8,128)(2,1)S(1)}, bf16[64,4096]{1,0:T(8,128)(2,1)S(1)}, u32[]{:S(2)}, u32[]{:S(2)}) %collective-permute-start.24) | collective-permute-done | bytes 524320 | tf_op jit(solution)/shard_map/ppermute | solution.py:472
  203.3 9.3 %collective-permute-done.33 = bf16[64,4096]{1,0:T(8,128)(2,1)S(1)} collective-permute-done((bf16[64,4096]{1,0:T(8,128)(2,1)S(1)}, bf16[64,4096]{1,0:T(8,128)(2,1)S(1)}, u32[]{:S(2)}, u32[]{:S(2)}) %collective-permute-start.33) | collective-permute-done | bytes 524320 | tf_op jit(solution)/shard_map/ppermute | solution.py:472
  (78 shorter events, 15.5 us)
Async XLA Ops:
  0.0 35.3 %collective-permute-start.4 = (bf16[256,8192]{1,0:T(8,128)(2,1)}, bf16[256,8192]{1,0:T(8,128)(2,1)}, u32[]{:S(2)}, u32[]{:S(2)}) collective-permute-start(bf16[256,8192]{1,0:T(8,128)(2,1)} %bitcast.22), channel_id=1, source_target_pairs={{0,1},{1,0},{2,3},{3,2},{4,5},{5,4},{6,7},{7,6},{8,9},{9,8},{10,11... | collective-permute-start | bytes 12582920 | tf_op jit(solution)/shard_map/ppermute | solution.py:28
  0.0 35.4 %collective-permute-start.3 = (bf16[8192,256]{1,0:T(8,128)(2,1)}, bf16[8192,256]{1,0:T(8,128)(2,1)}, u32[]{:S(2)}, u32[]{:S(2)}) collective-permute-start(bf16[8192,256]{1,0:T(8,128)(2,1)} %bitcast.34), channel_id=1, source_target_pairs={{0,1},{1,0},{2,3},{3,2},{4,5},{5,4},{6,7},{7,6},{8,9},{9,8},{10,11... | collective-permute-start | bytes 12582920 | tf_op jit(solution)/shard_map/ppermute | solution.py:28
  0.5 1.2 copy-start.1
  1.7 0.8 copy-start.6
  3.2 26.4 %collective-permute-start.1 = (bf16[64,8192]{1,0:T(8,128)(2,1)S(1)}, bf16[64,8192]{1,0:T(8,128)(2,1)S(1)}, u32[]{:S(2)}, u32[]{:S(2)}) collective-permute-start(bf16[64,8192]{1,0:T(8,128)(2,1)S(1)} %norm.1.refs_0_), channel_id=1, source_target_pairs={{0,2},{2,4},{4,6},{6,0},{1,3},{3,5},{5,7},{7,1},{8,10},{10,12},{12... | collective-permute-start | bytes 3145736 | tf_op jit(solution)/shard_map/ppermute | solution.py:28
  4.8 30.6 %collective-permute-start.5 = (bf16[64,8192]{1,0:T(8,128)(2,1)S(1)}, bf16[64,8192]{1,0:T(8,128)(2,1)S(1)}, u32[]{:S(2)}, u32[]{:S(2)}) collective-permute-start(bf16[64,8192]{1,0:T(8,128)(2,1)S(1)} %norm.1.refs_0_), channel_id=1, source_target_pairs={{0,6},{2,0},{4,2},{6,4},{1,7},{3,1},{5,3},{7,5},{8,14},{10,8},{12,... | collective-permute-start | bytes 3145736 | tf_op jit(solution)/shard_map/ppermute | solution.py:28
  6.5 28.9 %collective-permute-start.2 = (bf16[64,8192]{1,0:T(8,128)(2,1)}, bf16[64,8192]{1,0:T(8,128)(2,1)}, u32[]{:S(2)}, u32[]{:S(2)}) collective-permute-start(bf16[64,8192]{1,0:T(8,128)(2,1)} %bitcast.27), channel_id=1, source_target_pairs={{0,1},{1,0},{2,3},{3,2},{4,5},{5,4},{6,7},{7,6},{8,9},{9,8},{10,11... | collective-permute-start | bytes 3145736 | tf_op jit(solution)/shard_map/ppermute | solution.py:28
  29.6 25.9 %collective-permute-start = (bf16[64,8192]{1,0:T(8,128)(2,1)S(1)}, bf16[64,8192]{1,0:T(8,128)(2,1)}, u32[]{:S(2)}, u32[]{:S(2)}) collective-permute-start(bf16[64,8192]{1,0:T(8,128)(2,1)S(1)} %norm.1.refs_0_), channel_id=1, source_target_pairs={{0,8},{8,0},{1,9},{9,1},{2,10},{10,2},{3,11},{11,3},{4,12},{12,4},... | collective-permute-start | bytes 3145736 | tf_op jit(solution)/shard_map/ppermute | solution.py:28
  32.6 1.0 copy-start.5
  34.2 1.0 copy-start.3
  35.5 13.0 %collective-permute-start.7 = (bf16[32,8192]{1,0:T(8,128)(2,1)S(1)}, bf16[32,8192]{1,0:T(8,128)(2,1)}, u32[]{:S(2)}, u32[]{:S(2)}) collective-permute-start(bf16[32,8192]{1,0:T(8,128)(2,1)S(1)} %slice.27), channel_id=1, source_target_pairs={{0,6},{2,0},{4,2},{6,4},{1,7},{3,1},{5,3},{7,5},{8,14},{10,8},{12,... | collective-permute-start | bytes 1572872 | tf_op jit(solution)/shard_map/ppermute | solution.py:28
  37.3 13.7 %collective-permute-start.6 = (bf16[32,8192]{1,0:T(8,128)(2,1)S(1)}, bf16[32,8192]{1,0:T(8,128)(2,1)}, u32[]{:S(2)}, u32[]{:S(2)}) collective-permute-start(bf16[32,8192]{1,0:T(8,128)(2,1)S(1)} %slice.26), channel_id=1, source_target_pairs={{0,2},{2,4},{4,6},{6,0},{1,3},{3,5},{5,7},{7,1},{8,10},{10,12},{12... | collective-permute-start | bytes 1572872 | tf_op jit(solution)/shard_map/ppermute | solution.py:28
  51.0 20.9 %all-to-all-start = ((bf16[8,4,64,256]{3,2,1,0:T(8,128)(2,1)}), bf16[8,4,64,256]{3,2,1,0:T(8,128)(2,1)}, u32[]{:S(2)}, u32[]{:S(2)}) async-start(bf16[8,4,64,256]{3,2,1,0:T(8,128)(2,1)} %copy-done.3), calls=%async_computation | async-start | bytes 2097152 | tf_op jit(solution)/shard_map/all_to_all | solution.py:419
  55.5 35.2 %collective-permute-start.8 = (bf16[64,8192]{1,0:T(8,128)(2,1)}, bf16[64,8192]{1,0:T(8,128)(2,1)}, u32[]{:S(2)}, u32[]{:S(2)}) collective-permute-start(bf16[64,8192]{1,0:T(8,128)(2,1)} %collective-permute-done.refs_1_), channel_id=1, source_target_pairs={{0,2},{2,4},{4,6},{6,0},{1,3},{3,5},{5,7},{7,1},{8,10},{10,12},{12... | collective-permute-start | bytes 3145736 | tf_op jit(solution)/shard_map/ppermute | solution.py:28
  57.2 33.5 %collective-permute-start.9 = (bf16[64,8192]{1,0:T(8,128)(2,1)}, bf16[64,8192]{1,0:T(8,128)(2,1)}, u32[]{:S(2)}, u32[]{:S(2)}) collective-permute-start(bf16[64,8192]{1,0:T(8,128)(2,1)} %collective-permute-done.refs_1_), channel_id=1, source_target_pairs={{0,6},{2,0},{4,2},{6,4},{1,7},{3,1},{5,3},{7,5},{8,14},{10,8},{12,... | collective-permute-start | bytes 3145736 | tf_op jit(solution)/shard_map/ppermute | solution.py:28
  58.7 31.9 %collective-permute-start.11 = (bf16[32,8192]{1,0:T(8,128)(2,1)}, bf16[32,8192]{1,0:T(8,128)(2,1)}, u32[]{:S(2)}, u32[]{:S(2)}) collective-permute-start(bf16[32,8192]{1,0:T(8,128)(2,1)} %collective-permute-done.7.refs_5_), channel_id=1, source_target_pairs={{0,8},{8,0},{1,9},{9,1},{2,10},{10,2},{3,11},{11,3},{4,12},{12,4},... | collective-permute-start | bytes 1572872 | tf_op jit(solution)/shard_map/ppermute | solution.py:28
  61.9 29.5 %collective-permute-start.10 = (bf16[32,8192]{1,0:T(8,128)(2,1)}, bf16[32,8192]{1,0:T(8,128)(2,1)}, u32[]{:S(2)}, u32[]{:S(2)}) collective-permute-start(bf16[32,8192]{1,0:T(8,128)(2,1)} %collective-permute-done.6.refs_4_), channel_id=1, source_target_pairs={{0,8},{8,0},{1,9},{9,1},{2,10},{10,2},{3,11},{11,3},{4,12},{12,4},... | collective-permute-start | bytes 1572872 | tf_op jit(solution)/shard_map/ppermute | solution.py:28
  71.9 39.0 %collective-permute-start.12 = (bf16[8,4,64,256]{3,2,1,0:T(8,128)(2,1)}, bf16[8,4,64,256]{3,2,1,0:T(8,128)(2,1)S(1)}, u32[]{:S(2)}, u32[]{:S(2)}) collective-permute-start(bf16[8,4,64,256]{3,2,1,0:T(8,128)(2,1)} %all-to-all-done.own_ref), channel_id=1, source_target_pairs={{0,1},{1,0},{2,3},{3,2},{4,5},{5,4},{6,7},{7,6},{8,9},{9,8},{10,11... | collective-permute-start | bytes 3145736 | tf_op jit(solution)/shard_map/ppermute | solution.py:28
  75.9 15.5 %copy-start.4 = (bf16[1,8192,64]{1,2,0:T(8,128)(2,1)S(1)}, bf16[1,8192,64]{1,2,0:T(8,128)(2,1)}, u32[]{:S(2)}) copy-start(bf16[1,8192,64]{1,2,0:T(8,128)(2,1)} %param.12) | copy-start | bytes 3145732
  94.7 5.0 %collective-permute-start.13 = (bf16[8,64,128]{2,1,0:T(8,128)(2,1)S(1)}, bf16[8,64,128]{2,1,0:T(8,128)(2,1)S(1)}, u32[]{:S(2)}, u32[]{:S(2)}) collective-permute-start(bf16[8,64,128]{2,1,0:T(8,128)(2,1)S(1)} %pad_maximum_fusion.2), channel_id=1, source_target_pairs={{0,0},{2,4},{4,8},{6,12},{8,2},{10,6},{12,10},{14,14},{1,1},{3,5},... | collective-permute-start | bytes 393224 | tf_op jit(solution)/shard_map/ppermute | solution.py:432
  95.3 9.6 %collective-permute-start.14 = (bf16[8,64,128]{2,1,0:T(8,128)(2,1)S(1)}, bf16[8,64,128]{2,1,0:T(8,128)(2,1)S(1)}, u32[]{:S(2)}, u32[]{:S(2)}) collective-permute-start(bf16[8,64,128]{2,1,0:T(8,128)(2,1)S(1)} %pad_maximum_fusion.2), channel_id=1, source_target_pairs={{0,2},{2,6},{4,10},{6,14},{8,0},{10,4},{12,8},{14,12},{1,3},{3,7},... | collective-permute-start | bytes 393224 | tf_op jit(solution)/shard_map/ppermute | solution.py:432
  105.0 15.5 %collective-permute-start.15 = (bf16[2,8,64,128]{3,2,1,0:T(8,128)(2,1)S(1)}, bf16[2,8,64,128]{3,2,1,0:T(8,128)(2,1)S(1)}, u32[]{:S(2)}, u32[]{:S(2)}) collective-permute-start(bf16[2,8,64,128]{3,2,1,0:T(8,128)(2,1)S(1)} %pad_maximum_fusion.1.key_a.value_a), channel_id=1, source_target_pairs={{0,1},{1,0},{2,3},{3,2},{4,5},{5,4},{6,7},{7,6},{8,9},{9,8},{10,11... | collective-permute-start | bytes 786440 | tf_op jit(solution)/shard_map/ppermute | solution.py:28
  110.9 12.0 %copy-start = (bf16[1,256,8192]{2,1,0:T(8,128)(2,1)S(1)}, bf16[1,256,8192]{2,1,0:T(8,128)(2,1)}, u32[]{:S(2)}) copy-start(bf16[1,256,8192]{2,1,0:T(8,128)(2,1)} %param.13) | copy-start | bytes 12582916
  126.4 16.5 %collective-permute-start.21 = (bf16[64,4096]{1,0:T(8,128)(2,1)S(1)}, bf16[64,4096]{1,0:T(8,128)(2,1)S(1)}, u32[]{:S(2)}, u32[]{:S(2)}) collective-permute-start(bf16[64,4096]{1,0:T(8,128)(2,1)S(1)} %get-tuple-element.52), channel_id=1, source_target_pairs={{0,2},{2,4},{4,6},{6,0},{1,3},{3,5},{5,7},{7,1},{8,10},{10,12},{12... | collective-permute-start | bytes 1572872 | tf_op jit(solution)/shard_map/ppermute | solution.py:28
  127.5 25.2 %collective-permute-start.22 = (bf16[64,4096]{1,0:T(8,128)(2,1)S(1)}, bf16[64,4096]{1,0:T(8,128)(2,1)S(1)}, u32[]{:S(2)}, u32[]{:S(2)}) collective-permute-start(bf16[64,4096]{1,0:T(8,128)(2,1)S(1)} %get-tuple-element.66), channel_id=1, source_target_pairs={{0,6},{2,0},{4,2},{6,4},{1,7},{3,1},{5,3},{7,5},{8,14},{10,8},{12,... | collective-permute-start | bytes 1572872 | tf_op jit(solution)/shard_map/ppermute | solution.py:28
  130.2 24.6 %collective-permute-start.16 = (bf16[64,4096]{1,0:T(8,128)(2,1)S(1)}, bf16[64,4096]{1,0:T(8,128)(2,1)S(1)}, u32[]{:S(2)}, u32[]{:S(2)}) collective-permute-start(bf16[64,4096]{1,0:T(8,128)(2,1)S(1)} %get-tuple-element.59), channel_id=1, source_target_pairs={{0,8},{8,0},{1,9},{9,1},{2,10},{10,2},{3,11},{11,3},{4,12},{12,4},... | collective-permute-start | bytes 1572872 | tf_op jit(solution)/shard_map/ppermute | solution.py:28
  137.4 20.5 %collective-permute-start.25 = (bf16[64,4096]{1,0:T(8,128)(2,1)S(1)}, bf16[64,4096]{1,0:T(8,128)(2,1)S(1)}, u32[]{:S(2)}, u32[]{:S(2)}) collective-permute-start(bf16[64,4096]{1,0:T(8,128)(2,1)S(1)} %get-tuple-element.71), channel_id=1, source_target_pairs={{0,8},{8,0},{1,9},{9,1},{2,10},{10,2},{3,11},{11,3},{4,12},{12,4},... | collective-permute-start | bytes 1572872 | tf_op jit(solution)/shard_map/ppermute | solution.py:28
  137.5 26.5 %collective-permute-start.30 = (bf16[64,4096]{1,0:T(8,128)(2,1)S(1)}, bf16[64,4096]{1,0:T(8,128)(2,1)S(1)}, u32[]{:S(2)}, u32[]{:S(2)}) collective-permute-start(bf16[64,4096]{1,0:T(8,128)(2,1)S(1)} %get-tuple-element.54), channel_id=1, source_target_pairs={{0,2},{2,4},{4,6},{6,0},{1,3},{3,5},{5,7},{7,1},{8,10},{10,12},{12... | collective-permute-start | bytes 1572872 | tf_op jit(solution)/shard_map/ppermute | solution.py:28
  142.9 21.5 %collective-permute-start.31 = (bf16[64,4096]{1,0:T(8,128)(2,1)S(1)}, bf16[64,4096]{1,0:T(8,128)(2,1)S(1)}, u32[]{:S(2)}, u32[]{:S(2)}) collective-permute-start(bf16[64,4096]{1,0:T(8,128)(2,1)S(1)} %get-tuple-element.78), channel_id=1, source_target_pairs={{0,6},{2,0},{4,2},{6,4},{1,7},{3,1},{5,3},{7,5},{8,14},{10,8},{12,... | collective-permute-start | bytes 1572872 | tf_op jit(solution)/shard_map/ppermute | solution.py:28
  152.9 22.1 %collective-permute-start.23 = (bf16[64,4096]{1,0:T(8,128)(2,1)S(1)}, bf16[64,4096]{1,0:T(8,128)(2,1)S(1)}, u32[]{:S(2)}, u32[]{:S(2)}) collective-permute-start(bf16[64,4096]{1,0:T(8,128)(2,1)S(1)} %add.168), channel_id=1, source_target_pairs={{0,8},{8,0},{1,9},{9,1},{2,10},{10,2},{3,11},{11,3},{4,12},{12,4},... | collective-permute-start | bytes 1572872 | tf_op jit(solution)/shard_map/ppermute | solution.py:28
  154.9 12.6 %collective-permute-start.17 = (bf16[64,2048]{1,0:T(8,128)(2,1)S(1)}, bf16[64,2048]{1,0:T(8,128)(2,1)S(1)}, u32[]{:S(2)}, u32[]{:S(2)}) collective-permute-start(bf16[64,2048]{1,0:T(8,128)(2,1)S(1)} %get-tuple-element.60), channel_id=1, source_target_pairs={{0,2},{2,4},{4,6},{6,0},{1,3},{3,5},{5,7},{7,1},{8,10},{10,12},{12... | collective-permute-start | bytes 786440 | tf_op jit(solution)/shard_map/ppermute | solution.py:28
  157.9 11.6 %collective-permute-start.18 = (bf16[64,2048]{1,0:T(8,128)(2,1)S(1)}, bf16[64,2048]{1,0:T(8,128)(2,1)S(1)}, u32[]{:S(2)}, u32[]{:S(2)}) collective-permute-start(bf16[64,2048]{1,0:T(8,128)(2,1)S(1)} %get-tuple-element.62), channel_id=1, source_target_pairs={{0,6},{2,0},{4,2},{6,4},{1,7},{3,1},{5,3},{7,5},{8,14},{10,8},{12,... | collective-permute-start | bytes 786440 | tf_op jit(solution)/shard_map/ppermute | solution.py:28
  163.8 14.4 %copy-start.2 = (bf16[64,8192]{1,0:T(8,128)(2,1)S(1)}, bf16[64,8192]{1,0:T(8,128)(2,1)}, u32[]{:S(2)}) copy-start(bf16[64,8192]{1,0:T(8,128)(2,1)} %x_ref.1) | copy-start | bytes 3145732
  164.0 8.5 %collective-permute-start.26 = (bf16[64,2048]{1,0:T(8,128)(2,1)S(1)}, bf16[64,2048]{1,0:T(8,128)(2,1)S(1)}, u32[]{:S(2)}, u32[]{:S(2)}) collective-permute-start(bf16[64,2048]{1,0:T(8,128)(2,1)S(1)} %get-tuple-element.72), channel_id=1, source_target_pairs={{0,2},{2,4},{4,6},{6,0},{1,3},{3,5},{5,7},{7,1},{8,10},{10,12},{12... | collective-permute-start | bytes 786440 | tf_op jit(solution)/shard_map/ppermute | solution.py:28
  164.3 10.4 %collective-permute-start.27 = (bf16[64,2048]{1,0:T(8,128)(2,1)S(1)}, bf16[64,2048]{1,0:T(8,128)(2,1)S(1)}, u32[]{:S(2)}, u32[]{:S(2)}) collective-permute-start(bf16[64,2048]{1,0:T(8,128)(2,1)S(1)} %get-tuple-element.74), channel_id=1, source_target_pairs={{0,6},{2,0},{4,2},{6,4},{1,7},{3,1},{5,3},{7,5},{8,14},{10,8},{12,... | collective-permute-start | bytes 786440 | tf_op jit(solution)/shard_map/ppermute | solution.py:28
  167.5 22.1 %collective-permute-start.32 = (bf16[64,4096]{1,0:T(8,128)(2,1)S(1)}, bf16[64,4096]{1,0:T(8,128)(2,1)S(1)}, u32[]{:S(2)}, u32[]{:S(2)}) collective-permute-start(bf16[64,4096]{1,0:T(8,128)(2,1)S(1)} %add.170), channel_id=1, source_target_pairs={{0,8},{8,0},{1,9},{9,1},{2,10},{10,2},{3,11},{11,3},{4,12},{12,4},... | collective-permute-start | bytes 1572872 | tf_op jit(solution)/shard_map/ppermute | solution.py:28
  169.6 16.2 %collective-permute-start.19 = (bf16[64,4096]{1,0:T(8,128)(2,1)S(1)}, bf16[64,4096]{1,0:T(8,128)(2,1)S(1)}, u32[]{:S(2)}, u32[]{:S(2)}) collective-permute-start(bf16[64,4096]{1,0:T(8,128)(2,1)S(1)} %get-tuple-element.63), channel_id=1, source_target_pairs={{0,2},{2,4},{4,6},{6,0},{1,3},{3,5},{5,7},{7,1},{8,10},{10,12},{12... | collective-permute-start | bytes 1572872 | tf_op jit(solution)/shard_map/ppermute | solution.py:28
  172.5 14.9 %collective-permute-start.20 = (bf16[64,4096]{1,0:T(8,128)(2,1)S(1)}, bf16[64,4096]{1,0:T(8,128)(2,1)S(1)}, u32[]{:S(2)}, u32[]{:S(2)}) collective-permute-start(bf16[64,4096]{1,0:T(8,128)(2,1)S(1)} %get-tuple-element.64), channel_id=1, source_target_pairs={{0,6},{2,0},{4,2},{6,4},{1,7},{3,1},{5,3},{7,5},{8,14},{10,8},{12,... | collective-permute-start | bytes 1572872 | tf_op jit(solution)/shard_map/ppermute | solution.py:28
  174.9 19.3 %collective-permute-start.28 = (bf16[64,4096]{1,0:T(8,128)(2,1)S(1)}, bf16[64,4096]{1,0:T(8,128)(2,1)S(1)}, u32[]{:S(2)}, u32[]{:S(2)}) collective-permute-start(bf16[64,4096]{1,0:T(8,128)(2,1)S(1)} %get-tuple-element.75), channel_id=1, source_target_pairs={{0,2},{2,4},{4,6},{6,0},{1,3},{3,5},{5,7},{7,1},{8,10},{10,12},{12... | collective-permute-start | bytes 1572872 | tf_op jit(solution)/shard_map/ppermute | solution.py:28
  175.0 19.2 %collective-permute-start.29 = (bf16[64,4096]{1,0:T(8,128)(2,1)S(1)}, bf16[64,4096]{1,0:T(8,128)(2,1)S(1)}, u32[]{:S(2)}, u32[]{:S(2)}) collective-permute-start(bf16[64,4096]{1,0:T(8,128)(2,1)S(1)} %get-tuple-element.76), channel_id=1, source_target_pairs={{0,6},{2,0},{4,2},{6,4},{1,7},{3,1},{5,3},{7,5},{8,14},{10,8},{12,... | collective-permute-start | bytes 1572872 | tf_op jit(solution)/shard_map/ppermute | solution.py:28
  187.7 15.6 %collective-permute-start.24 = (bf16[64,4096]{1,0:T(8,128)(2,1)S(1)}, bf16[64,4096]{1,0:T(8,128)(2,1)S(1)}, u32[]{:S(2)}, u32[]{:S(2)}) collective-permute-start(bf16[64,4096]{1,0:T(8,128)(2,1)S(1)} %add.169), channel_id=1, source_target_pairs={{0,16},{16,32},{32,48},{48,64},{64,80},{80,96},{96,112},{112,128},... | collective-permute-start | bytes 1572872 | tf_op jit(solution)/shard_map/ppermute | solution.py:472
  194.6 18.0 %collective-permute-start.33 = (bf16[64,4096]{1,0:T(8,128)(2,1)S(1)}, bf16[64,4096]{1,0:T(8,128)(2,1)S(1)}, u32[]{:S(2)}, u32[]{:S(2)}) collective-permute-start(bf16[64,4096]{1,0:T(8,128)(2,1)S(1)} %add.171), channel_id=1, source_target_pairs={{0,16},{16,32},{32,48},{48,64},{64,80},{80,96},{96,112},{112,128},... | collective-permute-start | bytes 1572872 | tf_op jit(solution)/shard_map/ppermute | solution.py:472

commit v2 on v1

v2 whole, which is shorter than its diff:
```python
import functools

import jax
import jax.numpy as jnp
from jax import lax
from jax.experimental import pallas as pl
from jax.experimental.pallas import tpu as pltpu
from jax.sharding import Mesh, PartitionSpec as P

D = 8192
QH = 32
KVH = 4
HD = 128
PROMPT = 1024
NPROMPT = 4
RESP = 128
ROWS = 64
EPS = 1e-06
F32 = jnp.float32
BF16 = jnp.bfloat16
VMEM = 12 * 1024 * 1024
BRIEF = pl.CostEstimate(flops=1, bytes_accessed=1, transcendentals=0)

PLACES = ((0, 0), (1, 0), (0, 3), (0, 1), (0, 2), (1, 2), (1, 3), (1, 1))


def shift(value, axis, by):
    size = lax.axis_size(axis)
    return lax.ppermute(value, axis, [(i, (i + by) % size) for i in range(size)])


def params(**kw):
    return pltpu.CompilerParams(vmem_limit_bytes=VMEM, **kw)


def norm_kernel(x_ref, gain_ref, out_ref):
    wide = x_ref[...].astype(F32)
    mean = jnp.mean(wide * wide, axis=-1, keepdims=True)
    out_ref[...] = (wide * lax.rsqrt(mean + EPS) * gain_ref[...]).astype(BF16)


def norm(hidden, gain):
    return pl.pallas_call(
        norm_kernel,
        out_shape=jax.ShapeDtypeStruct((ROWS, D), BF16),
        grid=(2,),
        in_specs=[
            pl.BlockSpec((ROWS // 2, D), lambda i: (i, 0)),
            pl.BlockSpec((1, D), lambda i: (0, 0)),
        ],
        out_specs=pl.BlockSpec((ROWS // 2, D), lambda i: (i, 0)),
        compiler_params=params(),
        cost_estimate=BRIEF,
        name="norm",
    )(hidden, gain)


def turned(value, cosines, sines):
    return value * cosines + pltpu.roll(value, HD // 2, 1) * sines


def merge_kernel(places, *refs):
    out_ref, sems = refs[-2:]
    copies = [
        pltpu.make_async_copy(refs[source].at[there], out_ref.at[here], sems.at[i])
        for i, (source, there, here) in enumerate(places)
    ]
    for copy in copies:
        copy.start()
    for copy in copies:
        copy.wait()


def merge(own, other, shape, places):
    hbm = pl.BlockSpec(memory_space=pl.ANY)
    return pl.pallas_call(
        functools.partial(merge_kernel, places),
        out_shape=jax.ShapeDtypeStruct(shape, BF16),
        in_specs=[hbm, hbm],
        out_specs=pl.BlockSpec(memory_space=pltpu.VMEM),
        scratch_shapes=[pltpu.SemaphoreType.DMA((len(places),))],
        compiler_params=params(),
        cost_estimate=BRIEF,
        name="merge",
    )(own, other)


def merge_columns(own, other):
    rows, cols = own.shape
    every = slice(None)
    places = [
        (i, (every, every), (every, slice(i * cols, (i + 1) * cols))) for i in range(2)
    ]
    return merge(own, other, (rows, 2 * cols), places)


def merge_rows(own, other):
    rows, cols = own.shape
    every = slice(None)
    places = [
        (i, (every, every), (slice(i * rows, (i + 1) * rows), every)) for i in range(2)
    ]
    return merge(own, other, (2 * rows, cols), places)


def merge_cache(own, other):
    every = slice(None)
    places = [
        (i, (every, p), (p, slice(8 * i, 8 * (i + 1)))) for i in range(2) for p in range(NPROMPT)
    ]
    return merge(own, other, (NPROMPT, 16, ROWS, 2 * HD), places)


def query_kernel(count, *refs):
    pieces = refs[:count]
    w_ref, cos_ref, sin_ref, out_ref = refs[count:]
    depth = D // 2
    total = None
    for step in range(2):
        part = slice(step * depth, (step + 1) * depth)
        rows = jnp.concatenate([piece[:, part] for piece in pieces], axis=0)
        term = jnp.dot(rows, w_ref[part, :], preferred_element_type=F32)
        total = term if total is None else total + term
    for block in range(out_ref.shape[0]):
        for head in range(4):
            part = total[block * ROWS : (block + 1) * ROWS, head * HD : (head + 1) * HD]
            out_ref[block, head * ROWS : (head + 1) * ROWS, :] = turned(
                part, cos_ref[...], sin_ref[...]
            ).astype(BF16)


def project_queries(pieces, weight, cosines, sines):
    rows = sum(piece.shape[0] for piece in pieces)
    return pl.pallas_call(
        functools.partial(query_kernel, len(pieces)),
        out_shape=jax.ShapeDtypeStruct((rows // ROWS, 4 * ROWS, HD), BF16),
        compiler_params=params(),
        cost_estimate=BRIEF,
        name="queries",
    )(*pieces, weight, cosines, sines)


def dot_t(a, b):
    return lax.dot_general(a, b, (((1,), (1,)), ((), ())), preferred_element_type=F32)


def pair_kernel(count, *refs):
    pieces = refs[:count]
    core_ref, w_ref, cos_ref, sin_ref, out_ref = refs[count:]
    depth = D // 2
    total = None
    for step in range(2):
        part = slice(step * depth, (step + 1) * depth)
        rows = jnp.concatenate([piece[:, part] for piece in pieces], axis=0)
        term = dot_t(rows, w_ref[:, part])
        total = term if total is None else total + term
    pairs = total.astype(BF16).astype(F32)
    pairs = jnp.where(core_ref[0] == 0, pairs, pltpu.roll(pairs, HD // 2, 1))
    for block in range(out_ref.shape[0]):
        part = pairs[block * ROWS : (block + 1) * ROWS, :]
        out_ref[block] = turned(part, cos_ref[...], sin_ref[...]).astype(BF16)


def project_pairs(pieces, core, weight, cosines, sines):
    rows = sum(piece.shape[0] for piece in pieces)
    vmem = pl.BlockSpec(memory_space=pltpu.VMEM)
    return pl.pallas_call(
        functools.partial(pair_kernel, len(pieces)),
        out_shape=jax.ShapeDtypeStruct((rows // ROWS, ROWS, HD), BF16),
        in_specs=[vmem] * len(pieces) + [pl.BlockSpec(memory_space=pltpu.SMEM)] + [vmem] * 3,
        compiler_params=params(),
        cost_estimate=BRIEF,
        name="pairs",
    )(*pieces, core, weight, cosines, sines)


def sort_kernel(key_ref, value_ref, out_ref):
    out_ref[0, :, :, :HD] = key_ref[...]
    out_ref[0, :, :, HD:] = value_ref[...]


def sort_cache(cache):
    return pl.pallas_call(
        sort_kernel,
        out_shape=jax.ShapeDtypeStruct((2 * KVH, NPROMPT, ROWS, 2 * HD), BF16),
        grid=(2 * KVH,),
        in_specs=[
            pl.BlockSpec((NPROMPT, ROWS, HD), lambda i: (0, 0, i // 2)),
            pl.BlockSpec((NPROMPT, ROWS, HD), lambda i: (0, 0, KVH + i // 2)),
        ],
        out_specs=pl.BlockSpec((1, NPROMPT, ROWS, 2 * HD), lambda i: (i, 0, 0, 0)),
        compiler_params=params(),
        cost_estimate=BRIEF,
        name="sort_cache",
    )(cache, cache)


def prompt_kernel(prompt_ref, q_ref, cache_ref, acc_ref, state_ref):
    lane = lax.broadcasted_iota(jnp.int32, (4 * ROWS, HD), 1)

    @pl.loop(0, q_ref.shape[0])
    def _(i):
        cache = cache_ref[prompt_ref[i]].reshape(PROMPT, 2 * HD)
        scores = dot_t(q_ref[i], cache[:, :HD]) * HD ** (-0.5)
        top = jnp.max(scores, axis=-1, keepdims=True)
        probs = jnp.exp(scores - top)
        total = jnp.sum(probs, axis=-1, keepdims=True)
        acc_ref[i] = jnp.dot(probs.astype(BF16), cache[:, HD:], preferred_element_type=F32)
        state_ref[i] = jnp.where(lane < HD // 2, top, total)


def attend_prompt(queries, cache, prompts):
    shape = jax.ShapeDtypeStruct(queries.shape, F32)
    vmem = pl.BlockSpec(memory_space=pltpu.VMEM)
    return pl.pallas_call(
        prompt_kernel,
        out_shape=(shape, shape),
        in_specs=[pl.BlockSpec(memory_space=pltpu.SMEM), vmem, vmem],
        compiler_params=params(),
        cost_estimate=BRIEF,
        name="attend_prompt",
    )(prompts, queries, cache)


def own_kernel(info_ref, q_ref, acc_ref, state_ref, own_ref, other_ref, out_ref):
    lane = lax.broadcasted_iota(jnp.int32, (4 * ROWS, HD), 1)
    line = lax.broadcasted_iota(jnp.int32, (4 * ROWS, HD), 0) % ROWS

    @pl.loop(0, q_ref.shape[0])
    def _(i):
        length, core, kind = info_ref[0, i], info_ref[1, i], info_ref[2, i]
        key_at, value_at = info_ref[3, i], info_ref[4, i]
        keys = jnp.concatenate([own_ref[kind, key_at], other_ref[kind, key_at]], axis=0)
        values = jnp.concatenate(
            [own_ref[1 - kind, value_at], other_ref[1 - kind, value_at]], axis=0
        )
        scores = dot_t(q_ref[i], keys) * HD ** (-0.5)
        row = line + core * ROWS
        place = jnp.where(lane < ROWS, lane + core * ROWS, lane - core * ROWS)
        visible = (place <= row) & (place < length)
        scores = jnp.where(visible, scores, -jnp.inf)
        state = state_ref[i]
        top_a = state[:, :1]
        total_a = state[:, HD // 2 : HD // 2 + 1]
        top = jnp.maximum(top_a, jnp.max(scores, axis=-1, keepdims=True))
        scale = jnp.exp(top_a - top)
        probs = jnp.exp(scores - top)
        total = total_a * scale + jnp.sum(probs, axis=-1, keepdims=True)
        blended = acc_ref[i] * scale + jnp.dot(
            probs.astype(BF16), values, preferred_element_type=F32
        )
        blended = jnp.where(row < length, blended / total, 0.0).astype(BF16)
        for head in range(4):
            out_ref[i, :, head * HD : (head + 1) * HD] = blended[
                head * ROWS : (head + 1) * ROWS, :
            ]


def attend_own(queries, acc, state, pairs_own, pairs_other, info):
    count = queries.shape[0]
    vmem = pl.BlockSpec(memory_space=pltpu.VMEM)
    out = pl.pallas_call(
        own_kernel,
        out_shape=jax.ShapeDtypeStruct((count, ROWS, 4 * HD), BF16),
        in_specs=[pl.BlockSpec(memory_space=pltpu.SMEM)] + [vmem] * 5,
        compiler_params=params(),
        cost_estimate=BRIEF,
        name="attend_own",
    )(info, queries, acc, state, pairs_own, pairs_other)
    return out.reshape(count * ROWS, 4 * HD)


def output_kernel(counts, x_ref, w_ref, *out_refs):
    tile = 1024

    @pl.loop(0, D // 2 // tile)
    def _(step):
        inner = pl.ds(pl.multiple_of(step * tile, tile), tile)
        for side in range(2):
            part = pl.ds(pl.multiple_of(side * (D // 2) + step * tile, tile), tile)
            total = jnp.dot(x_ref[...], w_ref[:, part], preferred_element_type=F32)
            total = total.astype(BF16)
            at = 0
            for block, count in enumerate(counts):
                rows = total[block * ROWS : (block + 1) * ROWS, :]
                if count == 1:
                    out_refs[at][:, part] = rows
                else:
                    out_refs[at + side][:, inner] = rows
                at += count


def project_out(attended, weight, counts):
    return pl.pallas_call(
        functools.partial(output_kernel, counts),
        out_shape=[
            jax.ShapeDtypeStruct((ROWS, D // count), BF16) for count in counts for _ in range(count)
        ],
        compiler_params=params(),
        cost_estimate=BRIEF,
        name="project_out",
    )(attended, weight)


def sum_kernel(start, *refs):
    width = refs[-1].shape[1]
    total = 0.0
    for ref in refs[:-1]:
        low = start if ref.shape[1] > width else 0
        total += ref[:, low : low + width].astype(F32)
    refs[-1][...] = total.astype(BF16)


def split_kernel(a_ref, b_ref, low_ref, high_ref):
    total = (a_ref[...].astype(F32) + b_ref[...].astype(F32)).astype(BF16)
    half = low_ref.shape[1]
    low_ref[...] = total[:, :half]
    high_ref[...] = total[:, half:]


def split_sum(a, b):
    half = jax.ShapeDtypeStruct((a.shape[0], a.shape[1] // 2), BF16)
    return pl.pallas_call(
        split_kernel,
        out_shape=(half, half),
        compiler_params=params(),
        cost_estimate=BRIEF,
        name="split_sum",
    )(a, b)


def relay_kernel(a_ref, up_ref, b_ref, down_ref, a_out, b_out):
    half = up_ref.shape[1]
    a_out[:, :half] = (a_ref[:, :half].astype(F32) + up_ref[...].astype(F32)).astype(BF16)
    a_out[:, half:] = a_ref[:, half:]
    b_out[:, :half] = b_ref[:, :half]
    b_out[:, half:] = (b_ref[:, half:].astype(F32) + down_ref[...].astype(F32)).astype(BF16)


def relay_sum(a, up, b, down):
    whole = jax.ShapeDtypeStruct(a.shape, BF16)
    return pl.pallas_call(
        relay_kernel,
        out_shape=(whole, whole),
        compiler_params=params(),
        cost_estimate=BRIEF,
        name="relay_sum",
    )(a, up, b, down)


def add(*terms, start=0):
    width = min(term.shape[1] for term in terms)
    return pl.pallas_call(
        functools.partial(sum_kernel, start),
        out_shape=jax.ShapeDtypeStruct((terms[0].shape[0], width), BF16),
        compiler_params=params(),
        cost_estimate=BRIEF,
        name="add",
    )(*terms)


def after(value, *others):
    return lax.optimization_barrier((value, *others))[0]


def rope_tables():
    half = HD // 2
    position = (PROMPT + jnp.arange(RESP)).astype(F32)
    inverse = jnp.exp(-(2.0 * jnp.arange(half).astype(F32) / HD) * jnp.log(10000.0))
    angles = position[:, None] * inverse[None, :]
    cosines, sines = jnp.cos(angles), jnp.sin(angles)
    return (
        jnp.concatenate([cosines, cosines], axis=1),
        jnp.concatenate([-sines, sines], axis=1),
    )


def body(hidden, norm_gain, query_weight, kv_weight, out_weight, prompt_cache, resp_len, prompt_id):
    xh, y, core = lax.axis_index("xh"), lax.axis_index("y"), lax.axis_index("c")
    wq, wkv, wo = query_weight[0], kv_weight[0].T, out_weight[0]
    chips = ("xh", "y")

    normed = norm(hidden, norm_gain)
    b10 = shift(normed, "xh", 1)
    b03 = shift(normed, "y", 1)
    b01 = shift(normed, "y", -1)
    wq_other = shift(wq, "c", 1)
    wo_other = shift(wo, "c", 1)
    wkv_other = shift(after(wkv, wq_other), "c", 1)
    cache = sort_cache(after(prompt_cache[0], normed))
    cache = lax.all_to_all(cache, chips, 0, 0, tiled=True)

    cosines, sines = rope_tables()
    cosines = lax.dynamic_slice_in_dim(cosines, core * ROWS, ROWS, 0)
    sines = lax.dynamic_slice_in_dim(sines, core * ROWS, ROWS, 0)
    key_cosines = jnp.where(xh == 0, cosines, 1.0)
    key_sines = jnp.where(xh == 0, sines, 0.0)

    def pick(values, index):
        lanes = jnp.arange(8)
        return jnp.sum(jnp.where(index[:, None] == lanes[None, :], values[None, :], 0), axis=1)

    responses = jnp.stack([(xh ^ dx) * 4 + (y + dy) % 4 for dx, dy in PLACES])
    prompts = pick(prompt_id, responses).astype(jnp.int32)
    lengths = pick(resp_len, responses)
    maker_y = xh * 2 + y // 2
    table = [0] * 8
    for at, (dx, dy) in enumerate(PLACES):
        table[dx * 4 + dy] = at
    table = jnp.array(table, jnp.int32)
    away = (responses % 4 - maker_y) % 4
    key_at = pick(table, (responses // 4) * 4 + away)
    value_at = pick(table, (1 - responses // 4) * 4 + away)
    info = jnp.stack(
        [
            lengths,
            jnp.full((8,), core, jnp.int32),
            jnp.full((8,), y % 2, jnp.int32),
            key_at,
            value_at,
        ]
    ).astype(jnp.int32)
    core_word = jnp.full((1,), core, jnp.int32)

    b03 = after(b03, b10, wq_other, wo_other, info, prompts, key_cosines, key_sines, core_word)
    b01 = after(b01, b03, cache)
    upper, lower = b03[: ROWS // 2], b01[ROWS // 2 :]
    top02 = shift(upper, "y", 1)
    low02 = shift(lower, "y", -1)
    b02 = jnp.concatenate([top02, low02], axis=0)
    b12 = shift(b02, "xh", 1)
    b10 = after(b10, b02)
    b13 = shift(b10, "y", 1)
    b11 = shift(b10, "y", -1)
    cache = after(cache, b02)
    cache = merge_cache(cache, shift(cache, "c", 1))
    wkv = merge_rows(after(wkv, b02), wkv_other)
    wq = merge_columns(after(wq, b02), wq_other)

    near = [normed, b10, b03, b01, b02]
    far = [b12, b13, b11]
    pairs_near = project_pairs(near, core_word, wkv, key_cosines, key_sines)
    q_near = project_queries(near, wq, cosines, sines)
    acc_near, state_near = attend_prompt(q_near, cache, prompts[:5])
    wo = merge_rows(after(wo, acc_near), wo_other)
    far[0] = after(far[0], pairs_near, wo)
    pairs_far = project_pairs(far, core_word, wkv, key_cosines, key_sines)
    pairs = jnp.concatenate([pairs_near, pairs_far], axis=0)
    straight = [(g, 2 * g) for g in range(4)] + [(4 + g, 2 * g + 1) for g in range(4)]
    crossed = [(g, 2 * g + 1) for g in range(4)] + [(4 + g, 2 * g) for g in range(4)]
    first, second = lax.ppermute(pairs, chips, straight), lax.ppermute(pairs, chips, crossed)
    far[0] = after(far[0], pairs_far)
    q_far = project_queries(far, wq, cosines, sines)
    pairs = jnp.stack([after(first, q_far), second])
    pairs_other = shift(pairs, "c", 1)
    acc, state = attend_prompt(q_far, cache, prompts[5:])
    pairs_other = after(pairs_other, acc)
    att_far = attend_own(q_far, acc, state, pairs, pairs_other, info[:, 5:])

    p12b, p12a, p13, p11 = project_out(att_far, wo, (2, 1, 1))
    across_a = shift(p12a, "xh", 1)
    up = shift(p11, "y", 1)
    down = shift(p13, "y", -1)
    across_b = shift(p12b, "xh", 1)
    att_near = attend_own(
        q_near, acc_near, state_near, after(pairs, p11), pairs_other, info[:, :5]
    )
    p00, p10, p03b, p03a, p01b, p01a, p02b, p02a = project_out(att_near, wo, (1, 1, 2, 2, 2))
    up_a, down_a = split_sum(p02a, across_a)
    across = add(after(p10, up_a), up, down)
    up_b, down_b = split_sum(after(p02b, across), across_b)
    p01a = after(p01a, up_b)
    up_a, down_a = shift(up_a, "y", 1), shift(down_a, "y", -1)
    across = shift(across, "xh", 1)
    up_b, down_b = shift(up_b, "y", 1), shift(down_b, "y", -1)
    p01a, p03a = relay_sum(p01a, up_a, p03a, down_a)
    up_a, down_a = shift(p01a, "y", 1), shift(p03a, "y", -1)
    p01b, p03b = relay_sum(after(p01b, p01a), up_b, p03b, down_b)
    up_b, down_b = shift(p01b, "y", 1), shift(p03b, "y", -1)
    onward = [(i, (i + 1) % 16) for i in range(16)]
    total_a = add(hidden, p00, across, up_a, down_a, start=D // 2)
    total_b = add(after(hidden, total_a), p00, across, up_b, down_b)
    out_a = lax.ppermute(total_a, ("xl", "z"), onward)
    out_b = lax.ppermute(total_b, ("xl", "z"), onward)
    return jnp.concatenate([out_b, out_a], axis=1)


def solution(mesh):
    whole = Mesh(mesh.devices.reshape(2, 8, 2, 4, 2), ("xl", "z", "xh", "y", "c"))
    section, tp = ("xl", "z"), ("xh", "y", "c")
    in_specs = (
        P(section + tp, None),
        P(section, None),
        P(section, None, tp),
        P(section, None, tp),
        P(section, tp, None),
        P(section, None, tp, None),
        P(section),
        P(section),
    )
    out_specs = P(section + tp, None)
    return jax.shard_map(body, mesh=whole, in_specs=in_specs, out_specs=out_specs, check_vma=False)
```

time: 215 us -> 192 us (0.89)
  Pallas kernels: 52.9 us -> 38 us
  waiting for transfers between devices: 96.6 us -> 87.1 us
  local copies, waits for them, and re-layouts: 4.42 us -> 8.43 us
    all_to_all x1, waiting for transfers between devices: 9.69 us -> 3 us  [body(): cache = lax.all_to_all(cache, chips, 0, 0, tiled=True)]
    pallas_call x12 -> x13, Pallas kernels: 32 us -> 26.1 us  [the longest x4 6.61 us: merge(): pl.pallas_call(functools.partial(merge_kernel, places), out_shape=jax.Sha...]
    pallas_call x2, Pallas kernels: 12 us -> 6.16 us  [project_queries(): pl.pallas_call(functools.partial(query_kernel, len(pieces)), out_shape=ja...]
    unnamed x14 -> x23, local copies, waits for them, and re-layouts: 4 us -> 7.28 us
    pallas_call x2, Pallas kernels: 7.15 us -> 3.99 us  [project_pairs(): pl.pallas_call(functools.partial(pair_kernel, len(pieces)), out_shape=jax...]
    ppermute x30 -> x26, waiting for transfers between devices: 65.5 us -> 63.7 us  [shift(): lax.ppermute(value, axis, [(i, (i + by) % size) for i in range(size)])]
    ppermute x30 -> x26, starting transfers between devices: 42.8 us -> 42.9 us  [shift(): lax.ppermute(value, axis, [(i, (i + by) % size) for i in range(size)])]
  transfers between devices with their start and end apart: 35 -> 31, of which waited for: 16 -> 17; matrix products, arithmetic and copies ran while one was open for 1% -> 2% of each run, Pallas kernels for 22% -> 17%
where the time goes in v2:
time: 192 us
  waiting for transfers between devices  87.1 us (45%)
  starting transfers between devices  56 us (29%)
  Pallas kernels  38 us (20%)
  local copies, waits for them, and re-layouts  8.43 us (4%)
  other arithmetic  1.92 us (1%)
    ppermute x26, waiting for transfers between devices, shift(): lax.ppermute(value, axis, [(i, (i + by) % size) for i in range(size)])  63.7 us
    ppermute x26, starting transfers between devices, shift(): lax.ppermute(value, axis, [(i, (i + by) % size) for i in range(size)])  42.9 us
    ppermute x1, waiting for transfers between devices, body(): out_b = lax.ppermute(total_b, ('xl', 'z'), onward)  11.2 us
    unnamed x23, local copies, waits for them, and re-layouts  7.28 us
    pallas_call x4, Pallas kernels, merge(): pl.pallas_call(functools.partial(merge_kernel, places), out_shape=jax.Sha...  6.61 us
    pallas_call x2, Pallas kernels, attend_prompt(): pl.pallas_call(prompt_kernel, out_shape=(shape, shape), in_specs=[pl.Bloc...  6.59 us
    pallas_call x2, Pallas kernels, project_queries(): pl.pallas_call(functools.partial(query_kernel, len(pieces)), out_shape=ja...  6.16 us
    pallas_call x2, Pallas kernels, attend_own(): pl.pallas_call(own_kernel, out_shape=jax.ShapeDtypeStruct((count, ROWS, 4...  6.08 us
  transfers between devices with their start and end apart: 31, of which 17 were waited for; matrix products, arithmetic and copies ran while one was open for 2% of the time, Pallas kernels for 17%

profile of v2, /device:TPU:2, one launch (start us, length us, event | category | flops | bytes accessed | tf_op | source)
XLA Modules:
  0.0 191.8 jit_solution(12675851799157916160)
XLA Ops:
  0.6 1.2 copy-done
  3.3 2.2 %collective-permute-start = (bf16[64,8192]{1,0:T(8,128)(2,1)S(1)}, bf16[64,8192]{1,0:T(8,128)(2,1)}, u32[]{:S(2)}, u32[]{:S(2)}) collective-permute-start(bf16[64,8192]{1,0:T(8,128)(2,1)S(1)} %norm.1.refs_0_), channel_id=1, source_target_pairs={{0,8},{8,0},{1,9},{9,1},{2,10},{10,2},{3,11},{11,3},{4,12},{12,4},... | collective-permute-start | bytes 3145736 | tf_op jit(solution)/shard_map/ppermute | solution.py:29
  5.5 1.6 collective-permute-start.1
  7.0 1.7 collective-permute-start.5
  11.3 4.2 %all-to-all-start = ((bf16[8,4,64,256]{3,2,1,0:T(8,128)(2,1)}), bf16[8,4,64,256]{3,2,1,0:T(8,128)(2,1)}, u32[]{:S(2)}, u32[]{:S(2)}) async-start(bf16[8,4,64,256]{3,2,1,0:T(8,128)(2,1)} %copy-done.2), calls=%async_computation | async-start | bytes 2097152 | tf_op jit(solution)/shard_map/all_to_all | solution.py:391
  16.7 14.3 %collective-permute-done.refs_1_ = bf16[64,8192]{1,0:T(8,128)(2,1)} collective-permute-done((bf16[64,8192]{1,0:T(8,128)(2,1)S(1)}, bf16[64,8192]{1,0:T(8,128)(2,1)}, u32[]{:S(2)}, u32[]{:S(2)}) %collective-permute-start) | collective-permute-done | bytes 1048608 | tf_op jit(solution)/shard_map/ppermute | solution.py:29
  31.0 2.8 %collective-permute-done.1.refs_2_ = bf16[64,8192]{1,0:T(8,128)(2,1)S(1)} collective-permute-done((bf16[64,8192]{1,0:T(8,128)(2,1)S(1)}, bf16[64,8192]{1,0:T(8,128)(2,1)S(1)}, u32[]{:S(2)}, u32[]{:S(2)}) %collective-permute-start.1) | collective-permute-done | bytes 1048608 | tf_op jit(solution)/shard_map/ppermute | solution.py:29
  34.6 6.4 %collective-permute-start.4 = (bf16[32,8192]{1,0:T(8,128)(2,1)}, bf16[32,8192]{1,0:T(8,128)(2,1)}, u32[]{:S(2)}, u32[]{:S(2)}) collective-permute-start(bf16[32,8192]{1,0:T(8,128)(2,1)} %slice.19), channel_id=1, source_target_pairs={{0,2},{2,4},{4,6},{6,0},{1,3},{3,5},{5,7},{7,1},{8,10},{10,12},{12... | collective-permute-start | bytes 1572872 | tf_op jit(solution)/shard_map/ppermute | solution.py:29
  41.1 3.0 %all-to-all-done.refs_0_ = bf16[8,4,64,256]{3,2,1,0:T(8,128)(2,1)} async-done(((bf16[8,4,64,256]{3,2,1,0:T(8,128)(2,1)}), bf16[8,4,64,256]{3,2,1,0:T(8,128)(2,1)}, u32[]{:S(2)}, u32[]{:S(2)}) %all-to-all-start) | async-done | bytes 1048608 | tf_op jit(solution)/shard_map/all_to_all | solution.py:391
  44.1 1.9 %collective-permute-start.6 = (bf16[32,8192]{1,0:T(8,128)(2,1)S(1)}, bf16[32,8192]{1,0:T(8,128)(2,1)S(1)}, u32[]{:S(2)}, u32[]{:S(2)}) collective-permute-start(bf16[32,8192]{1,0:T(8,128)(2,1)S(1)} %slice.20), channel_id=1, source_target_pairs={{0,6},{2,0},{4,2},{6,4},{1,7},{3,1},{5,3},{7,5},{8,14},{10,8},{12,... | collective-permute-start | bytes 1572872 | tf_op jit(solution)/shard_map/ppermute | solution.py:29
  46.0 8.2 %collective-permute-done.4 = bf16[32,8192]{1,0:T(8,128)(2,1)} collective-permute-done((bf16[32,8192]{1,0:T(8,128)(2,1)}, bf16[32,8192]{1,0:T(8,128)(2,1)}, u32[]{:S(2)}, u32[]{:S(2)}) %collective-permute-start.4) | collective-permute-done | bytes 524320 | tf_op jit(solution)/shard_map/ppermute | solution.py:29
  56.0 1.6 collective-permute-start.9
  57.6 1.7 collective-permute-start.10
  59.3 1.8 collective-permute-start.11
  61.1 2.2 %copy-done.3 = bf16[1,8192,256]{2,1,0:T(8,128)(2,1)S(1)} copy-done((bf16[1,8192,256]{2,1,0:T(8,128)(2,1)S(1)}, bf16[1,8192,256]{2,1,0:T(8,128)(2,1)}, u32[]{:S(2)}) %copy-start.3) | copy-done | bytes 4194328
  63.3 2.5 %merge.4.refs_5_.refs_3_ = bf16[8192,512]{1,0:T(8,128)(2,1)S(1)} custom-call(bf16[8192,256]{1,0:T(8,128)(2,1)S(1)} %bitcast.25, bf16[8192,256]{1,0:T(8,128)(2,1)} %collective-permute-done.2.refs_1_), custom_call_target="tpu_custom_call" | custom-call | flops 1 | bytes 1 | tf_op jit(solution)/shard_map/merge/pallas_call | solution.py:76
  66.1 4.2 %queries.2.q_ref = bf16[5,256,128]{2,1,0:T(8,128)(2,1)S(1)} custom-call(bf16[64,8192]{1,0:T(8,128)(2,1)S(1)} %norm.1.refs_0_, bf16[64,8192]{1,0:T(8,128)(2,1)} %collective-permute-done.refs_1_, bf16[64,8192]{1,0:T(8,128)(2,1)S(1)} %collective-permute-done.1.refs_2_, bf16[64,8192]{1,0:T(8,128)(2,1)S(1)} %collective-permute-done.5.refs_3_, ...), custom_call_target="tpu_custom_call" | custom-call | flops 1 | bytes 1 | tf_op jit(solution)/shard_map/queries/pallas_call | solution.py:134
  70.3 2.9 %pairs.2 = bf16[5,64,128]{2,1,0:T(8,128)(2,1)S(1)} custom-call(bf16[64,8192]{1,0:T(8,128)(2,1)S(1)} %norm.1.refs_0_, bf16[64,8192]{1,0:T(8,128)(2,1)} %collective-permute-done.refs_1_, bf16[64,8192]{1,0:T(8,128)(2,1)S(1)} %collective-permute-done.1.refs_2_, bf16[64,8192]{1,0:T(8,128)(2,1)S(1)} %collective-permute-done.5.refs_3_, ...), custom_call_target="tpu_custom_call" | custom-call | flops 1 | bytes 1 | tf_op jit(solution)/shard_map/pairs/pallas_call | solution.py:167
  73.2 1.4 merge.5.cache_ref
  74.7 4.0 %attend_prompt.2 = (f32[5,256,128]{2,1,0:T(8,128)S(1)}, f32[5,256,128]{2,1,0:T(8,128)S(1)}) custom-call(s32[5]{0:T(128)S(1)} %bitcast.35, bf16[5,256,128]{2,1,0:T(8,128)(2,1)S(1)} %queries.2.q_ref, bf16[4,16,64,256]{3,2,1,0:T(8,128)(2,1)S(1)} %merge.5.cache_ref), custom_call_target="tpu_custom_call" | custom-call | flops 1 | bytes 1 | tf_op jit(solution)/shard_map/attend_prompt/pallas_call | solution.py:215
  78.7 2.5 %merge.7.w_ref = bf16[512,8192]{1,0:T(8,128)(2,1)S(1)} custom-call(bf16[256,8192]{1,0:T(8,128)(2,1)S(1)} %bitcast.27, bf16[256,8192]{1,0:T(8,128)(2,1)} %collective-permute-done.3.refs_1_), custom_call_target="tpu_custom_call" | custom-call | flops 1 | bytes 1 | tf_op jit(solution)/shard_map/merge/pallas_call | solution.py:76
  81.2 1.9 collective-permute-done.9.refs_0_
  83.1 1.8 collective-permute-done.10.refs_1_
  86.6 4.2 %collective-permute-start.13 = (bf16[8,64,128]{2,1,0:T(8,128)(2,1)S(1)}, bf16[8,64,128]{2,1,0:T(8,128)(2,1)S(1)}, u32[]{:S(2)}, u32[]{:S(2)}) collective-permute-start(bf16[8,64,128]{2,1,0:T(8,128)(2,1)S(1)} %pad_maximum_fusion.2), channel_id=1, source_target_pairs={{0,2},{2,6},{4,10},{6,14},{8,0},{10,4},{12,8},{14,12},{1,3},{3,7},... | collective-permute-start | bytes 393224 | tf_op jit(solution)/shard_map/ppermute | solution.py:451
  90.8 1.9 %queries.3.q_ref = bf16[3,256,128]{2,1,0:T(8,128)(2,1)S(1)} custom-call(bf16[64,8192]{1,0:T(8,128)(2,1)S(1)} %collective-permute-done.9.refs_0_, bf16[64,8192]{1,0:T(8,128)(2,1)S(1)} %collective-permute-done.10.refs_1_, bf16[64,8192]{1,0:T(8,128)(2,1)S(1)} %collective-permute-done.11.refs_2_, bf16[8192,512]{1,0:T(8,128)(2,1)S(1)} %merge.4.refs_5_.refs_3_, ...), custom_call_target="tpu_custom_call" | custom-call | flops 1 | bytes 1 | tf_op jit(solution)/shard_map/queries/pallas_call | solution.py:134
  92.8 4.8 %collective-permute-done.13 = bf16[8,64,128]{2,1,0:T(8,128)(2,1)S(1)} collective-permute-done((bf16[8,64,128]{2,1,0:T(8,128)(2,1)S(1)}, bf16[8,64,128]{2,1,0:T(8,128)(2,1)S(1)}, u32[]{:S(2)}, u32[]{:S(2)}) %collective-permute-start.13) | collective-permute-done | bytes 131104 | tf_op jit(solution)/shard_map/ppermute | solution.py:451
  97.8 2.6 %attend_prompt.3 = (f32[3,256,128]{2,1,0:T(8,128)S(1)}, f32[3,256,128]{2,1,0:T(8,128)S(1)}) custom-call(s32[3]{0:T(128)S(1)} %slice.23.prompt_ref, bf16[3,256,128]{2,1,0:T(8,128)(2,1)S(1)} %queries.3.q_ref, bf16[4,16,64,256]{3,2,1,0:T(8,128)(2,1)S(1)} %merge.5.cache_ref), custom_call_target="tpu_custom_call" | custom-call | flops 1 | bytes 1 | tf_op jit(solution)/shard_map/attend_prompt/pallas_call | solution.py:215
  100.5 2.4 %attend_own.2 = bf16[3,64,512]{2,1,0:T(8,128)(2,1)S(1)} custom-call(s32[5,3]{1,0:T(8,128)S(1)} %slice.22.info_ref, bf16[3,256,128]{2,1,0:T(8,128)(2,1)S(1)} %queries.3.q_ref, f32[3,256,128]{2,1,0:T(8,128)S(1)} %get-tuple-element.62.acc_ref, f32[3,256,128]{2,1,0:T(8,128)S(1)} %get-tuple-element.63.state_ref, ...), custom_call_target="tpu_custom_call" | custom-call | flops 1 | bytes 1 | tf_op jit(solution)/shard_map/attend_own/pallas_call | solution.py:262
  102.9 2.4 %project_out.2 = (bf16[64,4096]{1,0:T(8,128)(2,1)S(1)}, bf16[64,4096]{1,0:T(8,128)(2,1)S(1)}, bf16[64,8192]{1,0:T(8,128)(2,1)S(1)}, bf16[64,8192]{1,0:T(8,128)(2,1)S(1)}) custom-call(bf16[192,512]{1,0:T(8,128)(2,1)S(1)} %bitcast.33, bf16[512,8192]{1,0:T(8,128)(2,1)S(1)} %merge.7.w_ref), custom_call_target="tpu_custom_call" | custom-call | flops 1 | bytes 1 | tf_op jit(solution)/shard_map/project_out/pallas_call | solution.py:294
  105.8 3.2 %collective-permute-start.17 = (bf16[64,8192]{1,0:T(8,128)(2,1)S(1)}, bf16[64,8192]{1,0:T(8,128)(2,1)S(1)}, u32[]{:S(2)}, u32[]{:S(2)}) collective-permute-start(bf16[64,8192]{1,0:T(8,128)(2,1)S(1)} %get-tuple-element.73), channel_id=1, source_target_pairs={{0,6},{2,0},{4,2},{6,4},{1,7},{3,1},{5,3},{7,5},{8,14},{10,8},{12,... | collective-permute-start | bytes 3145736 | tf_op jit(solution)/shard_map/ppermute | solution.py:29
  109.0 2.9 %collective-permute-start.15 = (bf16[64,4096]{1,0:T(8,128)(2,1)S(1)}, bf16[64,4096]{1,0:T(8,128)(2,1)S(1)}, u32[]{:S(2)}, u32[]{:S(2)}) collective-permute-start(bf16[64,4096]{1,0:T(8,128)(2,1)S(1)} %get-tuple-element.70), channel_id=1, source_target_pairs={{0,8},{8,0},{1,9},{9,1},{2,10},{10,2},{3,11},{11,3},{4,12},{12,4},... | collective-permute-start | bytes 1572872 | tf_op jit(solution)/shard_map/ppermute | solution.py:29
  112.5 3.6 %attend_own.3 = bf16[5,64,512]{2,1,0:T(8,128)(2,1)S(1)} custom-call(s32[5,5]{1,0:T(8,128)S(1)} %bitcast.34, bf16[5,256,128]{2,1,0:T(8,128)(2,1)S(1)} %queries.2.q_ref, f32[5,256,128]{2,1,0:T(8,128)S(1)} %get-tuple-element.54.acc_ref, f32[5,256,128]{2,1,0:T(8,128)S(1)} %get-tuple-element.55.state_ref, bf16[2,8,64,128]{3,2,1,0:T(8,128)(2,1)S(1)} %pad_maximum_fusion.1.own_ref, ...), custom_call_target="tpu_custom_call" | custom-call | flops 1 | bytes 1 | tf_op jit(solution)/shard_map/attend_own/pallas_call | solution.py:262
  116.2 3.4 %project_out.3 = (bf16[64,8192]{1,0:T(8,128)(2,1)S(1)}, bf16[64,8192]{1,0:T(8,128)(2,1)S(1)}, bf16[64,4096]{1,0:T(8,128)(2,1)S(1)}, bf16[64,4096]{1,0:T(8,128)(2...) custom-call(bf16[320,512]{1,0:T(8,128)(2,1)S(1)} %bitcast.30, ...), custom_call_target="tpu_custom_call" | custom-call | flops 1 | bytes 1 | tf_op jit(solution)/shard_map/project_out/pallas_call | solution.py:294
  119.6 5.7 %collective-permute-done.15.b_ref = bf16[64,4096]{1,0:T(8,128)(2,1)S(1)} collective-permute-done((bf16[64,4096]{1,0:T(8,128)(2,1)S(1)}, bf16[64,4096]{1,0:T(8,128)(2,1)S(1)}, u32[]{:S(2)}, u32[]{:S(2)}) %collective-permute-start.15) | collective-permute-done | bytes 524320 | tf_op jit(solution)/shard_map/ppermute | solution.py:29
  125.4 7.3 %collective-permute-done.16.refs_1_ = bf16[64,8192]{1,0:T(8,128)(2,1)S(1)} collective-permute-done((bf16[64,8192]{1,0:T(8,128)(2,1)S(1)}, bf16[64,8192]{1,0:T(8,128)(2,1)S(1)}, u32[]{:S(2)}, u32[]{:S(2)}) %collective-permute-start.16) | collective-permute-done | bytes 1048608 | tf_op jit(solution)/shard_map/ppermute | solution.py:29
  133.4 2.5 %collective-permute-start.18 = (bf16[64,8192]{1,0:T(8,128)(2,1)S(1)}, bf16[64,8192]{1,0:T(8,128)(2,1)S(1)}, u32[]{:S(2)}, u32[]{:S(2)}) collective-permute-start(bf16[64,8192]{1,0:T(8,128)(2,1)S(1)} %add.167), channel_id=1, source_target_pairs={{0,8},{8,0},{1,9},{9,1},{2,10},{10,2},{3,11},{11,3},{4,12},{12,4},... | collective-permute-start | bytes 3145736 | tf_op jit(solution)/shard_map/ppermute | solution.py:29
  136.0 3.1 %collective-permute-start.21 = (bf16[64,2048]{1,0:T(8,128)(2,1)S(1)}, bf16[64,2048]{1,0:T(8,128)(2,1)S(1)}, u32[]{:S(2)}, u32[]{:S(2)}) collective-permute-start(bf16[64,2048]{1,0:T(8,128)(2,1)S(1)} %get-tuple-element.81), channel_id=1, source_target_pairs={{0,6},{2,0},{4,2},{6,4},{1,7},{3,1},{5,3},{7,5},{8,14},{10,8},{12,... | collective-permute-start | bytes 786440 | tf_op jit(solution)/shard_map/ppermute | solution.py:29
  139.3 3.2 %collective-permute-start.25 = (bf16[64,2048]{1,0:T(8,128)(2,1)S(1)}, bf16[64,2048]{1,0:T(8,128)(2,1)S(1)}, u32[]{:S(2)}, u32[]{:S(2)}) collective-permute-start(bf16[64,2048]{1,0:T(8,128)(2,1)S(1)} %get-tuple-element.88), channel_id=1, source_target_pairs={{0,6},{2,0},{4,2},{6,4},{1,7},{3,1},{5,3},{7,5},{8,14},{10,8},{12,... | collective-permute-start | bytes 786440 | tf_op jit(solution)/shard_map/ppermute | solution.py:29
  142.6 3.8 %collective-permute-done.20.up_ref = bf16[64,2048]{1,0:T(8,128)(2,1)S(1)} collective-permute-done((bf16[64,2048]{1,0:T(8,128)(2,1)S(1)}, bf16[64,2048]{1,0:T(8,128)(2,1)S(1)}, u32[]{:S(2)}, u32[]{:S(2)}) %collective-permute-start.20) | collective-permute-done | bytes 262176 | tf_op jit(solution)/shard_map/ppermute | solution.py:29
  147.7 2.2 %collective-permute-start.23 = (bf16[64,4096]{1,0:T(8,128)(2,1)S(1)}, bf16[64,4096]{1,0:T(8,128)(2,1)S(1)}, u32[]{:S(2)}, u32[]{:S(2)}) collective-permute-start(bf16[64,4096]{1,0:T(8,128)(2,1)S(1)} %get-tuple-element.83), channel_id=1, source_target_pairs={{0,6},{2,0},{4,2},{6,4},{1,7},{3,1},{5,3},{7,5},{8,14},{10,8},{12,... | collective-permute-start | bytes 1572872 | tf_op jit(solution)/shard_map/ppermute | solution.py:29
  149.9 2.1 %collective-permute-done.24.up_ref = bf16[64,2048]{1,0:T(8,128)(2,1)S(1)} collective-permute-done((bf16[64,2048]{1,0:T(8,128)(2,1)S(1)}, bf16[64,2048]{1,0:T(8,128)(2,1)S(1)}, u32[]{:S(2)}, u32[]{:S(2)}) %collective-permute-start.24) | collective-permute-done | bytes 262176 | tf_op jit(solution)/shard_map/ppermute | solution.py:29
  153.3 2.2 %collective-permute-start.27 = (bf16[64,4096]{1,0:T(8,128)(2,1)S(1)}, bf16[64,4096]{1,0:T(8,128)(2,1)S(1)}, u32[]{:S(2)}, u32[]{:S(2)}) collective-permute-start(bf16[64,4096]{1,0:T(8,128)(2,1)S(1)} %get-tuple-element.90), channel_id=1, source_target_pairs={{0,6},{2,0},{4,2},{6,4},{1,7},{3,1},{5,3},{7,5},{8,14},{10,8},{12,... | collective-permute-start | bytes 1572872 | tf_op jit(solution)/shard_map/ppermute | solution.py:29
  155.5 7.7 %collective-permute-done.22.refs_3_ = bf16[64,4096]{1,0:T(8,128)(2,1)S(1)} collective-permute-done((bf16[64,4096]{1,0:T(8,128)(2,1)S(1)}, bf16[64,4096]{1,0:T(8,128)(2,1)S(1)}, u32[]{:S(2)}, u32[]{:S(2)}) %collective-permute-start.22) | collective-permute-done | bytes 524320 | tf_op jit(solution)/shard_map/ppermute | solution.py:29
  163.5 2.0 %collective-permute-start.29 = (bf16[64,4096]{1,0:T(8,128)(2,1)S(1)}, bf16[64,4096]{1,0:T(8,128)(2,1)S(1)}, u32[]{:S(2)}, u32[]{:S(2)}) collective-permute-start(bf16[64,4096]{1,0:T(8,128)(2,1)S(1)} %add.168), channel_id=1, source_target_pairs={{0,16},{16,32},{32,48},{48,64},{64,80},{80,96},{96,112},{112,128},... | collective-permute-start | bytes 1572872 | tf_op jit(solution)/shard_map/ppermute | solution.py:483
  165.5 7.3 %collective-permute-done.26.refs_3_ = bf16[64,4096]{1,0:T(8,128)(2,1)S(1)} collective-permute-done((bf16[64,4096]{1,0:T(8,128)(2,1)S(1)}, bf16[64,4096]{1,0:T(8,128)(2,1)S(1)}, u32[]{:S(2)}, u32[]{:S(2)}) %collective-permute-start.26) | collective-permute-done | bytes 524320 | tf_op jit(solution)/shard_map/ppermute | solution.py:29
  173.2 2.0 %collective-permute-start.28 = (bf16[64,4096]{1,0:T(8,128)(2,1)S(1)}, bf16[64,4096]{1,0:T(8,128)(2,1)S(1)}, u32[]{:S(2)}, u32[]{:S(2)}) collective-permute-start(bf16[64,4096]{1,0:T(8,128)(2,1)S(1)} %add.169), channel_id=1, source_target_pairs={{0,16},{16,32},{32,48},{48,64},{64,80},{80,96},{96,112},{112,128},... | collective-permute-start | bytes 1572872 | tf_op jit(solution)/shard_map/ppermute | solution.py:484
  175.2 4.4 %collective-permute-done.29 = bf16[64,4096]{1,0:T(8,128)(2,1)S(1)} collective-permute-done((bf16[64,4096]{1,0:T(8,128)(2,1)S(1)}, bf16[64,4096]{1,0:T(8,128)(2,1)S(1)}, u32[]{:S(2)}, u32[]{:S(2)}) %collective-permute-start.29) | collective-permute-done | bytes 524320 | tf_op jit(solution)/shard_map/ppermute | solution.py:483
  179.6 11.2 %collective-permute-done.28 = bf16[64,4096]{1,0:T(8,128)(2,1)S(1)} collective-permute-done((bf16[64,4096]{1,0:T(8,128)(2,1)S(1)}, bf16[64,4096]{1,0:T(8,128)(2,1)S(1)}, u32[]{:S(2)}, u32[]{:S(2)}) %collective-permute-start.28) | collective-permute-done | bytes 524320 | tf_op jit(solution)/shard_map/ppermute | solution.py:484
  (80 shorter events, 17.1 us)
Async XLA Ops:
  0.0 15.9 %copy-start.10 = (s32[8]{0:T(128)S(1)}, s32[8]{0:T(128)}, u32[]{:S(2)}) copy-start(s32[8]{0:T(128)} %constant.114.clone) | copy-start | bytes 100
  0.0 15.7 %copy-start.8 = (s32[8]{0:T(128)S(1)}, s32[8]{0:T(128)}, u32[]{:S(2)}) copy-start(s32[8]{0:T(128)} %param.16) | copy-start | bytes 100
  0.0 15.7 %copy-start.9 = (s32[8]{0:T(128)S(1)}, s32[8]{0:T(128)}, u32[]{:S(2)}) copy-start(s32[8]{0:T(128)} %param.15) | copy-start | bytes 100
  0.0 33.8 %collective-permute-start.2 = (bf16[8192,256]{1,0:T(8,128)(2,1)}, bf16[8192,256]{1,0:T(8,128)(2,1)}, u32[]{:S(2)}, u32[]{:S(2)}) collective-permute-start(bf16[8192,256]{1,0:T(8,128)(2,1)} %bitcast.24), channel_id=1, source_target_pairs={{0,1},{1,0},{2,3},{3,2},{4,5},{5,4},{6,7},{7,6},{8,9},{9,8},{10,11... | collective-permute-start | bytes 12582920 | tf_op jit(solution)/shard_map/ppermute | solution.py:29
  0.1 33.7 %collective-permute-start.3 = (bf16[256,8192]{1,0:T(8,128)(2,1)}, bf16[256,8192]{1,0:T(8,128)(2,1)}, u32[]{:S(2)}, u32[]{:S(2)}) collective-permute-start(bf16[256,8192]{1,0:T(8,128)(2,1)} %bitcast.26), channel_id=1, source_target_pairs={{0,1},{1,0},{2,3},{3,2},{4,5},{5,4},{6,7},{7,6},{8,9},{9,8},{10,11... | collective-permute-start | bytes 12582920 | tf_op jit(solution)/shard_map/ppermute | solution.py:29
  0.6 1.2 copy-start
  1.8 0.8 copy-start.7
  3.3 27.7 %collective-permute-start = (bf16[64,8192]{1,0:T(8,128)(2,1)S(1)}, bf16[64,8192]{1,0:T(8,128)(2,1)}, u32[]{:S(2)}, u32[]{:S(2)}) collective-permute-start(bf16[64,8192]{1,0:T(8,128)(2,1)S(1)} %norm.1.refs_0_), channel_id=1, source_target_pairs={{0,8},{8,0},{1,9},{9,1},{2,10},{10,2},{3,11},{11,3},{4,12},{12,4},... | collective-permute-start | bytes 3145736 | tf_op jit(solution)/shard_map/ppermute | solution.py:29
  5.5 28.3 %collective-permute-start.1 = (bf16[64,8192]{1,0:T(8,128)(2,1)S(1)}, bf16[64,8192]{1,0:T(8,128)(2,1)S(1)}, u32[]{:S(2)}, u32[]{:S(2)}) collective-permute-start(bf16[64,8192]{1,0:T(8,128)(2,1)S(1)} %norm.1.refs_0_), channel_id=1, source_target_pairs={{0,2},{2,4},{4,6},{6,0},{1,3},{3,5},{5,7},{7,1},{8,10},{10,12},{12... | collective-permute-start | bytes 3145736 | tf_op jit(solution)/shard_map/ppermute | solution.py:29
  7.0 37.0 %collective-permute-start.5 = (bf16[64,8192]{1,0:T(8,128)(2,1)S(1)}, bf16[64,8192]{1,0:T(8,128)(2,1)S(1)}, u32[]{:S(2)}, u32[]{:S(2)}) collective-permute-start(bf16[64,8192]{1,0:T(8,128)(2,1)S(1)} %norm.1.refs_0_), channel_id=1, source_target_pairs={{0,6},{2,0},{4,2},{6,4},{1,7},{3,1},{5,3},{7,5},{8,14},{10,8},{12,... | collective-permute-start | bytes 3145736 | tf_op jit(solution)/shard_map/ppermute | solution.py:29
  8.7 1.0 copy-start.5
  10.3 1.0 copy-start.2
  11.3 32.8 %all-to-all-start = ((bf16[8,4,64,256]{3,2,1,0:T(8,128)(2,1)}), bf16[8,4,64,256]{3,2,1,0:T(8,128)(2,1)}, u32[]{:S(2)}, u32[]{:S(2)}) async-start(bf16[8,4,64,256]{3,2,1,0:T(8,128)(2,1)} %copy-done.2), calls=%async_computation | async-start | bytes 2097152 | tf_op jit(solution)/shard_map/all_to_all | solution.py:391
  34.6 19.6 %collective-permute-start.4 = (bf16[32,8192]{1,0:T(8,128)(2,1)}, bf16[32,8192]{1,0:T(8,128)(2,1)}, u32[]{:S(2)}, u32[]{:S(2)}) collective-permute-start(bf16[32,8192]{1,0:T(8,128)(2,1)} %slice.19), channel_id=1, source_target_pairs={{0,2},{2,4},{4,6},{6,0},{1,3},{3,5},{5,7},{7,1},{8,10},{10,12},{12... | collective-permute-start | bytes 1572872 | tf_op jit(solution)/shard_map/ppermute | solution.py:29
  44.1 11.7 %collective-permute-start.6 = (bf16[32,8192]{1,0:T(8,128)(2,1)S(1)}, bf16[32,8192]{1,0:T(8,128)(2,1)S(1)}, u32[]{:S(2)}, u32[]{:S(2)}) collective-permute-start(bf16[32,8192]{1,0:T(8,128)(2,1)S(1)} %slice.20), channel_id=1, source_target_pairs={{0,6},{2,0},{4,2},{6,4},{1,7},{3,1},{5,3},{7,5},{8,14},{10,8},{12,... | collective-permute-start | bytes 1572872 | tf_op jit(solution)/shard_map/ppermute | solution.py:29
  46.0 19.8 %collective-permute-start.8 = (bf16[64,8192]{1,0:T(8,128)(2,1)}, bf16[64,8192]{1,0:T(8,128)(2,1)S(1)}, u32[]{:S(2)}, u32[]{:S(2)}) collective-permute-start(bf16[64,8192]{1,0:T(8,128)(2,1)} %bitcast.31), channel_id=1, source_target_pairs={{0,1},{1,0},{2,3},{3,2},{4,5},{5,4},{6,7},{7,6},{8,9},{9,8},{10,11... | collective-permute-start | bytes 3145736 | tf_op jit(solution)/shard_map/ppermute | solution.py:29
  55.8 10.1 %copy-start.6 = (bf16[1,8192,64]{1,2,0:T(8,128)(2,1)S(1)}, bf16[1,8192,64]{1,2,0:T(8,128)(2,1)}, u32[]{:S(2)}) copy-start(bf16[1,8192,64]{1,2,0:T(8,128)(2,1)} %param.12) | copy-start | bytes 3145732
  55.9 17.4 %collective-permute-start.7 = (bf16[8,4,64,256]{3,2,1,0:T(8,128)(2,1)}, bf16[8,4,64,256]{3,2,1,0:T(8,128)(2,1)S(1)}, u32[]{:S(2)}, u32[]{:S(2)}) collective-permute-start(bf16[8,4,64,256]{3,2,1,0:T(8,128)(2,1)} %all-to-all-done.refs_0_), channel_id=1, source_target_pairs={{0,1},{1,0},{2,3},{3,2},{4,5},{5,4},{6,7},{7,6},{8,9},{9,8},{10,11... | collective-permute-start | bytes 3145736 | tf_op jit(solution)/shard_map/ppermute | solution.py:29
  56.0 27.1 %collective-permute-start.9 = (bf16[64,8192]{1,0:T(8,128)(2,1)S(1)}, bf16[64,8192]{1,0:T(8,128)(2,1)S(1)}, u32[]{:S(2)}, u32[]{:S(2)}) collective-permute-start(bf16[64,8192]{1,0:T(8,128)(2,1)S(1)} %constant_dynamic-update-slice_fusion.refs_4_), channel_id=1, source_target_pairs={{0,8},{8,0},{1,9},{9,1},{2,10},{10,2},{3,11},{11,3},{4,12},{12,4},... | collective-permute-start | bytes 3145736 | tf_op jit(solution)/shard_map/ppermute | solution.py:29
  57.6 27.2 %collective-permute-start.10 = (bf16[64,8192]{1,0:T(8,128)(2,1)}, bf16[64,8192]{1,0:T(8,128)(2,1)S(1)}, u32[]{:S(2)}, u32[]{:S(2)}) collective-permute-start(bf16[64,8192]{1,0:T(8,128)(2,1)} %collective-permute-done.refs_1_), channel_id=1, source_target_pairs={{0,2},{2,4},{4,6},{6,0},{1,3},{3,5},{5,7},{7,1},{8,10},{10,12},{12... | collective-permute-start | bytes 3145736 | tf_op jit(solution)/shard_map/ppermute | solution.py:29
  59.3 25.5 %collective-permute-start.11 = (bf16[64,8192]{1,0:T(8,128)(2,1)}, bf16[64,8192]{1,0:T(8,128)(2,1)S(1)}, u32[]{:S(2)}, u32[]{:S(2)}) collective-permute-start(bf16[64,8192]{1,0:T(8,128)(2,1)} %collective-permute-done.refs_1_), channel_id=1, source_target_pairs={{0,6},{2,0},{4,2},{6,4},{1,7},{3,1},{5,3},{7,5},{8,14},{10,8},{12,... | collective-permute-start | bytes 3145736 | tf_op jit(solution)/shard_map/ppermute | solution.py:29
  61.1 2.2 %copy-start.3 = (bf16[1,8192,256]{2,1,0:T(8,128)(2,1)S(1)}, bf16[1,8192,256]{2,1,0:T(8,128)(2,1)}, u32[]{:S(2)}) copy-start(bf16[1,8192,256]{2,1,0:T(8,128)(2,1)} %param.11) | copy-start | bytes 12582916
  73.2 5.4 %copy-start.4 = (bf16[1,256,8192]{2,1,0:T(8,128)(2,1)S(1)}, bf16[1,256,8192]{2,1,0:T(8,128)(2,1)}, u32[]{:S(2)}) copy-start(bf16[1,256,8192]{2,1,0:T(8,128)(2,1)} %param.13) | copy-start | bytes 12582916
  86.0 6.8 %collective-permute-start.12 = (bf16[8,64,128]{2,1,0:T(8,128)(2,1)S(1)}, bf16[8,64,128]{2,1,0:T(8,128)(2,1)S(1)}, u32[]{:S(2)}, u32[]{:S(2)}) collective-permute-start(bf16[8,64,128]{2,1,0:T(8,128)(2,1)S(1)} %pad_maximum_fusion.2), channel_id=1, source_target_pairs={{0,0},{2,4},{4,8},{6,12},{8,2},{10,6},{12,10},{14,14},{1,1},{3,5},... | collective-permute-start | bytes 393224 | tf_op jit(solution)/shard_map/ppermute | solution.py:451
  86.6 10.9 %collective-permute-start.13 = (bf16[8,64,128]{2,1,0:T(8,128)(2,1)S(1)}, bf16[8,64,128]{2,1,0:T(8,128)(2,1)S(1)}, u32[]{:S(2)}, u32[]{:S(2)}) collective-permute-start(bf16[8,64,128]{2,1,0:T(8,128)(2,1)S(1)} %pad_maximum_fusion.2), channel_id=1, source_target_pairs={{0,2},{2,6},{4,10},{6,14},{8,0},{10,4},{12,8},{14,12},{1,3},{3,7},... | collective-permute-start | bytes 393224 | tf_op jit(solution)/shard_map/ppermute | solution.py:451
  97.6 2.9 %collective-permute-start.14 = (bf16[2,8,64,128]{3,2,1,0:T(8,128)(2,1)S(1)}, bf16[2,8,64,128]{3,2,1,0:T(8,128)(2,1)S(1)}, u32[]{:S(2)}, u32[]{:S(2)}) collective-permute-start(bf16[2,8,64,128]{3,2,1,0:T(8,128)(2,1)S(1)} %pad_maximum_fusion.1.own_ref), channel_id=1, source_target_pairs={{0,1},{1,0},{2,3},{3,2},{4,5},{5,4},{6,7},{7,6},{8,9},{9,8},{10,11... | collective-permute-start | bytes 786440 | tf_op jit(solution)/shard_map/ppermute | solution.py:29
  105.3 27.4 %collective-permute-start.16 = (bf16[64,8192]{1,0:T(8,128)(2,1)S(1)}, bf16[64,8192]{1,0:T(8,128)(2,1)S(1)}, u32[]{:S(2)}, u32[]{:S(2)}) collective-permute-start(bf16[64,8192]{1,0:T(8,128)(2,1)S(1)} %get-tuple-element.65), channel_id=1, source_target_pairs={{0,2},{2,4},{4,6},{6,0},{1,3},{3,5},{5,7},{7,1},{8,10},{10,12},{12... | collective-permute-start | bytes 3145736 | tf_op jit(solution)/shard_map/ppermute | solution.py:29
  105.8 27.2 %collective-permute-start.17 = (bf16[64,8192]{1,0:T(8,128)(2,1)S(1)}, bf16[64,8192]{1,0:T(8,128)(2,1)S(1)}, u32[]{:S(2)}, u32[]{:S(2)}) collective-permute-start(bf16[64,8192]{1,0:T(8,128)(2,1)S(1)} %get-tuple-element.73), channel_id=1, source_target_pairs={{0,6},{2,0},{4,2},{6,4},{1,7},{3,1},{5,3},{7,5},{8,14},{10,8},{12,... | collective-permute-start | bytes 3145736 | tf_op jit(solution)/shard_map/ppermute | solution.py:29
  109.0 16.3 %collective-permute-start.15 = (bf16[64,4096]{1,0:T(8,128)(2,1)S(1)}, bf16[64,4096]{1,0:T(8,128)(2,1)S(1)}, u32[]{:S(2)}, u32[]{:S(2)}) collective-permute-start(bf16[64,4096]{1,0:T(8,128)(2,1)S(1)} %get-tuple-element.70), channel_id=1, source_target_pairs={{0,8},{8,0},{1,9},{9,1},{2,10},{10,2},{3,11},{11,3},{4,12},{12,4},... | collective-permute-start | bytes 1572872 | tf_op jit(solution)/shard_map/ppermute | solution.py:29
  111.9 27.2 %collective-permute-start.19 = (bf16[64,4096]{1,0:T(8,128)(2,1)S(1)}, bf16[64,4096]{1,0:T(8,128)(2,1)S(1)}, u32[]{:S(2)}, u32[]{:S(2)}) collective-permute-start(bf16[64,4096]{1,0:T(8,128)(2,1)S(1)} %get-tuple-element.77), channel_id=1, source_target_pairs={{0,8},{8,0},{1,9},{9,1},{2,10},{10,2},{3,11},{11,3},{4,12},{12,4},... | collective-permute-start | bytes 1572872 | tf_op jit(solution)/shard_map/ppermute | solution.py:29
  125.4 37.8 %copy-start.1 = (bf16[64,8192]{1,0:T(8,128)(2,1)S(1)}, bf16[64,8192]{1,0:T(8,128)(2,1)}, u32[]{:S(2)}) copy-start(bf16[64,8192]{1,0:T(8,128)(2,1)} %refs_0_.2) | copy-start | bytes 3145732
  133.4 29.8 %collective-permute-start.18 = (bf16[64,8192]{1,0:T(8,128)(2,1)S(1)}, bf16[64,8192]{1,0:T(8,128)(2,1)S(1)}, u32[]{:S(2)}, u32[]{:S(2)}) collective-permute-start(bf16[64,8192]{1,0:T(8,128)(2,1)S(1)} %add.167), channel_id=1, source_target_pairs={{0,8},{8,0},{1,9},{9,1},{2,10},{10,2},{3,11},{11,3},{4,12},{12,4},... | collective-permute-start | bytes 3145736 | tf_op jit(solution)/shard_map/ppermute | solution.py:29
  135.9 10.5 %collective-permute-start.20 = (bf16[64,2048]{1,0:T(8,128)(2,1)S(1)}, bf16[64,2048]{1,0:T(8,128)(2,1)S(1)}, u32[]{:S(2)}, u32[]{:S(2)}) collective-permute-start(bf16[64,2048]{1,0:T(8,128)(2,1)S(1)} %get-tuple-element.71), channel_id=1, source_target_pairs={{0,2},{2,4},{4,6},{6,0},{1,3},{3,5},{5,7},{7,1},{8,10},{10,12},{12... | collective-permute-start | bytes 786440 | tf_op jit(solution)/shard_map/ppermute | solution.py:29
  136.0 10.3 %collective-permute-start.21 = (bf16[64,2048]{1,0:T(8,128)(2,1)S(1)}, bf16[64,2048]{1,0:T(8,128)(2,1)S(1)}, u32[]{:S(2)}, u32[]{:S(2)}) collective-permute-start(bf16[64,2048]{1,0:T(8,128)(2,1)S(1)} %get-tuple-element.81), channel_id=1, source_target_pairs={{0,6},{2,0},{4,2},{6,4},{1,7},{3,1},{5,3},{7,5},{8,14},{10,8},{12,... | collective-permute-start | bytes 786440 | tf_op jit(solution)/shard_map/ppermute | solution.py:29
  139.3 12.7 %collective-permute-start.24 = (bf16[64,2048]{1,0:T(8,128)(2,1)S(1)}, bf16[64,2048]{1,0:T(8,128)(2,1)S(1)}, u32[]{:S(2)}, u32[]{:S(2)}) collective-permute-start(bf16[64,2048]{1,0:T(8,128)(2,1)S(1)} %get-tuple-element.78), channel_id=1, source_target_pairs={{0,2},{2,4},{4,6},{6,0},{1,3},{3,5},{5,7},{7,1},{8,10},{10,12},{12... | collective-permute-start | bytes 786440 | tf_op jit(solution)/shard_map/ppermute | solution.py:29
  139.3 12.6 %collective-permute-start.25 = (bf16[64,2048]{1,0:T(8,128)(2,1)S(1)}, bf16[64,2048]{1,0:T(8,128)(2,1)S(1)}, u32[]{:S(2)}, u32[]{:S(2)}) collective-permute-start(bf16[64,2048]{1,0:T(8,128)(2,1)S(1)} %get-tuple-element.88), channel_id=1, source_target_pairs={{0,6},{2,0},{4,2},{6,4},{1,7},{3,1},{5,3},{7,5},{8,14},{10,8},{12,... | collective-permute-start | bytes 786440 | tf_op jit(solution)/shard_map/ppermute | solution.py:29
  146.5 16.7 %collective-permute-start.22 = (bf16[64,4096]{1,0:T(8,128)(2,1)S(1)}, bf16[64,4096]{1,0:T(8,128)(2,1)S(1)}, u32[]{:S(2)}, u32[]{:S(2)}) collective-permute-start(bf16[64,4096]{1,0:T(8,128)(2,1)S(1)} %get-tuple-element.82), channel_id=1, source_target_pairs={{0,2},{2,4},{4,6},{6,0},{1,3},{3,5},{5,7},{7,1},{8,10},{10,12},{12... | collective-permute-start | bytes 1572872 | tf_op jit(solution)/shard_map/ppermute | solution.py:29
  147.7 15.5 %collective-permute-start.23 = (bf16[64,4096]{1,0:T(8,128)(2,1)S(1)}, bf16[64,4096]{1,0:T(8,128)(2,1)S(1)}, u32[]{:S(2)}, u32[]{:S(2)}) collective-permute-start(bf16[64,4096]{1,0:T(8,128)(2,1)S(1)} %get-tuple-element.83), channel_id=1, source_target_pairs={{0,6},{2,0},{4,2},{6,4},{1,7},{3,1},{5,3},{7,5},{8,14},{10,8},{12,... | collective-permute-start | bytes 1572872 | tf_op jit(solution)/shard_map/ppermute | solution.py:29
  152.1 20.7 %collective-permute-start.26 = (bf16[64,4096]{1,0:T(8,128)(2,1)S(1)}, bf16[64,4096]{1,0:T(8,128)(2,1)S(1)}, u32[]{:S(2)}, u32[]{:S(2)}) collective-permute-start(bf16[64,4096]{1,0:T(8,128)(2,1)S(1)} %get-tuple-element.89), channel_id=1, source_target_pairs={{0,2},{2,4},{4,6},{6,0},{1,3},{3,5},{5,7},{7,1},{8,10},{10,12},{12... | collective-permute-start | bytes 1572872 | tf_op jit(solution)/shard_map/ppermute | solution.py:29
  153.3 19.5 %collective-permute-start.27 = (bf16[64,4096]{1,0:T(8,128)(2,1)S(1)}, bf16[64,4096]{1,0:T(8,128)(2,1)S(1)}, u32[]{:S(2)}, u32[]{:S(2)}) collective-permute-start(bf16[64,4096]{1,0:T(8,128)(2,1)S(1)} %get-tuple-element.90), channel_id=1, source_target_pairs={{0,6},{2,0},{4,2},{6,4},{1,7},{3,1},{5,3},{7,5},{8,14},{10,8},{12,... | collective-permute-start | bytes 1572872 | tf_op jit(solution)/shard_map/ppermute | solution.py:29
  163.5 16.0 %collective-permute-start.29 = (bf16[64,4096]{1,0:T(8,128)(2,1)S(1)}, bf16[64,4096]{1,0:T(8,128)(2,1)S(1)}, u32[]{:S(2)}, u32[]{:S(2)}) collective-permute-start(bf16[64,4096]{1,0:T(8,128)(2,1)S(1)} %add.168), channel_id=1, source_target_pairs={{0,16},{16,32},{32,48},{48,64},{64,80},{80,96},{96,112},{112,128},... | collective-permute-start | bytes 1572872 | tf_op jit(solution)/shard_map/ppermute | solution.py:483
  173.2 17.6 %collective-permute-start.28 = (bf16[64,4096]{1,0:T(8,128)(2,1)S(1)}, bf16[64,4096]{1,0:T(8,128)(2,1)S(1)}, u32[]{:S(2)}, u32[]{:S(2)}) collective-permute-start(bf16[64,4096]{1,0:T(8,128)(2,1)S(1)} %add.169), channel_id=1, source_target_pairs={{0,16},{16,32},{32,48},{48,64},{64,80},{80,96},{96,112},{112,128},... | collective-permute-start | bytes 1572872 | tf_op jit(solution)/shard_map/ppermute | solution.py:484

commit v3 on v2

--- a/solution.py
+++ b/solution.py
@@ -21,7 +21,7 @@
 VMEM = 12 * 1024 * 1024
 BRIEF = pl.CostEstimate(flops=1, bytes_accessed=1, transcendentals=0)
 
-PLACES = ((0, 0), (1, 0), (0, 3), (0, 1), (0, 2), (1, 2), (1, 3), (1, 1))
+PLACES = ((0, 0), (1, 0), (0, 3), (0, 1), (0, 2), (1, 3), (1, 1), (1, 2))
 
 
 def shift(value, axis, by):
@@ -329,6 +329,30 @@
     )(a, b)
 
 
+def place_kernel(start, *refs):
+    value_ref, out_ref, sem = refs[-3:]
+    width = value_ref.shape[1]
+    copy = pltpu.make_async_copy(value_ref, out_ref.at[:, pl.ds(start, width)], sem)
+    copy.start()
+    copy.wait()
+
+
+def place(value, start, whole=None):
+    hbm = pl.BlockSpec(memory_space=pl.ANY)
+    given = () if whole is None else (whole,)
+    return pl.pallas_call(
+        functools.partial(place_kernel, start),
+        out_shape=jax.ShapeDtypeStruct((ROWS, D), BF16),
+        in_specs=[hbm] * (len(given) + 1),
+        out_specs=hbm,
+        scratch_shapes=[pltpu.SemaphoreType.DMA],
+        input_output_aliases={0: 0} if given else {},
+        compiler_params=params(),
+        cost_estimate=BRIEF,
+        name="place",
+    )(*given, value)
+
+
 def relay_kernel(a_ref, up_ref, b_ref, down_ref, a_out, b_out):
     half = up_ref.shape[1]
     a_out[:, :half] = (a_ref[:, :half].astype(F32) + up_ref[...].astype(F32)).astype(BF16)
@@ -384,9 +408,8 @@
     b10 = shift(normed, "xh", 1)
     b03 = shift(normed, "y", 1)
     b01 = shift(normed, "y", -1)
+    wkv_other = shift(wkv, "c", 1)
     wq_other = shift(wq, "c", 1)
-    wo_other = shift(wo, "c", 1)
-    wkv_other = shift(after(wkv, wq_other), "c", 1)
     cache = sort_cache(after(prompt_cache[0], normed))
     cache = lax.all_to_all(cache, chips, 0, 0, tiled=True)
 
@@ -422,28 +445,28 @@
     ).astype(jnp.int32)
     core_word = jnp.full((1,), core, jnp.int32)
 
-    b03 = after(b03, b10, wq_other, wo_other, info, prompts, key_cosines, key_sines, core_word)
+    b03 = after(b03, b10, wq_other, wkv_other, info, prompts, key_cosines, key_sines, core_word)
     b01 = after(b01, b03, cache)
     upper, lower = b03[: ROWS // 2], b01[ROWS // 2 :]
     top02 = shift(upper, "y", 1)
     low02 = shift(lower, "y", -1)
-    b02 = jnp.concatenate([top02, low02], axis=0)
+    wkv = merge_rows(after(wkv, lower), wkv_other)
+    wq = merge_columns(after(wq, lower), wq_other)
+    b02 = jnp.concatenate([after(top02, wkv, wq), low02], axis=0)
     b12 = shift(b02, "xh", 1)
-    b10 = after(b10, b02)
+    b10 = after(b10, lower)
     b13 = shift(b10, "y", 1)
     b11 = shift(b10, "y", -1)
-    cache = after(cache, b02)
+    cache = after(cache, lower)
     cache = merge_cache(cache, shift(cache, "c", 1))
-    wkv = merge_rows(after(wkv, b02), wkv_other)
-    wq = merge_columns(after(wq, b02), wq_other)
 
     near = [normed, b10, b03, b01, b02]
-    far = [b12, b13, b11]
+    far = [b13, b11, b12]
     pairs_near = project_pairs(near, core_word, wkv, key_cosines, key_sines)
     q_near = project_queries(near, wq, cosines, sines)
+    wo_other = shift(wo, "c", 1)
     acc_near, state_near = attend_prompt(q_near, cache, prompts[:5])
-    wo = merge_rows(after(wo, acc_near), wo_other)
-    far[0] = after(far[0], pairs_near, wo)
+    far[0] = after(far[0], pairs_near, acc_near)
     pairs_far = project_pairs(far, core_word, wkv, key_cosines, key_sines)
     pairs = jnp.concatenate([pairs_near, pairs_far], axis=0)
     straight = [(g, 2 * g) for g in range(4)] + [(4 + g, 2 * g + 1) for g in range(4)]
@@ -451,13 +474,14 @@
     first, second = lax.ppermute(pairs, chips, straight), lax.ppermute(pairs, chips, crossed)
     far[0] = after(far[0], pairs_far)
     q_far = project_queries(far, wq, cosines, sines)
-    pairs = jnp.stack([after(first, q_far), second])
+    wo = merge_rows(after(wo, q_far), wo_other)
+    pairs = jnp.stack([after(first, wo), second])
     pairs_other = shift(pairs, "c", 1)
     acc, state = attend_prompt(q_far, cache, prompts[5:])
     pairs_other = after(pairs_other, acc)
     att_far = attend_own(q_far, acc, state, pairs, pairs_other, info[:, 5:])
 
-    p12b, p12a, p13, p11 = project_out(att_far, wo, (2, 1, 1))
+    p13, p11, p12b, p12a = project_out(att_far, wo, (1, 1, 2))
     across_a = shift(p12a, "xh", 1)
     up = shift(p11, "y", 1)
     down = shift(p13, "y", -1)
@@ -482,7 +506,8 @@
     total_b = add(after(hidden, total_a), p00, across, up_b, down_b)
     out_a = lax.ppermute(total_a, ("xl", "z"), onward)
     out_b = lax.ppermute(total_b, ("xl", "z"), onward)
-    return jnp.concatenate([out_b, out_a], axis=1)
+    whole = place(out_a, D // 2)
+    return place(out_b, 0, whole)
 
 
 def solution(mesh):

time: 192 us -> 190 us (0.990)
  waiting for transfers between devices: 87.1 us -> 80.8 us
  Pallas kernels: 38 us -> 40.7 us
    ppermute x1, waiting for transfers between devices: 4.77 us -> 0.29 us  [body(): lax.ppermute(pairs, chips, crossed)]
  transfers between devices with their start and end apart: 31 -> 31, of which waited for: 17 -> 16; matrix products, arithmetic and copies ran while one was open for 2% -> 2% of each run, Pallas kernels for 17% -> 19%
where the time goes in v3:
time: 190 us; the launch traced here: 189 us
  waiting for transfers between devices  80.8 us (43%)
  starting transfers between devices  57.7 us (30%)
  Pallas kernels  40.7 us (21%)
  local copies, waits for them, and re-layouts  8.44 us (4%)
    ppermute x26, waiting for transfers between devices, shift(): lax.ppermute(value, axis, [(i, (i + by) % size) for i in range(size)])  63.2 us
    ppermute x26, starting transfers between devices, shift(): lax.ppermute(value, axis, [(i, (i + by) % size) for i in range(size)])  44 us
    ppermute x1, waiting for transfers between devices, body(): out_b = lax.ppermute(total_b, ('xl', 'z'), onward)  10.4 us
    pallas_call x4, Pallas kernels, merge(): pl.pallas_call(functools.partial(merge_kernel, places), out_shape=jax.Sha...  7.61 us
    unnamed x23, local copies, waits for them, and re-layouts  7.28 us
    pallas_call x2, Pallas kernels, attend_prompt(): pl.pallas_call(prompt_kernel, out_shape=(shape, shape), in_specs=[pl.Bloc...  6.6 us
    pallas_call x2, Pallas kernels, project_queries(): pl.pallas_call(functools.partial(query_kernel, len(pieces)), out_shape=ja...  6.25 us
    pallas_call x2, Pallas kernels, attend_own(): pl.pallas_call(own_kernel, out_shape=jax.ShapeDtypeStruct((count, ROWS, 4...  6.09 us
  transfers between devices with their start and end apart: 31, of which 16 were waited for; matrix products, arithmetic and copies ran while one was open for 2% of the time, Pallas kernels for 19%

profile of v3, /device:TPU:2, one launch (start us, length us, event | category | flops | bytes accessed | tf_op | source)
XLA Modules:
  0.0 189.2 jit_solution(16731029963381915833)
XLA Ops:
  2.8 2.2 %collective-permute-start = (bf16[64,8192]{1,0:T(8,128)(2,1)S(1)}, bf16[64,8192]{1,0:T(8,128)(2,1)}, u32[]{:S(2)}, u32[]{:S(2)}) collective-permute-start(bf16[64,8192]{1,0:T(8,128)(2,1)S(1)} %norm.1.refs_0_), channel_id=1, source_target_pairs={{0,8},{8,0},{1,9},{9,1},{2,10},{10,2},{3,11},{11,3},{4,12},{12,4},... | collective-permute-start | bytes 3145736 | tf_op jit(solution)/shard_map/ppermute | solution.py:29
  5.0 1.6 collective-permute-start.2
  6.5 1.7 collective-permute-start.1
  10.8 4.2 %all-to-all-start = ((bf16[8,4,64,256]{3,2,1,0:T(8,128)(2,1)}), bf16[8,4,64,256]{3,2,1,0:T(8,128)(2,1)}, u32[]{:S(2)}, u32[]{:S(2)}) async-start(bf16[8,4,64,256]{3,2,1,0:T(8,128)(2,1)} %copy-done.2), calls=%async_computation | async-start | bytes 2097152 | tf_op jit(solution)/shard_map/all_to_all | solution.py:414
  15.7 14.7 %collective-permute-done.refs_1_ = bf16[64,8192]{1,0:T(8,128)(2,1)} collective-permute-done((bf16[64,8192]{1,0:T(8,128)(2,1)S(1)}, bf16[64,8192]{1,0:T(8,128)(2,1)}, u32[]{:S(2)}, u32[]{:S(2)}) %collective-permute-start) | collective-permute-done | bytes 1048608 | tf_op jit(solution)/shard_map/ppermute | solution.py:29
  30.9 1.5 collective-permute-done.2.refs_2_
  33.2 7.3 %collective-permute-start.5 = (bf16[32,8192]{1,0:T(8,128)(2,1)}, bf16[32,8192]{1,0:T(8,128)(2,1)}, u32[]{:S(2)}, u32[]{:S(2)}) collective-permute-start(bf16[32,8192]{1,0:T(8,128)(2,1)} %slice.20), channel_id=1, source_target_pairs={{0,2},{2,4},{4,6},{6,0},{1,3},{3,5},{5,7},{7,1},{8,10},{10,12},{12... | collective-permute-start | bytes 1572872 | tf_op jit(solution)/shard_map/ppermute | solution.py:29
  40.5 3.0 %all-to-all-done.refs_0_ = bf16[8,4,64,256]{3,2,1,0:T(8,128)(2,1)} async-done(((bf16[8,4,64,256]{3,2,1,0:T(8,128)(2,1)}), bf16[8,4,64,256]{3,2,1,0:T(8,128)(2,1)}, u32[]{:S(2)}, u32[]{:S(2)}) %all-to-all-start) | async-done | bytes 1048608 | tf_op jit(solution)/shard_map/all_to_all | solution.py:414
  43.6 2.4 %collective-permute-start.6 = (bf16[32,8192]{1,0:T(8,128)(2,1)S(1)}, bf16[32,8192]{1,0:T(8,128)(2,1)S(1)}, u32[]{:S(2)}, u32[]{:S(2)}) collective-permute-start(bf16[32,8192]{1,0:T(8,128)(2,1)S(1)} %slice.19), channel_id=1, source_target_pairs={{0,6},{2,0},{4,2},{6,4},{1,7},{3,1},{5,3},{7,5},{8,14},{10,8},{12,... | collective-permute-start | bytes 1572872 | tf_op jit(solution)/shard_map/ppermute | solution.py:29
  45.9 3.2 %collective-permute-start.9 = (bf16[64,8192]{1,0:T(8,128)(2,1)}, bf16[64,8192]{1,0:T(8,128)(2,1)S(1)}, u32[]{:S(2)}, u32[]{:S(2)}) collective-permute-start(bf16[64,8192]{1,0:T(8,128)(2,1)} %collective-permute-done.refs_1_), channel_id=1, source_target_pairs={{0,6},{2,0},{4,2},{6,4},{1,7},{3,1},{5,3},{7,5},{8,14},{10,8},{12,... | collective-permute-start | bytes 3145736 | tf_op jit(solution)/shard_map/ppermute | solution.py:29
  49.2 2.2 %copy-done.3 = bf16[1,8192,256]{2,1,0:T(8,128)(2,1)S(1)} copy-done((bf16[1,8192,256]{2,1,0:T(8,128)(2,1)S(1)}, bf16[1,8192,256]{2,1,0:T(8,128)(2,1)}, u32[]{:S(2)}) %copy-start.3) | copy-done | bytes 4194328
  51.4 2.5 %merge.5.refs_5_.refs_3_ = bf16[8192,512]{1,0:T(8,128)(2,1)S(1)} custom-call(bf16[8192,256]{1,0:T(8,128)(2,1)S(1)} %bitcast.25, bf16[8192,256]{1,0:T(8,128)(2,1)} %collective-permute-done.3.refs_1_), custom_call_target="tpu_custom_call" | custom-call | flops 1 | bytes 1 | tf_op jit(solution)/shard_map/merge/pallas_call | solution.py:76
  53.9 1.3 merge.4.refs_6_.refs_4_
  56.4 2.1 %collective-permute-done.6 = bf16[32,8192]{1,0:T(8,128)(2,1)S(1)} collective-permute-done((bf16[32,8192]{1,0:T(8,128)(2,1)S(1)}, bf16[32,8192]{1,0:T(8,128)(2,1)S(1)}, u32[]{:S(2)}, u32[]{:S(2)}) %collective-permute-start.6) | collective-permute-done | bytes 524320 | tf_op jit(solution)/shard_map/ppermute | solution.py:29
  58.5 1.7 collective-permute-start.10
  60.2 2.9 %pairs.2 = bf16[5,64,128]{2,1,0:T(8,128)(2,1)S(1)} custom-call(bf16[64,8192]{1,0:T(8,128)(2,1)S(1)} %norm.1.refs_0_, bf16[64,8192]{1,0:T(8,128)(2,1)} %collective-permute-done.refs_1_, bf16[64,8192]{1,0:T(8,128)(2,1)S(1)} %collective-permute-done.2.refs_2_, bf16[64,8192]{1,0:T(8,128)(2,1)S(1)} %collective-permute-done.1.refs_3_, ...), custom_call_target="tpu_custom_call" | custom-call | flops 1 | bytes 1 | tf_op jit(solution)/shard_map/pairs/pallas_call | solution.py:167
  63.1 4.3 %queries.2.q_ref = bf16[5,256,128]{2,1,0:T(8,128)(2,1)S(1)} custom-call(bf16[64,8192]{1,0:T(8,128)(2,1)S(1)} %norm.1.refs_0_, bf16[64,8192]{1,0:T(8,128)(2,1)} %collective-permute-done.refs_1_, bf16[64,8192]{1,0:T(8,128)(2,1)S(1)} %collective-permute-done.2.refs_2_, bf16[64,8192]{1,0:T(8,128)(2,1)S(1)} %collective-permute-done.1.refs_3_, ...), custom_call_target="tpu_custom_call" | custom-call | flops 1 | bytes 1 | tf_op jit(solution)/shard_map/queries/pallas_call | solution.py:134
  67.5 1.3 merge.6.cache_ref
  68.7 4.0 %attend_prompt.2 = (f32[5,256,128]{2,1,0:T(8,128)S(1)}, f32[5,256,128]{2,1,0:T(8,128)S(1)}) custom-call(s32[5]{0:T(128)S(1)} %bitcast.35, bf16[5,256,128]{2,1,0:T(8,128)(2,1)S(1)} %queries.2.q_ref, bf16[4,16,64,256]{3,2,1,0:T(8,128)(2,1)S(1)} %merge.6.cache_ref), custom_call_target="tpu_custom_call" | custom-call | flops 1 | bytes 1 | tf_op jit(solution)/shard_map/attend_prompt/pallas_call | solution.py:215
  72.7 3.7 %collective-permute-done.8.refs_0_ = bf16[64,8192]{1,0:T(8,128)(2,1)S(1)} collective-permute-done((bf16[64,8192]{1,0:T(8,128)(2,1)}, bf16[64,8192]{1,0:T(8,128)(2,1)S(1)}, u32[]{:S(2)}, u32[]{:S(2)}) %collective-permute-start.8) | collective-permute-done | bytes 1048608 | tf_op jit(solution)/shard_map/ppermute | solution.py:29
  76.5 2.5 %collective-permute-done.9.refs_1_ = bf16[64,8192]{1,0:T(8,128)(2,1)S(1)} collective-permute-done((bf16[64,8192]{1,0:T(8,128)(2,1)}, bf16[64,8192]{1,0:T(8,128)(2,1)S(1)}, u32[]{:S(2)}, u32[]{:S(2)}) %collective-permute-start.9) | collective-permute-done | bytes 1048608 | tf_op jit(solution)/shard_map/ppermute | solution.py:29
  78.9 4.9 %collective-permute-done.10.refs_2_ = bf16[64,8192]{1,0:T(8,128)(2,1)S(1)} collective-permute-done((bf16[64,8192]{1,0:T(8,128)(2,1)S(1)}, bf16[64,8192]{1,0:T(8,128)(2,1)S(1)}, u32[]{:S(2)}, u32[]{:S(2)}) %collective-permute-start.10) | collective-permute-done | bytes 1048608 | tf_op jit(solution)/shard_map/ppermute | solution.py:29
  85.8 4.7 %collective-permute-start.13 = (bf16[8,64,128]{2,1,0:T(8,128)(2,1)S(1)}, bf16[8,64,128]{2,1,0:T(8,128)(2,1)S(1)}, u32[]{:S(2)}, u32[]{:S(2)}) collective-permute-start(bf16[8,64,128]{2,1,0:T(8,128)(2,1)S(1)} %pad_maximum_fusion.1), channel_id=1, source_target_pairs={{0,2},{2,6},{4,10},{6,14},{8,0},{10,4},{12,8},{14,12},{1,3},{3,7},... | collective-permute-start | bytes 393224 | tf_op jit(solution)/shard_map/ppermute | solution.py:474
  90.5 1.9 %queries.3.q_ref = bf16[3,256,128]{2,1,0:T(8,128)(2,1)S(1)} custom-call(bf16[64,8192]{1,0:T(8,128)(2,1)S(1)} %collective-permute-done.8.refs_0_, bf16[64,8192]{1,0:T(8,128)(2,1)S(1)} %collective-permute-done.9.refs_1_, bf16[64,8192]{1,0:T(8,128)(2,1)S(1)} %collective-permute-done.10.refs_2_, bf16[8192,512]{1,0:T(8,128)(2,1)S(1)} %merge.5.refs_5_.refs_3_, ...), custom_call_target="tpu_custom_call" | custom-call | flops 1 | bytes 1 | tf_op jit(solution)/shard_map/queries/pallas_call | solution.py:134
  92.4 2.5 %merge.7.w_ref = bf16[512,8192]{1,0:T(8,128)(2,1)S(1)} custom-call(bf16[256,8192]{1,0:T(8,128)(2,1)S(1)} %bitcast.27, bf16[256,8192]{1,0:T(8,128)(2,1)} %collective-permute-done.12.refs_1_), custom_call_target="tpu_custom_call" | custom-call | flops 1 | bytes 1 | tf_op jit(solution)/shard_map/merge/pallas_call | solution.py:76
  95.5 2.6 %attend_prompt.3 = (f32[3,256,128]{2,1,0:T(8,128)S(1)}, f32[3,256,128]{2,1,0:T(8,128)S(1)}) custom-call(s32[3]{0:T(128)S(1)} %slice.23.prompt_ref, bf16[3,256,128]{2,1,0:T(8,128)(2,1)S(1)} %queries.3.q_ref, bf16[4,16,64,256]{3,2,1,0:T(8,128)(2,1)S(1)} %merge.6.cache_ref), custom_call_target="tpu_custom_call" | custom-call | flops 1 | bytes 1 | tf_op jit(solution)/shard_map/attend_prompt/pallas_call | solution.py:215
  98.1 2.4 %attend_own.2 = bf16[3,64,512]{2,1,0:T(8,128)(2,1)S(1)} custom-call(s32[5,3]{1,0:T(8,128)S(1)} %slice.22.info_ref, bf16[3,256,128]{2,1,0:T(8,128)(2,1)S(1)} %queries.3.q_ref, f32[3,256,128]{2,1,0:T(8,128)S(1)} %get-tuple-element.62.acc_ref, f32[3,256,128]{2,1,0:T(8,128)S(1)} %get-tuple-element.63.state_ref, ...), custom_call_target="tpu_custom_call" | custom-call | flops 1 | bytes 1 | tf_op jit(solution)/shard_map/attend_own/pallas_call | solution.py:262
  100.5 2.4 %project_out.2 = (bf16[64,8192]{1,0:T(8,128)(2,1)S(1)}, bf16[64,8192]{1,0:T(8,128)(2,1)S(1)}, bf16[64,4096]{1,0:T(8,128)(2,1)S(1)}, bf16[64,4096]{1,0:T(8,128)(2,1)S(1)}) custom-call(bf16[192,512]{1,0:T(8,128)(2,1)S(1)} %bitcast.33, bf16[512,8192]{1,0:T(8,128)(2,1)S(1)} %merge.7.w_ref), custom_call_target="tpu_custom_call" | custom-call | flops 1 | bytes 1 | tf_op jit(solution)/shard_map/project_out/pallas_call | solution.py:294
  102.9 2.1 %collective-permute-start.16 = (bf16[64,8192]{1,0:T(8,128)(2,1)S(1)}, bf16[64,8192]{1,0:T(8,128)(2,1)S(1)}, u32[]{:S(2)}, u32[]{:S(2)}) collective-permute-start(bf16[64,8192]{1,0:T(8,128)(2,1)S(1)} %get-tuple-element.65), channel_id=1, source_target_pairs={{0,2},{2,4},{4,6},{6,0},{1,3},{3,5},{5,7},{7,1},{8,10},{10,12},{12... | collective-permute-start | bytes 3145736 | tf_op jit(solution)/shard_map/ppermute | solution.py:29
  105.0 2.1 %collective-permute-start.17 = (bf16[64,8192]{1,0:T(8,128)(2,1)S(1)}, bf16[64,8192]{1,0:T(8,128)(2,1)S(1)}, u32[]{:S(2)}, u32[]{:S(2)}) collective-permute-start(bf16[64,8192]{1,0:T(8,128)(2,1)S(1)} %get-tuple-element.73), channel_id=1, source_target_pairs={{0,6},{2,0},{4,2},{6,4},{1,7},{3,1},{5,3},{7,5},{8,14},{10,8},{12,... | collective-permute-start | bytes 3145736 | tf_op jit(solution)/shard_map/ppermute | solution.py:29
  107.1 2.7 %collective-permute-start.15 = (bf16[64,4096]{1,0:T(8,128)(2,1)S(1)}, bf16[64,4096]{1,0:T(8,128)(2,1)S(1)}, u32[]{:S(2)}, u32[]{:S(2)}) collective-permute-start(bf16[64,4096]{1,0:T(8,128)(2,1)S(1)} %get-tuple-element.70), channel_id=1, source_target_pairs={{0,8},{8,0},{1,9},{9,1},{2,10},{10,2},{3,11},{11,3},{4,12},{12,4},... | collective-permute-start | bytes 1572872 | tf_op jit(solution)/shard_map/ppermute | solution.py:29
  110.6 3.7 %attend_own.3 = bf16[5,64,512]{2,1,0:T(8,128)(2,1)S(1)} custom-call(s32[5,5]{1,0:T(8,128)S(1)} %bitcast.34, bf16[5,256,128]{2,1,0:T(8,128)(2,1)S(1)} %queries.2.q_ref, f32[5,256,128]{2,1,0:T(8,128)S(1)} %get-tuple-element.56.acc_ref, f32[5,256,128]{2,1,0:T(8,128)S(1)} %get-tuple-element.57.state_ref, bf16[2,8,64,128]{3,2,1,0:T(8,128)(2,1)S(1)} %pad_maximum_fusion.own_ref, ...), custom_call_target="tpu_custom_call" | custom-call | flops 1 | bytes 1 | tf_op jit(solution)/shard_map/attend_own/pallas_call | solution.py:262
  114.3 3.4 %project_out.3 = (bf16[64,8192]{1,0:T(8,128)(2,1)S(1)}, bf16[64,8192]{1,0:T(8,128)(2,1)S(1)}, bf16[64,4096]{1,0:T(8,128)(2,1)S(1)}, bf16[64,4096]{1,0:T(8,128)(2...) custom-call(bf16[320,512]{1,0:T(8,128)(2,1)S(1)} %bitcast.30, ...), custom_call_target="tpu_custom_call" | custom-call | flops 1 | bytes 1 | tf_op jit(solution)/shard_map/project_out/pallas_call | solution.py:294
  117.7 5.7 %collective-permute-done.15.b_ref = bf16[64,4096]{1,0:T(8,128)(2,1)S(1)} collective-permute-done((bf16[64,4096]{1,0:T(8,128)(2,1)S(1)}, bf16[64,4096]{1,0:T(8,128)(2,1)S(1)}, u32[]{:S(2)}, u32[]{:S(2)}) %collective-permute-start.15) | collective-permute-done | bytes 524320 | tf_op jit(solution)/shard_map/ppermute | solution.py:29
  123.5 7.3 %collective-permute-done.16.refs_1_ = bf16[64,8192]{1,0:T(8,128)(2,1)S(1)} collective-permute-done((bf16[64,8192]{1,0:T(8,128)(2,1)S(1)}, bf16[64,8192]{1,0:T(8,128)(2,1)S(1)}, u32[]{:S(2)}, u32[]{:S(2)}) %collective-permute-start.16) | collective-permute-done | bytes 1048608 | tf_op jit(solution)/shard_map/ppermute | solution.py:29
  131.2 2.6 %collective-permute-start.18 = (bf16[64,8192]{1,0:T(8,128)(2,1)S(1)}, bf16[64,8192]{1,0:T(8,128)(2,1)S(1)}, u32[]{:S(2)}, u32[]{:S(2)}) collective-permute-start(bf16[64,8192]{1,0:T(8,128)(2,1)S(1)} %add.167), channel_id=1, source_target_pairs={{0,8},{8,0},{1,9},{9,1},{2,10},{10,2},{3,11},{11,3},{4,12},{12,4},... | collective-permute-start | bytes 3145736 | tf_op jit(solution)/shard_map/ppermute | solution.py:29
  134.2 2.9 %collective-permute-start.21 = (bf16[64,2048]{1,0:T(8,128)(2,1)S(1)}, bf16[64,2048]{1,0:T(8,128)(2,1)S(1)}, u32[]{:S(2)}, u32[]{:S(2)}) collective-permute-start(bf16[64,2048]{1,0:T(8,128)(2,1)S(1)} %get-tuple-element.81), channel_id=1, source_target_pairs={{0,6},{2,0},{4,2},{6,4},{1,7},{3,1},{5,3},{7,5},{8,14},{10,8},{12,... | collective-permute-start | bytes 786440 | tf_op jit(solution)/shard_map/ppermute | solution.py:29
  137.3 3.2 %collective-permute-start.26 = (bf16[64,2048]{1,0:T(8,128)(2,1)S(1)}, bf16[64,2048]{1,0:T(8,128)(2,1)S(1)}, u32[]{:S(2)}, u32[]{:S(2)}) collective-permute-start(bf16[64,2048]{1,0:T(8,128)(2,1)S(1)} %get-tuple-element.88), channel_id=1, source_target_pairs={{0,6},{2,0},{4,2},{6,4},{1,7},{3,1},{5,3},{7,5},{8,14},{10,8},{12,... | collective-permute-start | bytes 786440 | tf_op jit(solution)/shard_map/ppermute | solution.py:29
  140.5 3.8 %collective-permute-done.20.up_ref = bf16[64,2048]{1,0:T(8,128)(2,1)S(1)} collective-permute-done((bf16[64,2048]{1,0:T(8,128)(2,1)S(1)}, bf16[64,2048]{1,0:T(8,128)(2,1)S(1)}, u32[]{:S(2)}, u32[]{:S(2)}) %collective-permute-start.20) | collective-permute-done | bytes 262176 | tf_op jit(solution)/shard_map/ppermute | solution.py:29
  145.7 2.2 %collective-permute-start.23 = (bf16[64,4096]{1,0:T(8,128)(2,1)S(1)}, bf16[64,4096]{1,0:T(8,128)(2,1)S(1)}, u32[]{:S(2)}, u32[]{:S(2)}) collective-permute-start(bf16[64,4096]{1,0:T(8,128)(2,1)S(1)} %get-tuple-element.83), channel_id=1, source_target_pairs={{0,6},{2,0},{4,2},{6,4},{1,7},{3,1},{5,3},{7,5},{8,14},{10,8},{12,... | collective-permute-start | bytes 1572872 | tf_op jit(solution)/shard_map/ppermute | solution.py:29
  147.9 2.1 %collective-permute-done.25.up_ref = bf16[64,2048]{1,0:T(8,128)(2,1)S(1)} collective-permute-done((bf16[64,2048]{1,0:T(8,128)(2,1)S(1)}, bf16[64,2048]{1,0:T(8,128)(2,1)S(1)}, u32[]{:S(2)}, u32[]{:S(2)}) %collective-permute-start.25) | collective-permute-done | bytes 262176 | tf_op jit(solution)/shard_map/ppermute | solution.py:29
  151.3 2.2 %collective-permute-start.28 = (bf16[64,4096]{1,0:T(8,128)(2,1)S(1)}, bf16[64,4096]{1,0:T(8,128)(2,1)S(1)}, u32[]{:S(2)}, u32[]{:S(2)}) collective-permute-start(bf16[64,4096]{1,0:T(8,128)(2,1)S(1)} %get-tuple-element.90), channel_id=1, source_target_pairs={{0,6},{2,0},{4,2},{6,4},{1,7},{3,1},{5,3},{7,5},{8,14},{10,8},{12,... | collective-permute-start | bytes 1572872 | tf_op jit(solution)/shard_map/ppermute | solution.py:29
  153.5 7.7 %collective-permute-done.22.refs_3_ = bf16[64,4096]{1,0:T(8,128)(2,1)S(1)} collective-permute-done((bf16[64,4096]{1,0:T(8,128)(2,1)S(1)}, bf16[64,4096]{1,0:T(8,128)(2,1)S(1)}, u32[]{:S(2)}, u32[]{:S(2)}) %collective-permute-start.22) | collective-permute-done | bytes 524320 | tf_op jit(solution)/shard_map/ppermute | solution.py:29
  161.5 2.0 %collective-permute-start.24 = (bf16[64,4096]{1,0:T(8,128)(2,1)S(1)}, bf16[64,4096]{1,0:T(8,128)(2,1)S(1)}, u32[]{:S(2)}, u32[]{:S(2)}) collective-permute-start(bf16[64,4096]{1,0:T(8,128)(2,1)S(1)} %add.168), channel_id=1, source_target_pairs={{0,16},{16,32},{32,48},{48,64},{64,80},{80,96},{96,112},{112,128},... | collective-permute-start | bytes 1572872 | tf_op jit(solution)/shard_map/ppermute | solution.py:507
  163.5 7.3 %collective-permute-done.27.refs_3_ = bf16[64,4096]{1,0:T(8,128)(2,1)S(1)} collective-permute-done((bf16[64,4096]{1,0:T(8,128)(2,1)S(1)}, bf16[64,4096]{1,0:T(8,128)(2,1)S(1)}, u32[]{:S(2)}, u32[]{:S(2)}) %collective-permute-start.27) | collective-permute-done | bytes 524320 | tf_op jit(solution)/shard_map/ppermute | solution.py:29
  171.1 2.0 %collective-permute-start.29 = (bf16[64,4096]{1,0:T(8,128)(2,1)S(1)}, bf16[64,4096]{1,0:T(8,128)(2,1)S(1)}, u32[]{:S(2)}, u32[]{:S(2)}) collective-permute-start(bf16[64,4096]{1,0:T(8,128)(2,1)S(1)} %add.169), channel_id=1, source_target_pairs={{0,16},{16,32},{32,48},{48,64},{64,80},{80,96},{96,112},{112,128},... | collective-permute-start | bytes 1572872 | tf_op jit(solution)/shard_map/ppermute | solution.py:508
  173.1 3.8 %collective-permute-done.24.refs_0_ = bf16[64,4096]{1,0:T(8,128)(2,1)S(1)} collective-permute-done((bf16[64,4096]{1,0:T(8,128)(2,1)S(1)}, bf16[64,4096]{1,0:T(8,128)(2,1)S(1)}, u32[]{:S(2)}, u32[]{:S(2)}) %collective-permute-start.24) | collective-permute-done | bytes 524320 | tf_op jit(solution)/shard_map/ppermute | solution.py:507
  177.7 10.4 %collective-permute-done.29.refs_1_ = bf16[64,4096]{1,0:T(8,128)(2,1)S(1)} collective-permute-done((bf16[64,4096]{1,0:T(8,128)(2,1)S(1)}, bf16[64,4096]{1,0:T(8,128)(2,1)S(1)}, u32[]{:S(2)}, u32[]{:S(2)}) %collective-permute-start.29) | collective-permute-done | bytes 524320 | tf_op jit(solution)/shard_map/ppermute | solution.py:508
  (81 shorter events, 17.6 us)
Async XLA Ops:
  0.0 15.5 %copy-start.10 = (s32[8]{0:T(128)S(1)}, s32[8]{0:T(128)}, u32[]{:S(2)}) copy-start(s32[8]{0:T(128)} %constant.114.clone) | copy-start | bytes 100
  0.0 15.2 %copy-start.9 = (s32[8]{0:T(128)S(1)}, s32[8]{0:T(128)}, u32[]{:S(2)}) copy-start(s32[8]{0:T(128)} %param.15) | copy-start | bytes 100
  0.0 15.2 %copy-start.8 = (s32[8]{0:T(128)S(1)}, s32[8]{0:T(128)}, u32[]{:S(2)}) copy-start(s32[8]{0:T(128)} %param.16) | copy-start | bytes 100
  0.0 32.4 %collective-permute-start.3 = (bf16[8192,256]{1,0:T(8,128)(2,1)}, bf16[8192,256]{1,0:T(8,128)(2,1)}, u32[]{:S(2)}, u32[]{:S(2)}) collective-permute-start(bf16[8192,256]{1,0:T(8,128)(2,1)} %bitcast.24), channel_id=1, source_target_pairs={{0,1},{1,0},{2,3},{3,2},{4,5},{5,4},{6,7},{7,6},{8,9},{9,8},{10,11... | collective-permute-start | bytes 12582920 | tf_op jit(solution)/shard_map/ppermute | solution.py:29
  0.1 1.2 copy-start
  1.3 0.8 copy-start.7
  2.8 27.7 %collective-permute-start = (bf16[64,8192]{1,0:T(8,128)(2,1)S(1)}, bf16[64,8192]{1,0:T(8,128)(2,1)}, u32[]{:S(2)}, u32[]{:S(2)}) collective-permute-start(bf16[64,8192]{1,0:T(8,128)(2,1)S(1)} %norm.1.refs_0_), channel_id=1, source_target_pairs={{0,8},{8,0},{1,9},{9,1},{2,10},{10,2},{3,11},{11,3},{4,12},{12,4},... | collective-permute-start | bytes 3145736 | tf_op jit(solution)/shard_map/ppermute | solution.py:29
  5.0 27.4 %collective-permute-start.2 = (bf16[64,8192]{1,0:T(8,128)(2,1)S(1)}, bf16[64,8192]{1,0:T(8,128)(2,1)S(1)}, u32[]{:S(2)}, u32[]{:S(2)}) collective-permute-start(bf16[64,8192]{1,0:T(8,128)(2,1)S(1)} %norm.1.refs_0_), channel_id=1, source_target_pairs={{0,2},{2,4},{4,6},{6,0},{1,3},{3,5},{5,7},{7,1},{8,10},{10,12},{12... | collective-permute-start | bytes 3145736 | tf_op jit(solution)/shard_map/ppermute | solution.py:29
  6.5 37.0 %collective-permute-start.1 = (bf16[64,8192]{1,0:T(8,128)(2,1)S(1)}, bf16[64,8192]{1,0:T(8,128)(2,1)S(1)}, u32[]{:S(2)}, u32[]{:S(2)}) collective-permute-start(bf16[64,8192]{1,0:T(8,128)(2,1)S(1)} %norm.1.refs_0_), channel_id=1, source_target_pairs={{0,6},{2,0},{4,2},{6,4},{1,7},{3,1},{5,3},{7,5},{8,14},{10,8},{12,... | collective-permute-start | bytes 3145736 | tf_op jit(solution)/shard_map/ppermute | solution.py:29
  8.2 24.2 %collective-permute-start.4 = (bf16[64,8192]{1,0:T(8,128)(2,1)}, bf16[64,8192]{1,0:T(8,128)(2,1)}, u32[]{:S(2)}, u32[]{:S(2)}) collective-permute-start(bf16[64,8192]{1,0:T(8,128)(2,1)} %bitcast.31), channel_id=1, source_target_pairs={{0,1},{1,0},{2,3},{3,2},{4,5},{5,4},{6,7},{7,6},{8,9},{9,8},{10,11... | collective-permute-start | bytes 3145736 | tf_op jit(solution)/shard_map/ppermute | solution.py:29
  8.2 1.0 copy-start.5
  9.8 1.0 copy-start.2
  10.8 32.7 %all-to-all-start = ((bf16[8,4,64,256]{3,2,1,0:T(8,128)(2,1)}), bf16[8,4,64,256]{3,2,1,0:T(8,128)(2,1)}, u32[]{:S(2)}, u32[]{:S(2)}) async-start(bf16[8,4,64,256]{3,2,1,0:T(8,128)(2,1)} %copy-done.2), calls=%async_computation | async-start | bytes 2097152 | tf_op jit(solution)/shard_map/all_to_all | solution.py:414
  30.4 62.0 %collective-permute-start.12 = (bf16[256,8192]{1,0:T(8,128)(2,1)}, bf16[256,8192]{1,0:T(8,128)(2,1)}, u32[]{:S(2)}, u32[]{:S(2)}) collective-permute-start(bf16[256,8192]{1,0:T(8,128)(2,1)} %bitcast.26), channel_id=1, source_target_pairs={{0,1},{1,0},{2,3},{3,2},{4,5},{5,4},{6,7},{7,6},{8,9},{9,8},{10,11... | collective-permute-start | bytes 12582920 | tf_op jit(solution)/shard_map/ppermute | solution.py:29
  33.2 22.0 %collective-permute-start.5 = (bf16[32,8192]{1,0:T(8,128)(2,1)}, bf16[32,8192]{1,0:T(8,128)(2,1)}, u32[]{:S(2)}, u32[]{:S(2)}) collective-permute-start(bf16[32,8192]{1,0:T(8,128)(2,1)} %slice.20), channel_id=1, source_target_pairs={{0,2},{2,4},{4,6},{6,0},{1,3},{3,5},{5,7},{7,1},{8,10},{10,12},{12... | collective-permute-start | bytes 1572872 | tf_op jit(solution)/shard_map/ppermute | solution.py:29
  43.5 10.4 %copy-start.6 = (bf16[1,8192,64]{1,2,0:T(8,128)(2,1)S(1)}, bf16[1,8192,64]{1,2,0:T(8,128)(2,1)}, u32[]{:S(2)}) copy-start(bf16[1,8192,64]{1,2,0:T(8,128)(2,1)} %param.12) | copy-start | bytes 3145732
  43.6 14.9 %collective-permute-start.6 = (bf16[32,8192]{1,0:T(8,128)(2,1)S(1)}, bf16[32,8192]{1,0:T(8,128)(2,1)S(1)}, u32[]{:S(2)}, u32[]{:S(2)}) collective-permute-start(bf16[32,8192]{1,0:T(8,128)(2,1)S(1)} %slice.19), channel_id=1, source_target_pairs={{0,6},{2,0},{4,2},{6,4},{1,7},{3,1},{5,3},{7,5},{8,14},{10,8},{12,... | collective-permute-start | bytes 1572872 | tf_op jit(solution)/shard_map/ppermute | solution.py:29
  45.9 30.5 %collective-permute-start.8 = (bf16[64,8192]{1,0:T(8,128)(2,1)}, bf16[64,8192]{1,0:T(8,128)(2,1)S(1)}, u32[]{:S(2)}, u32[]{:S(2)}) collective-permute-start(bf16[64,8192]{1,0:T(8,128)(2,1)} %collective-permute-done.refs_1_), channel_id=1, source_target_pairs={{0,2},{2,4},{4,6},{6,0},{1,3},{3,5},{5,7},{7,1},{8,10},{10,12},{12... | collective-permute-start | bytes 3145736 | tf_op jit(solution)/shard_map/ppermute | solution.py:29
  45.9 33.0 %collective-permute-start.9 = (bf16[64,8192]{1,0:T(8,128)(2,1)}, bf16[64,8192]{1,0:T(8,128)(2,1)S(1)}, u32[]{:S(2)}, u32[]{:S(2)}) collective-permute-start(bf16[64,8192]{1,0:T(8,128)(2,1)} %collective-permute-done.refs_1_), channel_id=1, source_target_pairs={{0,6},{2,0},{4,2},{6,4},{1,7},{3,1},{5,3},{7,5},{8,14},{10,8},{12,... | collective-permute-start | bytes 3145736 | tf_op jit(solution)/shard_map/ppermute | solution.py:29
  49.2 2.2 %copy-start.3 = (bf16[1,8192,256]{2,1,0:T(8,128)(2,1)S(1)}, bf16[1,8192,256]{2,1,0:T(8,128)(2,1)}, u32[]{:S(2)}) copy-start(bf16[1,8192,256]{2,1,0:T(8,128)(2,1)} %param.11) | copy-start | bytes 12582916
  55.3 12.2 %collective-permute-start.7 = (bf16[8,4,64,256]{3,2,1,0:T(8,128)(2,1)}, bf16[8,4,64,256]{3,2,1,0:T(8,128)(2,1)S(1)}, u32[]{:S(2)}, u32[]{:S(2)}) collective-permute-start(bf16[8,4,64,256]{3,2,1,0:T(8,128)(2,1)} %all-to-all-done.refs_0_), channel_id=1, source_target_pairs={{0,1},{1,0},{2,3},{3,2},{4,5},{5,4},{6,7},{7,6},{8,9},{9,8},{10,11... | collective-permute-start | bytes 3145736 | tf_op jit(solution)/shard_map/ppermute | solution.py:29
  58.5 25.3 %collective-permute-start.10 = (bf16[64,8192]{1,0:T(8,128)(2,1)S(1)}, bf16[64,8192]{1,0:T(8,128)(2,1)S(1)}, u32[]{:S(2)}, u32[]{:S(2)}) collective-permute-start(bf16[64,8192]{1,0:T(8,128)(2,1)S(1)} %constant_dynamic-update-slice_fusion.refs_4_), channel_id=1, source_target_pairs={{0,8},{8,0},{1,9},{9,1},{2,10},{10,2},{3,11},{11,3},{4,12},{12,4},... | collective-permute-start | bytes 3145736 | tf_op jit(solution)/shard_map/ppermute | solution.py:29
  85.0 7.4 %copy-start.4 = (bf16[1,256,8192]{2,1,0:T(8,128)(2,1)S(1)}, bf16[1,256,8192]{2,1,0:T(8,128)(2,1)}, u32[]{:S(2)}) copy-start(bf16[1,256,8192]{2,1,0:T(8,128)(2,1)} %param.13) | copy-start | bytes 12582916
  85.0 9.9 %collective-permute-start.11 = (bf16[8,64,128]{2,1,0:T(8,128)(2,1)S(1)}, bf16[8,64,128]{2,1,0:T(8,128)(2,1)S(1)}, u32[]{:S(2)}, u32[]{:S(2)}) collective-permute-start(bf16[8,64,128]{2,1,0:T(8,128)(2,1)S(1)} %pad_maximum_fusion.1), channel_id=1, source_target_pairs={{0,0},{2,4},{4,8},{6,12},{8,2},{10,6},{12,10},{14,14},{1,1},{3,5},... | collective-permute-start | bytes 393224 | tf_op jit(solution)/shard_map/ppermute | solution.py:474
  85.8 9.4 %collective-permute-start.13 = (bf16[8,64,128]{2,1,0:T(8,128)(2,1)S(1)}, bf16[8,64,128]{2,1,0:T(8,128)(2,1)S(1)}, u32[]{:S(2)}, u32[]{:S(2)}) collective-permute-start(bf16[8,64,128]{2,1,0:T(8,128)(2,1)S(1)} %pad_maximum_fusion.1), channel_id=1, source_target_pairs={{0,2},{2,6},{4,10},{6,14},{8,0},{10,4},{12,8},{14,12},{1,3},{3,7},... | collective-permute-start | bytes 393224 | tf_op jit(solution)/shard_map/ppermute | solution.py:474
  95.2 2.9 %collective-permute-start.14 = (bf16[2,8,64,128]{3,2,1,0:T(8,128)(2,1)S(1)}, bf16[2,8,64,128]{3,2,1,0:T(8,128)(2,1)S(1)}, u32[]{:S(2)}, u32[]{:S(2)}) collective-permute-start(bf16[2,8,64,128]{3,2,1,0:T(8,128)(2,1)S(1)} %pad_maximum_fusion.own_ref), channel_id=1, source_target_pairs={{0,1},{1,0},{2,3},{3,2},{4,5},{5,4},{6,7},{7,6},{8,9},{9,8},{10,11... | collective-permute-start | bytes 786440 | tf_op jit(solution)/shard_map/ppermute | solution.py:29
  102.9 27.9 %collective-permute-start.16 = (bf16[64,8192]{1,0:T(8,128)(2,1)S(1)}, bf16[64,8192]{1,0:T(8,128)(2,1)S(1)}, u32[]{:S(2)}, u32[]{:S(2)}) collective-permute-start(bf16[64,8192]{1,0:T(8,128)(2,1)S(1)} %get-tuple-element.65), channel_id=1, source_target_pairs={{0,2},{2,4},{4,6},{6,0},{1,3},{3,5},{5,7},{7,1},{8,10},{10,12},{12... | collective-permute-start | bytes 3145736 | tf_op jit(solution)/shard_map/ppermute | solution.py:29
  105.0 25.8 %collective-permute-start.17 = (bf16[64,8192]{1,0:T(8,128)(2,1)S(1)}, bf16[64,8192]{1,0:T(8,128)(2,1)S(1)}, u32[]{:S(2)}, u32[]{:S(2)}) collective-permute-start(bf16[64,8192]{1,0:T(8,128)(2,1)S(1)} %get-tuple-element.73), channel_id=1, source_target_pairs={{0,6},{2,0},{4,2},{6,4},{1,7},{3,1},{5,3},{7,5},{8,14},{10,8},{12,... | collective-permute-start | bytes 3145736 | tf_op jit(solution)/shard_map/ppermute | solution.py:29
  107.1 16.3 %collective-permute-start.15 = (bf16[64,4096]{1,0:T(8,128)(2,1)S(1)}, bf16[64,4096]{1,0:T(8,128)(2,1)S(1)}, u32[]{:S(2)}, u32[]{:S(2)}) collective-permute-start(bf16[64,4096]{1,0:T(8,128)(2,1)S(1)} %get-tuple-element.70), channel_id=1, source_target_pairs={{0,8},{8,0},{1,9},{9,1},{2,10},{10,2},{3,11},{11,3},{4,12},{12,4},... | collective-permute-start | bytes 1572872 | tf_op jit(solution)/shard_map/ppermute | solution.py:29
  109.9 27.2 %collective-permute-start.19 = (bf16[64,4096]{1,0:T(8,128)(2,1)S(1)}, bf16[64,4096]{1,0:T(8,128)(2,1)S(1)}, u32[]{:S(2)}, u32[]{:S(2)}) collective-permute-start(bf16[64,4096]{1,0:T(8,128)(2,1)S(1)} %get-tuple-element.77), channel_id=1, source_target_pairs={{0,8},{8,0},{1,9},{9,1},{2,10},{10,2},{3,11},{11,3},{4,12},{12,4},... | collective-permute-start | bytes 1572872 | tf_op jit(solution)/shard_map/ppermute | solution.py:29
  123.5 37.7 %copy-start.1 = (bf16[64,8192]{1,0:T(8,128)(2,1)S(1)}, bf16[64,8192]{1,0:T(8,128)(2,1)}, u32[]{:S(2)}) copy-start(bf16[64,8192]{1,0:T(8,128)(2,1)} %refs_0_.2) | copy-start | bytes 3145732
  131.2 29.9 %collective-permute-start.18 = (bf16[64,8192]{1,0:T(8,128)(2,1)S(1)}, bf16[64,8192]{1,0:T(8,128)(2,1)S(1)}, u32[]{:S(2)}, u32[]{:S(2)}) collective-permute-start(bf16[64,8192]{1,0:T(8,128)(2,1)S(1)} %add.167), channel_id=1, source_target_pairs={{0,8},{8,0},{1,9},{9,1},{2,10},{10,2},{3,11},{11,3},{4,12},{12,4},... | collective-permute-start | bytes 3145736 | tf_op jit(solution)/shard_map/ppermute | solution.py:29
  133.9 10.5 %collective-permute-start.20 = (bf16[64,2048]{1,0:T(8,128)(2,1)S(1)}, bf16[64,2048]{1,0:T(8,128)(2,1)S(1)}, u32[]{:S(2)}, u32[]{:S(2)}) collective-permute-start(bf16[64,2048]{1,0:T(8,128)(2,1)S(1)} %get-tuple-element.71), channel_id=1, source_target_pairs={{0,2},{2,4},{4,6},{6,0},{1,3},{3,5},{5,7},{7,1},{8,10},{10,12},{12... | collective-permute-start | bytes 786440 | tf_op jit(solution)/shard_map/ppermute | solution.py:29
  134.2 10.2 %collective-permute-start.21 = (bf16[64,2048]{1,0:T(8,128)(2,1)S(1)}, bf16[64,2048]{1,0:T(8,128)(2,1)S(1)}, u32[]{:S(2)}, u32[]{:S(2)}) collective-permute-start(bf16[64,2048]{1,0:T(8,128)(2,1)S(1)} %get-tuple-element.81), channel_id=1, source_target_pairs={{0,6},{2,0},{4,2},{6,4},{1,7},{3,1},{5,3},{7,5},{8,14},{10,8},{12,... | collective-permute-start | bytes 786440 | tf_op jit(solution)/shard_map/ppermute | solution.py:29
  137.2 12.7 %collective-permute-start.25 = (bf16[64,2048]{1,0:T(8,128)(2,1)S(1)}, bf16[64,2048]{1,0:T(8,128)(2,1)S(1)}, u32[]{:S(2)}, u32[]{:S(2)}) collective-permute-start(bf16[64,2048]{1,0:T(8,128)(2,1)S(1)} %get-tuple-element.78), channel_id=1, source_target_pairs={{0,2},{2,4},{4,6},{6,0},{1,3},{3,5},{5,7},{7,1},{8,10},{10,12},{12... | collective-permute-start | bytes 786440 | tf_op jit(solution)/shard_map/ppermute | solution.py:29
  137.3 12.6 %collective-permute-start.26 = (bf16[64,2048]{1,0:T(8,128)(2,1)S(1)}, bf16[64,2048]{1,0:T(8,128)(2,1)S(1)}, u32[]{:S(2)}, u32[]{:S(2)}) collective-permute-start(bf16[64,2048]{1,0:T(8,128)(2,1)S(1)} %get-tuple-element.88), channel_id=1, source_target_pairs={{0,6},{2,0},{4,2},{6,4},{1,7},{3,1},{5,3},{7,5},{8,14},{10,8},{12,... | collective-permute-start | bytes 786440 | tf_op jit(solution)/shard_map/ppermute | solution.py:29
  144.5 16.7 %collective-permute-start.22 = (bf16[64,4096]{1,0:T(8,128)(2,1)S(1)}, bf16[64,4096]{1,0:T(8,128)(2,1)S(1)}, u32[]{:S(2)}, u32[]{:S(2)}) collective-permute-start(bf16[64,4096]{1,0:T(8,128)(2,1)S(1)} %get-tuple-element.82), channel_id=1, source_target_pairs={{0,2},{2,4},{4,6},{6,0},{1,3},{3,5},{5,7},{7,1},{8,10},{10,12},{12... | collective-permute-start | bytes 1572872 | tf_op jit(solution)/shard_map/ppermute | solution.py:29
  145.7 15.5 %collective-permute-start.23 = (bf16[64,4096]{1,0:T(8,128)(2,1)S(1)}, bf16[64,4096]{1,0:T(8,128)(2,1)S(1)}, u32[]{:S(2)}, u32[]{:S(2)}) collective-permute-start(bf16[64,4096]{1,0:T(8,128)(2,1)S(1)} %get-tuple-element.83), channel_id=1, source_target_pairs={{0,6},{2,0},{4,2},{6,4},{1,7},{3,1},{5,3},{7,5},{8,14},{10,8},{12,... | collective-permute-start | bytes 1572872 | tf_op jit(solution)/shard_map/ppermute | solution.py:29
  150.1 20.7 %collective-permute-start.27 = (bf16[64,4096]{1,0:T(8,128)(2,1)S(1)}, bf16[64,4096]{1,0:T(8,128)(2,1)S(1)}, u32[]{:S(2)}, u32[]{:S(2)}) collective-permute-start(bf16[64,4096]{1,0:T(8,128)(2,1)S(1)} %get-tuple-element.89), channel_id=1, source_target_pairs={{0,2},{2,4},{4,6},{6,0},{1,3},{3,5},{5,7},{7,1},{8,10},{10,12},{12... | collective-permute-start | bytes 1572872 | tf_op jit(solution)/shard_map/ppermute | solution.py:29
  151.3 19.5 %collective-permute-start.28 = (bf16[64,4096]{1,0:T(8,128)(2,1)S(1)}, bf16[64,4096]{1,0:T(8,128)(2,1)S(1)}, u32[]{:S(2)}, u32[]{:S(2)}) collective-permute-start(bf16[64,4096]{1,0:T(8,128)(2,1)S(1)} %get-tuple-element.90), channel_id=1, source_target_pairs={{0,6},{2,0},{4,2},{6,4},{1,7},{3,1},{5,3},{7,5},{8,14},{10,8},{12,... | collective-permute-start | bytes 1572872 | tf_op jit(solution)/shard_map/ppermute | solution.py:29
  161.5 15.4 %collective-permute-start.24 = (bf16[64,4096]{1,0:T(8,128)(2,1)S(1)}, bf16[64,4096]{1,0:T(8,128)(2,1)S(1)}, u32[]{:S(2)}, u32[]{:S(2)}) collective-permute-start(bf16[64,4096]{1,0:T(8,128)(2,1)S(1)} %add.168), channel_id=1, source_target_pairs={{0,16},{16,32},{32,48},{48,64},{64,80},{80,96},{96,112},{112,128},... | collective-permute-start | bytes 1572872 | tf_op jit(solution)/shard_map/ppermute | solution.py:507
  171.1 17.0 %collective-permute-start.29 = (bf16[64,4096]{1,0:T(8,128)(2,1)S(1)}, bf16[64,4096]{1,0:T(8,128)(2,1)S(1)}, u32[]{:S(2)}, u32[]{:S(2)}) collective-permute-start(bf16[64,4096]{1,0:T(8,128)(2,1)S(1)} %add.169), channel_id=1, source_target_pairs={{0,16},{16,32},{32,48},{48,64},{64,80},{80,96},{96,112},{112,128},... | collective-permute-start | bytes 1572872 | tf_op jit(solution)/shard_map/ppermute | solution.py:508

commit v4 on v3

--- a/solution.py
+++ b/solution.py
@@ -481,29 +481,33 @@
     pairs_other = after(pairs_other, acc)
     att_far = attend_own(q_far, acc, state, pairs, pairs_other, info[:, 5:])
 
-    p13, p11, p12b, p12a = project_out(att_far, wo, (1, 1, 2))
+    p13b, p13a, p11b, p11a, p12b, p12a = project_out(att_far, wo, (2, 2, 2))
     across_a = shift(p12a, "xh", 1)
-    up = shift(p11, "y", 1)
-    down = shift(p13, "y", -1)
+    up_a, down_a = shift(p11a, "y", 1), shift(p13a, "y", -1)
     across_b = shift(p12b, "xh", 1)
     att_near = attend_own(
-        q_near, acc_near, state_near, after(pairs, p11), pairs_other, info[:, :5]
+        q_near, acc_near, state_near, after(pairs, p11a), pairs_other, info[:, :5]
     )
-    p00, p10, p03b, p03a, p01b, p01a, p02b, p02a = project_out(att_near, wo, (1, 1, 2, 2, 2))
+    p00, p10b, p10a, p03b, p03a, p01b, p01a, p02b, p02a = project_out(
+        att_near, wo, (1, 2, 2, 2, 2)
+    )
+    p11b = after(p11b, p00)
+    from_b, onto_b = shift(p11b, "y", 1), shift(after(p13b, p00), "y", -1)
+    from_a, onto_a = up_a, down_a
     up_a, down_a = split_sum(p02a, across_a)
-    across = add(after(p10, up_a), up, down)
-    up_b, down_b = split_sum(after(p02b, across), across_b)
-    p01a = after(p01a, up_b)
+    up_b, down_b = split_sum(after(p02b, up_a), across_b)
+    over_a = add(after(p10a, up_a), from_a, onto_a)
+    over_b = add(after(p10b, over_a), from_b, onto_b)
     up_a, down_a = shift(up_a, "y", 1), shift(down_a, "y", -1)
-    across = shift(across, "xh", 1)
     up_b, down_b = shift(up_b, "y", 1), shift(down_b, "y", -1)
+    over_a, over_b = shift(over_a, "xh", 1), shift(over_b, "xh", 1)
     p01a, p03a = relay_sum(p01a, up_a, p03a, down_a)
     up_a, down_a = shift(p01a, "y", 1), shift(p03a, "y", -1)
     p01b, p03b = relay_sum(after(p01b, p01a), up_b, p03b, down_b)
     up_b, down_b = shift(p01b, "y", 1), shift(p03b, "y", -1)
     onward = [(i, (i + 1) % 16) for i in range(16)]
-    total_a = add(hidden, p00, across, up_a, down_a, start=D // 2)
-    total_b = add(after(hidden, total_a), p00, across, up_b, down_b)
+    total_a = add(hidden, p00, over_a, up_a, down_a, start=D // 2)
+    total_b = add(after(hidden, total_a), p00, over_b, up_b, down_b)
     out_a = lax.ppermute(total_a, ("xl", "z"), onward)
     out_b = lax.ppermute(total_b, ("xl", "z"), onward)
     whole = place(out_a, D // 2)

time: 190 us -> 190 us (level)
  waiting for transfers between devices: 80.8 us -> 74.4 us
  starting transfers between devices: 57.7 us -> 62.6 us
    ppermute x26 -> x29, waiting for transfers between devices: 63.2 us -> 57.1 us  [shift(): lax.ppermute(value, axis, [(i, (i + by) % size) for i in range(size)])]
    ppermute x26 -> x29, starting transfers between devices: 44 us -> 48.9 us  [shift(): lax.ppermute(value, axis, [(i, (i + by) % size) for i in range(size)])]
  transfers between devices with their start and end apart: 31 -> 34, of which waited for: 16 -> 20; matrix products, arithmetic and copies ran while one was open for 2% -> 2% of each run, Pallas kernels for 19% -> 19%
where the time goes in v4:
time: 190 us; the launch traced here: 188 us
  waiting for transfers between devices  74.4 us (39%)
  starting transfers between devices  62.6 us (33%)
  Pallas kernels  40.7 us (21%)
  local copies, waits for them, and re-layouts  8.43 us (4%)
    ppermute x29, waiting for transfers between devices, shift(): lax.ppermute(value, axis, [(i, (i + by) % size) for i in range(size)])  57.1 us
    ppermute x29, starting transfers between devices, shift(): lax.ppermute(value, axis, [(i, (i + by) % size) for i in range(size)])  48.9 us
    ppermute x1, waiting for transfers between devices, body(): out_b = lax.ppermute(total_b, ('xl', 'z'), onward)  9.37 us
    pallas_call x4, Pallas kernels, merge(): pl.pallas_call(functools.partial(merge_kernel, places), out_shape=jax.Sha...  7.61 us
    unnamed x23, local copies, waits for them, and re-layouts  7.28 us
    pallas_call x2, Pallas kernels, attend_prompt(): pl.pallas_call(prompt_kernel, out_shape=(shape, shape), in_specs=[pl.Bloc...  6.61 us
    pallas_call x2, Pallas kernels, project_queries(): pl.pallas_call(functools.partial(query_kernel, len(pieces)), out_shape=ja...  6.25 us
    pallas_call x2, Pallas kernels, attend_own(): pl.pallas_call(own_kernel, out_shape=jax.ShapeDtypeStruct((count, ROWS, 4...  6.09 us
  transfers between devices with their start and end apart: 34, of which 20 were waited for; matrix products, arithmetic and copies ran while one was open for 2% of the time, Pallas kernels for 19%

profile of v4, /device:TPU:2, one launch (start us, length us, event | category | flops | bytes accessed | tf_op | source)
XLA Modules:
  0.0 187.7 jit_solution(5976907029941608573)
XLA Ops:
  2.8 2.2 %collective-permute-start = (bf16[64,8192]{1,0:T(8,128)(2,1)S(1)}, bf16[64,8192]{1,0:T(8,128)(2,1)}, u32[]{:S(2)}, u32[]{:S(2)}) collective-permute-start(bf16[64,8192]{1,0:T(8,128)(2,1)S(1)} %norm.1.refs_0_), channel_id=1, source_target_pairs={{0,8},{8,0},{1,9},{9,1},{2,10},{10,2},{3,11},{11,3},{4,12},{12,4},... | collective-permute-start | bytes 3145736 | tf_op jit(solution)/shard_map/ppermute | solution.py:29
  5.0 1.6 collective-permute-start.2
  6.5 1.7 collective-permute-start.1
  10.8 4.2 %all-to-all-start = ((bf16[8,4,64,256]{3,2,1,0:T(8,128)(2,1)}), bf16[8,4,64,256]{3,2,1,0:T(8,128)(2,1)}, u32[]{:S(2)}, u32[]{:S(2)}) async-start(bf16[8,4,64,256]{3,2,1,0:T(8,128)(2,1)} %copy-done.2), calls=%async_computation | async-start | bytes 2097152 | tf_op jit(solution)/shard_map/all_to_all | solution.py:414
  15.7 14.7 %collective-permute-done.refs_1_ = bf16[64,8192]{1,0:T(8,128)(2,1)} collective-permute-done((bf16[64,8192]{1,0:T(8,128)(2,1)S(1)}, bf16[64,8192]{1,0:T(8,128)(2,1)}, u32[]{:S(2)}, u32[]{:S(2)}) %collective-permute-start) | collective-permute-done | bytes 1048608 | tf_op jit(solution)/shard_map/ppermute | solution.py:29
  30.9 1.5 collective-permute-done.2.refs_2_
  33.2 7.3 %collective-permute-start.5 = (bf16[32,8192]{1,0:T(8,128)(2,1)}, bf16[32,8192]{1,0:T(8,128)(2,1)}, u32[]{:S(2)}, u32[]{:S(2)}) collective-permute-start(bf16[32,8192]{1,0:T(8,128)(2,1)} %slice.20), channel_id=1, source_target_pairs={{0,2},{2,4},{4,6},{6,0},{1,3},{3,5},{5,7},{7,1},{8,10},{10,12},{12... | collective-permute-start | bytes 1572872 | tf_op jit(solution)/shard_map/ppermute | solution.py:29
  40.5 3.0 %all-to-all-done.refs_0_ = bf16[8,4,64,256]{3,2,1,0:T(8,128)(2,1)} async-done(((bf16[8,4,64,256]{3,2,1,0:T(8,128)(2,1)}), bf16[8,4,64,256]{3,2,1,0:T(8,128)(2,1)}, u32[]{:S(2)}, u32[]{:S(2)}) %all-to-all-start) | async-done | bytes 1048608 | tf_op jit(solution)/shard_map/all_to_all | solution.py:414
  43.6 2.4 %collective-permute-start.6 = (bf16[32,8192]{1,0:T(8,128)(2,1)S(1)}, bf16[32,8192]{1,0:T(8,128)(2,1)S(1)}, u32[]{:S(2)}, u32[]{:S(2)}) collective-permute-start(bf16[32,8192]{1,0:T(8,128)(2,1)S(1)} %slice.19), channel_id=1, source_target_pairs={{0,6},{2,0},{4,2},{6,4},{1,7},{3,1},{5,3},{7,5},{8,14},{10,8},{12,... | collective-permute-start | bytes 1572872 | tf_op jit(solution)/shard_map/ppermute | solution.py:29
  45.9 3.2 %collective-permute-start.9 = (bf16[64,8192]{1,0:T(8,128)(2,1)}, bf16[64,8192]{1,0:T(8,128)(2,1)S(1)}, u32[]{:S(2)}, u32[]{:S(2)}) collective-permute-start(bf16[64,8192]{1,0:T(8,128)(2,1)} %collective-permute-done.refs_1_), channel_id=1, source_target_pairs={{0,6},{2,0},{4,2},{6,4},{1,7},{3,1},{5,3},{7,5},{8,14},{10,8},{12,... | collective-permute-start | bytes 3145736 | tf_op jit(solution)/shard_map/ppermute | solution.py:29
  49.2 2.2 %copy-done.3 = bf16[1,8192,256]{2,1,0:T(8,128)(2,1)S(1)} copy-done((bf16[1,8192,256]{2,1,0:T(8,128)(2,1)S(1)}, bf16[1,8192,256]{2,1,0:T(8,128)(2,1)}, u32[]{:S(2)}) %copy-start.3) | copy-done | bytes 4194328
  51.4 2.5 %merge.5.refs_5_.refs_3_ = bf16[8192,512]{1,0:T(8,128)(2,1)S(1)} custom-call(bf16[8192,256]{1,0:T(8,128)(2,1)S(1)} %bitcast.25, bf16[8192,256]{1,0:T(8,128)(2,1)} %collective-permute-done.3.refs_1_), custom_call_target="tpu_custom_call" | custom-call | flops 1 | bytes 1 | tf_op jit(solution)/shard_map/merge/pallas_call | solution.py:76
  56.4 2.1 %collective-permute-done.6 = bf16[32,8192]{1,0:T(8,128)(2,1)S(1)} collective-permute-done((bf16[32,8192]{1,0:T(8,128)(2,1)S(1)}, bf16[32,8192]{1,0:T(8,128)(2,1)S(1)}, u32[]{:S(2)}, u32[]{:S(2)}) %collective-permute-start.6) | collective-permute-done | bytes 524320 | tf_op jit(solution)/shard_map/ppermute | solution.py:29
  58.5 1.7 collective-permute-start.10
  60.2 2.9 %pairs.2 = bf16[5,64,128]{2,1,0:T(8,128)(2,1)S(1)} custom-call(bf16[64,8192]{1,0:T(8,128)(2,1)S(1)} %norm.1.refs_0_, bf16[64,8192]{1,0:T(8,128)(2,1)} %collective-permute-done.refs_1_, bf16[64,8192]{1,0:T(8,128)(2,1)S(1)} %collective-permute-done.2.refs_2_, bf16[64,8192]{1,0:T(8,128)(2,1)S(1)} %collective-permute-done.1.refs_3_, ...), custom_call_target="tpu_custom_call" | custom-call | flops 1 | bytes 1 | tf_op jit(solution)/shard_map/pairs/pallas_call | solution.py:167
  63.1 4.3 %queries.2.q_ref = bf16[5,256,128]{2,1,0:T(8,128)(2,1)S(1)} custom-call(bf16[64,8192]{1,0:T(8,128)(2,1)S(1)} %norm.1.refs_0_, bf16[64,8192]{1,0:T(8,128)(2,1)} %collective-permute-done.refs_1_, bf16[64,8192]{1,0:T(8,128)(2,1)S(1)} %collective-permute-done.2.refs_2_, bf16[64,8192]{1,0:T(8,128)(2,1)S(1)} %collective-permute-done.1.refs_3_, ...), custom_call_target="tpu_custom_call" | custom-call | flops 1 | bytes 1 | tf_op jit(solution)/shard_map/queries/pallas_call | solution.py:134
  68.7 4.0 %attend_prompt.2 = (f32[5,256,128]{2,1,0:T(8,128)S(1)}, f32[5,256,128]{2,1,0:T(8,128)S(1)}) custom-call(s32[5]{0:T(128)S(1)} %bitcast.35, bf16[5,256,128]{2,1,0:T(8,128)(2,1)S(1)} %queries.2.q_ref, bf16[4,16,64,256]{3,2,1,0:T(8,128)(2,1)S(1)} %merge.6.cache_ref), custom_call_target="tpu_custom_call" | custom-call | flops 1 | bytes 1 | tf_op jit(solution)/shard_map/attend_prompt/pallas_call | solution.py:215
  72.7 3.7 %collective-permute-done.8.refs_0_ = bf16[64,8192]{1,0:T(8,128)(2,1)S(1)} collective-permute-done((bf16[64,8192]{1,0:T(8,128)(2,1)}, bf16[64,8192]{1,0:T(8,128)(2,1)S(1)}, u32[]{:S(2)}, u32[]{:S(2)}) %collective-permute-start.8) | collective-permute-done | bytes 1048608 | tf_op jit(solution)/shard_map/ppermute | solution.py:29
  76.5 2.5 %collective-permute-done.9.refs_1_ = bf16[64,8192]{1,0:T(8,128)(2,1)S(1)} collective-permute-done((bf16[64,8192]{1,0:T(8,128)(2,1)}, bf16[64,8192]{1,0:T(8,128)(2,1)S(1)}, u32[]{:S(2)}, u32[]{:S(2)}) %collective-permute-start.9) | collective-permute-done | bytes 1048608 | tf_op jit(solution)/shard_map/ppermute | solution.py:29
  78.9 4.9 %collective-permute-done.10.refs_2_ = bf16[64,8192]{1,0:T(8,128)(2,1)S(1)} collective-permute-done((bf16[64,8192]{1,0:T(8,128)(2,1)S(1)}, bf16[64,8192]{1,0:T(8,128)(2,1)S(1)}, u32[]{:S(2)}, u32[]{:S(2)}) %collective-permute-start.10) | collective-permute-done | bytes 1048608 | tf_op jit(solution)/shard_map/ppermute | solution.py:29
  85.8 4.7 %collective-permute-start.13 = (bf16[8,64,128]{2,1,0:T(8,128)(2,1)S(1)}, bf16[8,64,128]{2,1,0:T(8,128)(2,1)S(1)}, u32[]{:S(2)}, u32[]{:S(2)}) collective-permute-start(bf16[8,64,128]{2,1,0:T(8,128)(2,1)S(1)} %pad_maximum_fusion.1), channel_id=1, source_target_pairs={{0,2},{2,6},{4,10},{6,14},{8,0},{10,4},{12,8},{14,12},{1,3},{3,7},... | collective-permute-start | bytes 393224 | tf_op jit(solution)/shard_map/ppermute | solution.py:474
  90.4 1.9 %queries.3.q_ref = bf16[3,256,128]{2,1,0:T(8,128)(2,1)S(1)} custom-call(bf16[64,8192]{1,0:T(8,128)(2,1)S(1)} %collective-permute-done.8.refs_0_, bf16[64,8192]{1,0:T(8,128)(2,1)S(1)} %collective-permute-done.9.refs_1_, bf16[64,8192]{1,0:T(8,128)(2,1)S(1)} %collective-permute-done.10.refs_2_, bf16[8192,512]{1,0:T(8,128)(2,1)S(1)} %merge.5.refs_5_.refs_3_, ...), custom_call_target="tpu_custom_call" | custom-call | flops 1 | bytes 1 | tf_op jit(solution)/shard_map/queries/pallas_call | solution.py:134
  92.4 2.5 %merge.7.w_ref = bf16[512,8192]{1,0:T(8,128)(2,1)S(1)} custom-call(bf16[256,8192]{1,0:T(8,128)(2,1)S(1)} %bitcast.27, bf16[256,8192]{1,0:T(8,128)(2,1)} %collective-permute-done.12.refs_1_), custom_call_target="tpu_custom_call" | custom-call | flops 1 | bytes 1 | tf_op jit(solution)/shard_map/merge/pallas_call | solution.py:76
  95.5 2.6 %attend_prompt.3 = (f32[3,256,128]{2,1,0:T(8,128)S(1)}, f32[3,256,128]{2,1,0:T(8,128)S(1)}) custom-call(s32[3]{0:T(128)S(1)} %slice.23.prompt_ref, bf16[3,256,128]{2,1,0:T(8,128)(2,1)S(1)} %queries.3.q_ref, bf16[4,16,64,256]{3,2,1,0:T(8,128)(2,1)S(1)} %merge.6.cache_ref), custom_call_target="tpu_custom_call" | custom-call | flops 1 | bytes 1 | tf_op jit(solution)/shard_map/attend_prompt/pallas_call | solution.py:215
  98.1 2.4 %attend_own.2 = bf16[3,64,512]{2,1,0:T(8,128)(2,1)S(1)} custom-call(s32[5,3]{1,0:T(8,128)S(1)} %slice.22.info_ref, bf16[3,256,128]{2,1,0:T(8,128)(2,1)S(1)} %queries.3.q_ref, f32[3,256,128]{2,1,0:T(8,128)S(1)} %get-tuple-element.67.acc_ref, f32[3,256,128]{2,1,0:T(8,128)S(1)} %get-tuple-element.68.state_ref, ...), custom_call_target="tpu_custom_call" | custom-call | flops 1 | bytes 1 | tf_op jit(solution)/shard_map/attend_own/pallas_call | solution.py:262
  100.5 2.4 %project_out.2 = (bf16[64,4096]{1,0:T(8,128)(2,1)S(1)}, bf16[64,4096]{1,0:T(8,128)(2,1)S(1)}, bf16[64,4096]{1,0:T(8,128)(2,1)S(1)}, bf16[64,4096]{1,0:T(8,128)(2...) custom-call(bf16[192,512]{1,0:T(8,128)(2,1)S(1)} %bitcast.33, bf16[512,8192]{1,0:T(8,128)(2,1)S(1)} %merge.7.w_ref), custom_call_target="tpu_custom_call" | custom-call | flops 1 | bytes 1 | tf_op jit(solution)/shard_map/project_out/pallas_call | solution.py:294
  102.9 3.7 %collective-permute-start.15 = (bf16[64,4096]{1,0:T(8,128)(2,1)S(1)}, bf16[64,4096]{1,0:T(8,128)(2,1)S(1)}, u32[]{:S(2)}, u32[]{:S(2)}) collective-permute-start(bf16[64,4096]{1,0:T(8,128)(2,1)S(1)} %get-tuple-element.75), channel_id=1, source_target_pairs={{0,8},{8,0},{1,9},{9,1},{2,10},{10,2},{3,11},{11,3},{4,12},{12,4},... | collective-permute-start | bytes 1572872 | tf_op jit(solution)/shard_map/ppermute | solution.py:29
  106.6 1.4 collective-permute-start.16
  108.0 1.8 collective-permute-start.17
  110.6 3.7 %attend_own.3 = bf16[5,64,512]{2,1,0:T(8,128)(2,1)S(1)} custom-call(s32[5,5]{1,0:T(8,128)S(1)} %bitcast.34, bf16[5,256,128]{2,1,0:T(8,128)(2,1)S(1)} %queries.2.q_ref, f32[5,256,128]{2,1,0:T(8,128)S(1)} %get-tuple-element.61.acc_ref, f32[5,256,128]{2,1,0:T(8,128)S(1)} %get-tuple-element.62.state_ref, bf16[2,8,64,128]{3,2,1,0:T(8,128)(2,1)S(1)} %pad_maximum_fusion.own_ref, ...), custom_call_target="tpu_custom_call" | custom-call | flops 1 | bytes 1 | tf_op jit(solution)/shard_map/attend_own/pallas_call | solution.py:262
  114.2 3.4 %project_out.3 = (bf16[64,8192]{1,0:T(8,128)(2,1)S(1)}, bf16[64,4096]{1,0:T(8,128)(2,1)S(1)}, bf16[64,4096]{1,0:T(8,128)(2,1)S(1)}, bf16[64,4096]{1,0:T(8,128)(2...) custom-call(bf16[320,512]{1,0:T(8,128)(2,1)S(1)} %bitcast.30, ...), custom_call_target="tpu_custom_call" | custom-call | flops 1 | bytes 1 | tf_op jit(solution)/shard_map/project_out/pallas_call | solution.py:294
  117.6 2.3 %collective-permute-start.25 = (bf16[64,4096]{1,0:T(8,128)(2,1)S(1)}, bf16[64,4096]{1,0:T(8,128)(2,1)S(1)}, u32[]{:S(2)}, u32[]{:S(2)}) collective-permute-start(bf16[64,4096]{1,0:T(8,128)(2,1)S(1)} %get-tuple-element.90), channel_id=1, source_target_pairs={{0,6},{2,0},{4,2},{6,4},{1,7},{3,1},{5,3},{7,5},{8,14},{10,8},{12,... | collective-permute-start | bytes 1572872 | tf_op jit(solution)/shard_map/ppermute | solution.py:29
  123.0 1.7 collective-permute-start.18
  125.4 5.3 %collective-permute-done.27.b_ref = bf16[64,4096]{1,0:T(8,128)(2,1)S(1)} collective-permute-done((bf16[64,4096]{1,0:T(8,128)(2,1)S(1)}, bf16[64,4096]{1,0:T(8,128)(2,1)S(1)}, u32[]{:S(2)}, u32[]{:S(2)}) %collective-permute-start.27) | collective-permute-done | bytes 524320 | tf_op jit(solution)/shard_map/ppermute | solution.py:29
  130.6 3.8 %collective-permute-start.20 = (bf16[64,2048]{1,0:T(8,128)(2,1)S(1)}, bf16[64,2048]{1,0:T(8,128)(2,1)S(1)}, u32[]{:S(2)}, u32[]{:S(2)}) collective-permute-start(bf16[64,2048]{1,0:T(8,128)(2,1)S(1)} %get-tuple-element.81), channel_id=1, source_target_pairs={{0,6},{2,0},{4,2},{6,4},{1,7},{3,1},{5,3},{7,5},{8,14},{10,8},{12,... | collective-permute-start | bytes 786440 | tf_op jit(solution)/shard_map/ppermute | solution.py:29
  134.7 1.4 collective-permute-done.24.refs_1_
  136.1 2.0 %collective-permute-start.29 = (bf16[64,2048]{1,0:T(8,128)(2,1)S(1)}, bf16[64,2048]{1,0:T(8,128)(2,1)S(1)}, u32[]{:S(2)}, u32[]{:S(2)}) collective-permute-start(bf16[64,2048]{1,0:T(8,128)(2,1)S(1)} %get-tuple-element.98), channel_id=1, source_target_pairs={{0,6},{2,0},{4,2},{6,4},{1,7},{3,1},{5,3},{7,5},{8,14},{10,8},{12,... | collective-permute-start | bytes 786440 | tf_op jit(solution)/shard_map/ppermute | solution.py:29
  138.3 3.4 %collective-permute-done.19.up_ref = bf16[64,2048]{1,0:T(8,128)(2,1)S(1)} collective-permute-done((bf16[64,2048]{1,0:T(8,128)(2,1)S(1)}, bf16[64,2048]{1,0:T(8,128)(2,1)S(1)}, u32[]{:S(2)}, u32[]{:S(2)}) %collective-permute-start.19) | collective-permute-done | bytes 262176 | tf_op jit(solution)/shard_map/ppermute | solution.py:29
  141.7 2.9 %collective-permute-start.26 = (bf16[64,4096]{1,0:T(8,128)(2,1)S(1)}, bf16[64,4096]{1,0:T(8,128)(2,1)S(1)}, u32[]{:S(2)}, u32[]{:S(2)}) collective-permute-start(bf16[64,4096]{1,0:T(8,128)(2,1)S(1)} %add.170), channel_id=1, source_target_pairs={{0,8},{8,0},{1,9},{9,1},{2,10},{10,2},{3,11},{11,3},{4,12},{12,4},... | collective-permute-start | bytes 1572872 | tf_op jit(solution)/shard_map/ppermute | solution.py:29
  145.0 1.8 collective-permute-done.28.up_ref
  146.7 2.6 %collective-permute-start.22 = (bf16[64,4096]{1,0:T(8,128)(2,1)S(1)}, bf16[64,4096]{1,0:T(8,128)(2,1)S(1)}, u32[]{:S(2)}, u32[]{:S(2)}) collective-permute-start(bf16[64,4096]{1,0:T(8,128)(2,1)S(1)} %get-tuple-element.83), channel_id=1, source_target_pairs={{0,6},{2,0},{4,2},{6,4},{1,7},{3,1},{5,3},{7,5},{8,14},{10,8},{12,... | collective-permute-start | bytes 1572872 | tf_op jit(solution)/shard_map/ppermute | solution.py:29
  149.6 3.2 %collective-permute-start.31 = (bf16[64,4096]{1,0:T(8,128)(2,1)S(1)}, bf16[64,4096]{1,0:T(8,128)(2,1)S(1)}, u32[]{:S(2)}, u32[]{:S(2)}) collective-permute-start(bf16[64,4096]{1,0:T(8,128)(2,1)S(1)} %get-tuple-element.100), channel_id=1, source_target_pairs={{0,6},{2,0},{4,2},{6,4},{1,7},{3,1},{5,3},{7,5},{8,14},{10,8},{12,... | collective-permute-start | bytes 1572872 | tf_op jit(solution)/shard_map/ppermute | solution.py:29
  152.8 8.0 %collective-permute-done.21.refs_3_ = bf16[64,4096]{1,0:T(8,128)(2,1)S(1)} collective-permute-done((bf16[64,4096]{1,0:T(8,128)(2,1)S(1)}, bf16[64,4096]{1,0:T(8,128)(2,1)S(1)}, u32[]{:S(2)}, u32[]{:S(2)}) %collective-permute-start.21) | collective-permute-done | bytes 524320 | tf_op jit(solution)/shard_map/ppermute | solution.py:29
  162.0 2.0 %collective-permute-start.23 = (bf16[64,4096]{1,0:T(8,128)(2,1)S(1)}, bf16[64,4096]{1,0:T(8,128)(2,1)S(1)}, u32[]{:S(2)}, u32[]{:S(2)}) collective-permute-start(bf16[64,4096]{1,0:T(8,128)(2,1)S(1)} %add.169), channel_id=1, source_target_pairs={{0,16},{16,32},{32,48},{48,64},{64,80},{80,96},{96,112},{112,128},... | collective-permute-start | bytes 1572872 | tf_op jit(solution)/shard_map/ppermute | solution.py:511
  164.1 4.3 %collective-permute-done.30.refs_3_ = bf16[64,4096]{1,0:T(8,128)(2,1)S(1)} collective-permute-done((bf16[64,4096]{1,0:T(8,128)(2,1)S(1)}, bf16[64,4096]{1,0:T(8,128)(2,1)S(1)}, u32[]{:S(2)}, u32[]{:S(2)}) %collective-permute-start.30) | collective-permute-done | bytes 524320 | tf_op jit(solution)/shard_map/ppermute | solution.py:29
  170.0 2.0 %collective-permute-start.32 = (bf16[64,4096]{1,0:T(8,128)(2,1)S(1)}, bf16[64,4096]{1,0:T(8,128)(2,1)S(1)}, u32[]{:S(2)}, u32[]{:S(2)}) collective-permute-start(bf16[64,4096]{1,0:T(8,128)(2,1)S(1)} %add.171), channel_id=1, source_target_pairs={{0,16},{16,32},{32,48},{48,64},{64,80},{80,96},{96,112},{112,128},... | collective-permute-start | bytes 1572872 | tf_op jit(solution)/shard_map/ppermute | solution.py:512
  172.0 4.5 %collective-permute-done.23.refs_0_ = bf16[64,4096]{1,0:T(8,128)(2,1)S(1)} collective-permute-done((bf16[64,4096]{1,0:T(8,128)(2,1)S(1)}, bf16[64,4096]{1,0:T(8,128)(2,1)S(1)}, u32[]{:S(2)}, u32[]{:S(2)}) %collective-permute-start.23) | collective-permute-done | bytes 524320 | tf_op jit(solution)/shard_map/ppermute | solution.py:511
  177.3 9.4 %collective-permute-done.32.refs_1_ = bf16[64,4096]{1,0:T(8,128)(2,1)S(1)} collective-permute-done((bf16[64,4096]{1,0:T(8,128)(2,1)S(1)}, bf16[64,4096]{1,0:T(8,128)(2,1)S(1)}, u32[]{:S(2)}, u32[]{:S(2)}) %collective-permute-start.32) | collective-permute-done | bytes 524320 | tf_op jit(solution)/shard_map/ppermute | solution.py:512
  (88 shorter events, 23.3 us)
Async XLA Ops:
  0.0 15.5 %copy-start.10 = (s32[8]{0:T(128)S(1)}, s32[8]{0:T(128)}, u32[]{:S(2)}) copy-start(s32[8]{0:T(128)} %constant.114.clone) | copy-start | bytes 100
  0.0 15.2 %copy-start.9 = (s32[8]{0:T(128)S(1)}, s32[8]{0:T(128)}, u32[]{:S(2)}) copy-start(s32[8]{0:T(128)} %param.15) | copy-start | bytes 100
  0.0 15.2 %copy-start.8 = (s32[8]{0:T(128)S(1)}, s32[8]{0:T(128)}, u32[]{:S(2)}) copy-start(s32[8]{0:T(128)} %param.16) | copy-start | bytes 100
  0.0 32.4 %collective-permute-start.3 = (bf16[8192,256]{1,0:T(8,128)(2,1)}, bf16[8192,256]{1,0:T(8,128)(2,1)}, u32[]{:S(2)}, u32[]{:S(2)}) collective-permute-start(bf16[8192,256]{1,0:T(8,128)(2,1)} %bitcast.24), channel_id=1, source_target_pairs={{0,1},{1,0},{2,3},{3,2},{4,5},{5,4},{6,7},{7,6},{8,9},{9,8},{10,11... | collective-permute-start | bytes 12582920 | tf_op jit(solution)/shard_map/ppermute | solution.py:29
  0.1 1.2 copy-start
  1.3 0.8 copy-start.7
  2.8 27.7 %collective-permute-start = (bf16[64,8192]{1,0:T(8,128)(2,1)S(1)}, bf16[64,8192]{1,0:T(8,128)(2,1)}, u32[]{:S(2)}, u32[]{:S(2)}) collective-permute-start(bf16[64,8192]{1,0:T(8,128)(2,1)S(1)} %norm.1.refs_0_), channel_id=1, source_target_pairs={{0,8},{8,0},{1,9},{9,1},{2,10},{10,2},{3,11},{11,3},{4,12},{12,4},... | collective-permute-start | bytes 3145736 | tf_op jit(solution)/shard_map/ppermute | solution.py:29
  5.0 27.4 %collective-permute-start.2 = (bf16[64,8192]{1,0:T(8,128)(2,1)S(1)}, bf16[64,8192]{1,0:T(8,128)(2,1)S(1)}, u32[]{:S(2)}, u32[]{:S(2)}) collective-permute-start(bf16[64,8192]{1,0:T(8,128)(2,1)S(1)} %norm.1.refs_0_), channel_id=1, source_target_pairs={{0,2},{2,4},{4,6},{6,0},{1,3},{3,5},{5,7},{7,1},{8,10},{10,12},{12... | collective-permute-start | bytes 3145736 | tf_op jit(solution)/shard_map/ppermute | solution.py:29
  6.5 37.0 %collective-permute-start.1 = (bf16[64,8192]{1,0:T(8,128)(2,1)S(1)}, bf16[64,8192]{1,0:T(8,128)(2,1)S(1)}, u32[]{:S(2)}, u32[]{:S(2)}) collective-permute-start(bf16[64,8192]{1,0:T(8,128)(2,1)S(1)} %norm.1.refs_0_), channel_id=1, source_target_pairs={{0,6},{2,0},{4,2},{6,4},{1,7},{3,1},{5,3},{7,5},{8,14},{10,8},{12,... | collective-permute-start | bytes 3145736 | tf_op jit(solution)/shard_map/ppermute | solution.py:29
  8.2 24.2 %collective-permute-start.4 = (bf16[64,8192]{1,0:T(8,128)(2,1)}, bf16[64,8192]{1,0:T(8,128)(2,1)}, u32[]{:S(2)}, u32[]{:S(2)}) collective-permute-start(bf16[64,8192]{1,0:T(8,128)(2,1)} %bitcast.31), channel_id=1, source_target_pairs={{0,1},{1,0},{2,3},{3,2},{4,5},{5,4},{6,7},{7,6},{8,9},{9,8},{10,11... | collective-permute-start | bytes 3145736 | tf_op jit(solution)/shard_map/ppermute | solution.py:29
  8.2 1.0 copy-start.5
  9.8 1.0 copy-start.2
  10.8 32.7 %all-to-all-start = ((bf16[8,4,64,256]{3,2,1,0:T(8,128)(2,1)}), bf16[8,4,64,256]{3,2,1,0:T(8,128)(2,1)}, u32[]{:S(2)}, u32[]{:S(2)}) async-start(bf16[8,4,64,256]{3,2,1,0:T(8,128)(2,1)} %copy-done.2), calls=%async_computation | async-start | bytes 2097152 | tf_op jit(solution)/shard_map/all_to_all | solution.py:414
  30.4 62.0 %collective-permute-start.12 = (bf16[256,8192]{1,0:T(8,128)(2,1)}, bf16[256,8192]{1,0:T(8,128)(2,1)}, u32[]{:S(2)}, u32[]{:S(2)}) collective-permute-start(bf16[256,8192]{1,0:T(8,128)(2,1)} %bitcast.26), channel_id=1, source_target_pairs={{0,1},{1,0},{2,3},{3,2},{4,5},{5,4},{6,7},{7,6},{8,9},{9,8},{10,11... | collective-permute-start | bytes 12582920 | tf_op jit(solution)/shard_map/ppermute | solution.py:29
  33.2 22.1 %collective-permute-start.5 = (bf16[32,8192]{1,0:T(8,128)(2,1)}, bf16[32,8192]{1,0:T(8,128)(2,1)}, u32[]{:S(2)}, u32[]{:S(2)}) collective-permute-start(bf16[32,8192]{1,0:T(8,128)(2,1)} %slice.20), channel_id=1, source_target_pairs={{0,2},{2,4},{4,6},{6,0},{1,3},{3,5},{5,7},{7,1},{8,10},{10,12},{12... | collective-permute-start | bytes 1572872 | tf_op jit(solution)/shard_map/ppermute | solution.py:29
  43.5 10.4 %copy-start.6 = (bf16[1,8192,64]{1,2,0:T(8,128)(2,1)S(1)}, bf16[1,8192,64]{1,2,0:T(8,128)(2,1)}, u32[]{:S(2)}) copy-start(bf16[1,8192,64]{1,2,0:T(8,128)(2,1)} %param.12) | copy-start | bytes 3145732
  43.6 14.9 %collective-permute-start.6 = (bf16[32,8192]{1,0:T(8,128)(2,1)S(1)}, bf16[32,8192]{1,0:T(8,128)(2,1)S(1)}, u32[]{:S(2)}, u32[]{:S(2)}) collective-permute-start(bf16[32,8192]{1,0:T(8,128)(2,1)S(1)} %slice.19), channel_id=1, source_target_pairs={{0,6},{2,0},{4,2},{6,4},{1,7},{3,1},{5,3},{7,5},{8,14},{10,8},{12,... | collective-permute-start | bytes 1572872 | tf_op jit(solution)/shard_map/ppermute | solution.py:29
  45.9 30.5 %collective-permute-start.8 = (bf16[64,8192]{1,0:T(8,128)(2,1)}, bf16[64,8192]{1,0:T(8,128)(2,1)S(1)}, u32[]{:S(2)}, u32[]{:S(2)}) collective-permute-start(bf16[64,8192]{1,0:T(8,128)(2,1)} %collective-permute-done.refs_1_), channel_id=1, source_target_pairs={{0,2},{2,4},{4,6},{6,0},{1,3},{3,5},{5,7},{7,1},{8,10},{10,12},{12... | collective-permute-start | bytes 3145736 | tf_op jit(solution)/shard_map/ppermute | solution.py:29
  45.9 33.0 %collective-permute-start.9 = (bf16[64,8192]{1,0:T(8,128)(2,1)}, bf16[64,8192]{1,0:T(8,128)(2,1)S(1)}, u32[]{:S(2)}, u32[]{:S(2)}) collective-permute-start(bf16[64,8192]{1,0:T(8,128)(2,1)} %collective-permute-done.refs_1_), channel_id=1, source_target_pairs={{0,6},{2,0},{4,2},{6,4},{1,7},{3,1},{5,3},{7,5},{8,14},{10,8},{12,... | collective-permute-start | bytes 3145736 | tf_op jit(solution)/shard_map/ppermute | solution.py:29
  49.2 2.2 %copy-start.3 = (bf16[1,8192,256]{2,1,0:T(8,128)(2,1)S(1)}, bf16[1,8192,256]{2,1,0:T(8,128)(2,1)}, u32[]{:S(2)}) copy-start(bf16[1,8192,256]{2,1,0:T(8,128)(2,1)} %param.11) | copy-start | bytes 12582916
  55.3 12.2 %collective-permute-start.7 = (bf16[8,4,64,256]{3,2,1,0:T(8,128)(2,1)}, bf16[8,4,64,256]{3,2,1,0:T(8,128)(2,1)S(1)}, u32[]{:S(2)}, u32[]{:S(2)}) collective-permute-start(bf16[8,4,64,256]{3,2,1,0:T(8,128)(2,1)} %all-to-all-done.refs_0_), channel_id=1, source_target_pairs={{0,1},{1,0},{2,3},{3,2},{4,5},{5,4},{6,7},{7,6},{8,9},{9,8},{10,11... | collective-permute-start | bytes 3145736 | tf_op jit(solution)/shard_map/ppermute | solution.py:29
  58.5 25.3 %collective-permute-start.10 = (bf16[64,8192]{1,0:T(8,128)(2,1)S(1)}, bf16[64,8192]{1,0:T(8,128)(2,1)S(1)}, u32[]{:S(2)}, u32[]{:S(2)}) collective-permute-start(bf16[64,8192]{1,0:T(8,128)(2,1)S(1)} %constant_dynamic-update-slice_fusion.refs_4_), channel_id=1, source_target_pairs={{0,8},{8,0},{1,9},{9,1},{2,10},{10,2},{3,11},{11,3},{4,12},{12,4},... | collective-permute-start | bytes 3145736 | tf_op jit(solution)/shard_map/ppermute | solution.py:29
  85.0 7.4 %copy-start.4 = (bf16[1,256,8192]{2,1,0:T(8,128)(2,1)S(1)}, bf16[1,256,8192]{2,1,0:T(8,128)(2,1)}, u32[]{:S(2)}) copy-start(bf16[1,256,8192]{2,1,0:T(8,128)(2,1)} %param.13) | copy-start | bytes 12582916
  85.0 9.9 %collective-permute-start.11 = (bf16[8,64,128]{2,1,0:T(8,128)(2,1)S(1)}, bf16[8,64,128]{2,1,0:T(8,128)(2,1)S(1)}, u32[]{:S(2)}, u32[]{:S(2)}) collective-permute-start(bf16[8,64,128]{2,1,0:T(8,128)(2,1)S(1)} %pad_maximum_fusion.1), channel_id=1, source_target_pairs={{0,0},{2,4},{4,8},{6,12},{8,2},{10,6},{12,10},{14,14},{1,1},{3,5},... | collective-permute-start | bytes 393224 | tf_op jit(solution)/shard_map/ppermute | solution.py:474
  85.8 9.4 %collective-permute-start.13 = (bf16[8,64,128]{2,1,0:T(8,128)(2,1)S(1)}, bf16[8,64,128]{2,1,0:T(8,128)(2,1)S(1)}, u32[]{:S(2)}, u32[]{:S(2)}) collective-permute-start(bf16[8,64,128]{2,1,0:T(8,128)(2,1)S(1)} %pad_maximum_fusion.1), channel_id=1, source_target_pairs={{0,2},{2,6},{4,10},{6,14},{8,0},{10,4},{12,8},{14,12},{1,3},{3,7},... | collective-permute-start | bytes 393224 | tf_op jit(solution)/shard_map/ppermute | solution.py:474
  95.2 2.9 %collective-permute-start.14 = (bf16[2,8,64,128]{3,2,1,0:T(8,128)(2,1)S(1)}, bf16[2,8,64,128]{3,2,1,0:T(8,128)(2,1)S(1)}, u32[]{:S(2)}, u32[]{:S(2)}) collective-permute-start(bf16[2,8,64,128]{3,2,1,0:T(8,128)(2,1)S(1)} %pad_maximum_fusion.own_ref), channel_id=1, source_target_pairs={{0,1},{1,0},{2,3},{3,2},{4,5},{5,4},{6,7},{7,6},{8,9},{9,8},{10,11... | collective-permute-start | bytes 786440 | tf_op jit(solution)/shard_map/ppermute | solution.py:29
  102.9 17.0 %collective-permute-start.15 = (bf16[64,4096]{1,0:T(8,128)(2,1)S(1)}, bf16[64,4096]{1,0:T(8,128)(2,1)S(1)}, u32[]{:S(2)}, u32[]{:S(2)}) collective-permute-start(bf16[64,4096]{1,0:T(8,128)(2,1)S(1)} %get-tuple-element.75), channel_id=1, source_target_pairs={{0,8},{8,0},{1,9},{9,1},{2,10},{10,2},{3,11},{11,3},{4,12},{12,4},... | collective-permute-start | bytes 1572872 | tf_op jit(solution)/shard_map/ppermute | solution.py:29
  106.6 15.3 %collective-permute-start.16 = (bf16[64,4096]{1,0:T(8,128)(2,1)S(1)}, bf16[64,4096]{1,0:T(8,128)(2,1)S(1)}, u32[]{:S(2)}, u32[]{:S(2)}) collective-permute-start(bf16[64,4096]{1,0:T(8,128)(2,1)S(1)} %get-tuple-element.70), channel_id=1, source_target_pairs={{0,2},{2,4},{4,6},{6,0},{1,3},{3,5},{5,7},{7,1},{8,10},{10,12},{12... | collective-permute-start | bytes 1572872 | tf_op jit(solution)/shard_map/ppermute | solution.py:29
  108.0 14.8 %collective-permute-start.17 = (bf16[64,4096]{1,0:T(8,128)(2,1)S(1)}, bf16[64,4096]{1,0:T(8,128)(2,1)S(1)}, u32[]{:S(2)}, u32[]{:S(2)}) collective-permute-start(bf16[64,4096]{1,0:T(8,128)(2,1)S(1)} %get-tuple-element.78), channel_id=1, source_target_pairs={{0,6},{2,0},{4,2},{6,4},{1,7},{3,1},{5,3},{7,5},{8,14},{10,8},{12,... | collective-permute-start | bytes 1572872 | tf_op jit(solution)/shard_map/ppermute | solution.py:29
  109.9 20.8 %collective-permute-start.27 = (bf16[64,4096]{1,0:T(8,128)(2,1)S(1)}, bf16[64,4096]{1,0:T(8,128)(2,1)S(1)}, u32[]{:S(2)}, u32[]{:S(2)}) collective-permute-start(bf16[64,4096]{1,0:T(8,128)(2,1)S(1)} %get-tuple-element.95), channel_id=1, source_target_pairs={{0,8},{8,0},{1,9},{9,1},{2,10},{10,2},{3,11},{11,3},{4,12},{12,4},... | collective-permute-start | bytes 1572872 | tf_op jit(solution)/shard_map/ppermute | solution.py:29
  117.6 17.0 %collective-permute-start.25 = (bf16[64,4096]{1,0:T(8,128)(2,1)S(1)}, bf16[64,4096]{1,0:T(8,128)(2,1)S(1)}, u32[]{:S(2)}, u32[]{:S(2)}) collective-permute-start(bf16[64,4096]{1,0:T(8,128)(2,1)S(1)} %get-tuple-element.90), channel_id=1, source_target_pairs={{0,6},{2,0},{4,2},{6,4},{1,7},{3,1},{5,3},{7,5},{8,14},{10,8},{12,... | collective-permute-start | bytes 1572872 | tf_op jit(solution)/shard_map/ppermute | solution.py:29
  119.9 16.1 %collective-permute-start.24 = (bf16[64,4096]{1,0:T(8,128)(2,1)S(1)}, bf16[64,4096]{1,0:T(8,128)(2,1)S(1)}, u32[]{:S(2)}, u32[]{:S(2)}) collective-permute-start(bf16[64,4096]{1,0:T(8,128)(2,1)S(1)} %get-tuple-element.88), channel_id=1, source_target_pairs={{0,2},{2,4},{4,6},{6,0},{1,3},{3,5},{5,7},{7,1},{8,10},{10,12},{12... | collective-permute-start | bytes 1572872 | tf_op jit(solution)/shard_map/ppermute | solution.py:29
  121.4 40.3 %copy-start.1 = (bf16[64,8192]{1,0:T(8,128)(2,1)S(1)}, bf16[64,8192]{1,0:T(8,128)(2,1)}, u32[]{:S(2)}) copy-start(bf16[64,8192]{1,0:T(8,128)(2,1)} %refs_0_.2) | copy-start | bytes 3145732
  123.0 26.5 %collective-permute-start.18 = (bf16[64,4096]{1,0:T(8,128)(2,1)S(1)}, bf16[64,4096]{1,0:T(8,128)(2,1)S(1)}, u32[]{:S(2)}, u32[]{:S(2)}) collective-permute-start(bf16[64,4096]{1,0:T(8,128)(2,1)S(1)} %add.168), channel_id=1, source_target_pairs={{0,8},{8,0},{1,9},{9,1},{2,10},{10,2},{3,11},{11,3},{4,12},{12,4},... | collective-permute-start | bytes 1572872 | tf_op jit(solution)/shard_map/ppermute | solution.py:29
  124.7 17.0 %collective-permute-start.19 = (bf16[64,2048]{1,0:T(8,128)(2,1)S(1)}, bf16[64,2048]{1,0:T(8,128)(2,1)S(1)}, u32[]{:S(2)}, u32[]{:S(2)}) collective-permute-start(bf16[64,2048]{1,0:T(8,128)(2,1)S(1)} %get-tuple-element.76), channel_id=1, source_target_pairs={{0,2},{2,4},{4,6},{6,0},{1,3},{3,5},{5,7},{7,1},{8,10},{10,12},{12... | collective-permute-start | bytes 786440 | tf_op jit(solution)/shard_map/ppermute | solution.py:29
  130.6 13.9 %collective-permute-start.20 = (bf16[64,2048]{1,0:T(8,128)(2,1)S(1)}, bf16[64,2048]{1,0:T(8,128)(2,1)S(1)}, u32[]{:S(2)}, u32[]{:S(2)}) collective-permute-start(bf16[64,2048]{1,0:T(8,128)(2,1)S(1)} %get-tuple-element.81), channel_id=1, source_target_pairs={{0,6},{2,0},{4,2},{6,4},{1,7},{3,1},{5,3},{7,5},{8,14},{10,8},{12,... | collective-permute-start | bytes 786440 | tf_op jit(solution)/shard_map/ppermute | solution.py:29
  134.6 12.1 %collective-permute-start.28 = (bf16[64,2048]{1,0:T(8,128)(2,1)S(1)}, bf16[64,2048]{1,0:T(8,128)(2,1)S(1)}, u32[]{:S(2)}, u32[]{:S(2)}) collective-permute-start(bf16[64,2048]{1,0:T(8,128)(2,1)S(1)} %get-tuple-element.96), channel_id=1, source_target_pairs={{0,2},{2,4},{4,6},{6,0},{1,3},{3,5},{5,7},{7,1},{8,10},{10,12},{12... | collective-permute-start | bytes 786440 | tf_op jit(solution)/shard_map/ppermute | solution.py:29
  136.1 13.3 %collective-permute-start.29 = (bf16[64,2048]{1,0:T(8,128)(2,1)S(1)}, bf16[64,2048]{1,0:T(8,128)(2,1)S(1)}, u32[]{:S(2)}, u32[]{:S(2)}) collective-permute-start(bf16[64,2048]{1,0:T(8,128)(2,1)S(1)} %get-tuple-element.98), channel_id=1, source_target_pairs={{0,6},{2,0},{4,2},{6,4},{1,7},{3,1},{5,3},{7,5},{8,14},{10,8},{12,... | collective-permute-start | bytes 786440 | tf_op jit(solution)/shard_map/ppermute | solution.py:29
  141.7 22.4 %collective-permute-start.26 = (bf16[64,4096]{1,0:T(8,128)(2,1)S(1)}, bf16[64,4096]{1,0:T(8,128)(2,1)S(1)}, u32[]{:S(2)}, u32[]{:S(2)}) collective-permute-start(bf16[64,4096]{1,0:T(8,128)(2,1)S(1)} %add.170), channel_id=1, source_target_pairs={{0,8},{8,0},{1,9},{9,1},{2,10},{10,2},{3,11},{11,3},{4,12},{12,4},... | collective-permute-start | bytes 1572872 | tf_op jit(solution)/shard_map/ppermute | solution.py:29
  144.7 16.1 %collective-permute-start.21 = (bf16[64,4096]{1,0:T(8,128)(2,1)S(1)}, bf16[64,4096]{1,0:T(8,128)(2,1)S(1)}, u32[]{:S(2)}, u32[]{:S(2)}) collective-permute-start(bf16[64,4096]{1,0:T(8,128)(2,1)S(1)} %get-tuple-element.82), channel_id=1, source_target_pairs={{0,2},{2,4},{4,6},{6,0},{1,3},{3,5},{5,7},{7,1},{8,10},{10,12},{12... | collective-permute-start | bytes 1572872 | tf_op jit(solution)/shard_map/ppermute | solution.py:29
  146.7 15.0 %collective-permute-start.22 = (bf16[64,4096]{1,0:T(8,128)(2,1)S(1)}, bf16[64,4096]{1,0:T(8,128)(2,1)S(1)}, u32[]{:S(2)}, u32[]{:S(2)}) collective-permute-start(bf16[64,4096]{1,0:T(8,128)(2,1)S(1)} %get-tuple-element.83), channel_id=1, source_target_pairs={{0,6},{2,0},{4,2},{6,4},{1,7},{3,1},{5,3},{7,5},{8,14},{10,8},{12,... | collective-permute-start | bytes 1572872 | tf_op jit(solution)/shard_map/ppermute | solution.py:29
  149.5 18.9 %collective-permute-start.30 = (bf16[64,4096]{1,0:T(8,128)(2,1)S(1)}, bf16[64,4096]{1,0:T(8,128)(2,1)S(1)}, u32[]{:S(2)}, u32[]{:S(2)}) collective-permute-start(bf16[64,4096]{1,0:T(8,128)(2,1)S(1)} %get-tuple-element.99), channel_id=1, source_target_pairs={{0,2},{2,4},{4,6},{6,0},{1,3},{3,5},{5,7},{7,1},{8,10},{10,12},{12... | collective-permute-start | bytes 1572872 | tf_op jit(solution)/shard_map/ppermute | solution.py:29
  149.6 20.1 %collective-permute-start.31 = (bf16[64,4096]{1,0:T(8,128)(2,1)S(1)}, bf16[64,4096]{1,0:T(8,128)(2,1)S(1)}, u32[]{:S(2)}, u32[]{:S(2)}) collective-permute-start(bf16[64,4096]{1,0:T(8,128)(2,1)S(1)} %get-tuple-element.100), channel_id=1, source_target_pairs={{0,6},{2,0},{4,2},{6,4},{1,7},{3,1},{5,3},{7,5},{8,14},{10,8},{12,... | collective-permute-start | bytes 1572872 | tf_op jit(solution)/shard_map/ppermute | solution.py:29
  162.0 14.5 %collective-permute-start.23 = (bf16[64,4096]{1,0:T(8,128)(2,1)S(1)}, bf16[64,4096]{1,0:T(8,128)(2,1)S(1)}, u32[]{:S(2)}, u32[]{:S(2)}) collective-permute-start(bf16[64,4096]{1,0:T(8,128)(2,1)S(1)} %add.169), channel_id=1, source_target_pairs={{0,16},{16,32},{32,48},{48,64},{64,80},{80,96},{96,112},{112,128},... | collective-permute-start | bytes 1572872 | tf_op jit(solution)/shard_map/ppermute | solution.py:511
  170.0 16.7 %collective-permute-start.32 = (bf16[64,4096]{1,0:T(8,128)(2,1)S(1)}, bf16[64,4096]{1,0:T(8,128)(2,1)S(1)}, u32[]{:S(2)}, u32[]{:S(2)}) collective-permute-start(bf16[64,4096]{1,0:T(8,128)(2,1)S(1)} %add.171), channel_id=1, source_target_pairs={{0,16},{16,32},{32,48},{48,64},{64,80},{80,96},{96,112},{112,128},... | collective-permute-start | bytes 1572872 | tf_op jit(solution)/shard_map/ppermute | solution.py:512
